TPU v7x, 512 devices: a whole 4x4x16 slice. The times are simulated.
512 devices in a mesh: branch: 4 (over x), row: 16 (over y, z_hi, core), col: 8 (over z_lo).
Axes of the slice: x: 4, y: 4, z: 16 (z_hi: 2, z_lo: 8; z = z_hi * 8 + z_lo), core: 2. Of those that a mesh axis runs over, the one named last changes fastest.
Arguments:
- feature_one: bfloat16 [512, 73728], P(('branch', 'row'), 'col'), may hold values from -6 to 6
- feature_two: bfloat16 [256, 73728], P(('branch', 'row'), 'col'), may hold values from -6 to 6
- feature_three: bfloat16 [128, 73728], P(('branch', 'row'), 'col'), may hold values from -6 to 6
- feature_four: bfloat16 [64, 73728], P(('branch', 'row'), 'col'), may hold values from -6 to 6
- output_one: bfloat16 [512, 73728], P(('branch', 'row'), 'col'), may hold values from -6 to 6
- output_two: bfloat16 [256, 73728], P(('branch', 'row'), 'col'), may hold values from -6 to 6
- output_three: bfloat16 [128, 73728], P(('branch', 'row'), 'col'), may hold values from -6 to 6
- upstream_one: bfloat16 [512, 73728], P(('branch', 'row'), 'col'), may hold values from -6 to 6
- upstream_two: bfloat16 [256, 73728], P(('branch', 'row'), 'col'), may hold values from -6 to 6
- upstream_three: bfloat16 [128, 73728], P(('branch', 'row'), 'col'), may hold values from -6 to 6
- kernel_one: bfloat16 [3, 3, 48, 48], replicated, may hold values from -0.3125 to 0.3125
- kernel_two: bfloat16 [3, 3, 96, 96], replicated, may hold values from -0.21875 to 0.21875
- kernel_three: bfloat16 [3, 3, 192, 192], replicated, may hold values from -0.15625 to 0.15625
- stride_one_two: bfloat16 [3, 3, 48, 96], replicated, may hold values from -0.3125 to 0.3125
- stride_two_three: bfloat16 [3, 3, 96, 192], replicated, may hold values from -0.21875 to 0.21875
- mixer_two_one: bfloat16 [96, 48], replicated, may hold values from -0.625 to 0.625
- mixer_three_one: bfloat16 [192, 48], replicated, may hold values from -0.4375 to 0.4375
- mixer_four_one: bfloat16 [384, 48], replicated, may hold values from -0.3125 to 0.3125
- mixer_three_two: bfloat16 [192, 96], replicated, may hold values from -0.4375 to 0.4375
- mixer_four_two: bfloat16 [384, 96], replicated, may hold values from -0.3125 to 0.3125
- mixer_four_three: bfloat16 [384, 192], replicated, may hold values from -0.3125 to 0.3125
Outputs:
- grad_one: bfloat16 [512, 73728], P(('branch', 'row'), 'col')
- grad_two: bfloat16 [256, 73728], P(('branch', 'row'), 'col')
- grad_three: bfloat16 [128, 73728], P(('branch', 'row'), 'col')
- grad_four: bfloat16 [64, 73728], P(('branch', 'row'), 'col')
- weight_grads: float32 [804096], P(('row', 'col'))
All inputs are finite; a program needn't handle non-finite values.
Results may differ from a plain program's by a relative error of at most 0.008.
Values may be sent and summed in bfloat16 or wider, within the bound.
A program may use at most 64 MiB of HBM per device.

v0:
```python
import jax
import jax.numpy as jnp
from jax import lax
from jax.sharding import PartitionSpec as P

EPSILON = 1e-06
PARITY = ((1, 1), (0, 0), (1, 0))


def passed_along(value, axis, steps):
    count = lax.axis_size(axis)
    leading, last = (max(0, -steps), min(count, count - steps))
    return lax.ppermute(value, axis, [(source, source + steps) for source in range(leading, last)])


def with_halo(cells, sides, width):
    for axis, dim in sides:
        count = lax.axis_size(axis)
        ends = count - 1
        head = lax.slice_in_dim(cells, 0, width, axis=dim)
        tail = lax.slice_in_dim(cells, cells.shape[dim] - width, cells.shape[dim], axis=dim)
        cells = jnp.concatenate(
            [
                lax.ppermute(tail, axis, [(i, (i + 1) % count) for i in range(ends)]),
                cells,
                lax.ppermute(head, axis, [((i + 1) % count, i) for i in range(ends)]),
            ],
            axis=dim,
        )
    return cells


def as_cells(flat, channels):
    return flat.reshape(flat.shape[0], flat.shape[1] // channels, channels)


def pool_sum(field_in, factor):
    height, breadth, channels = field_in.shape
    return field_in.reshape(height // factor, factor, breadth // factor, factor, channels).sum(
        axis=(1, 3), dtype=jnp.float32
    )


def project(field_in, mixer):
    return jnp.einsum("hwi,ji->hwj", field_in, mixer, preferred_element_type=jnp.float32)


def mixer_grad(source, pooled):
    return jnp.einsum("hwj,hwi->ji", source, pooled, preferred_element_type=jnp.float32)


def extend_next(field_in):
    below = passed_along(field_in[:1], ("branch", "row"), -1)
    taller = jnp.concatenate([field_in, below], axis=0)
    beside = passed_along(taller[:, :1], "col", -1)
    return jnp.concatenate([taller, beside], axis=1)


def with_frame(field_in):
    return with_halo(field_in, ((("branch", "row"), 0), ("col", 1)), 1)


def down_backward(source, grad_ext, weight):
    tile_rows = grad_ext.shape[0] - 1
    tile_cols = grad_ext.shape[1] - 1
    channels = source.shape[2]
    parts = source.reshape(tile_rows, 2, tile_cols, 2, channels)
    blocks = [jnp.zeros((tile_rows, tile_cols, channels), jnp.float32) for repeat in range(4)]
    kernel_rows = []
    for tap_row in range(3):
        row_parity, row_offset = PARITY[tap_row]
        kernel_row = []
        for tap_col in range(3):
            col_parity, col_offset = PARITY[tap_col]
            grad_piece = grad_ext[
                row_offset : row_offset + tile_rows, col_offset : col_offset + tile_cols
            ]
            parity_part = parts[:, row_parity, :, col_parity]
            kernel_row.append(
                jnp.einsum(
                    "hwi,hwo->io", parity_part, grad_piece, preferred_element_type=jnp.float32
                )
            )
            block_slot = 2 * row_parity + col_parity
            blocks[block_slot] = blocks[block_slot] + jnp.einsum(
                "hwo,io->hwi",
                grad_piece,
                weight[tap_row, tap_col],
                preferred_element_type=jnp.float32,
            )
        kernel_rows.append(jnp.stack(kernel_row))
    upper_half = jnp.stack([blocks[0], blocks[1]], axis=2)
    lower_half = jnp.stack([blocks[2], blocks[3]], axis=2)
    full_grid = jnp.stack([upper_half, lower_half], axis=1).reshape(
        2 * tile_rows, 2 * tile_cols, channels
    )
    return (full_grid, jnp.stack(kernel_rows))


def conv_backward(source, grad_pad, weight):
    tile_rows, tile_cols = (source.shape[0], source.shape[1])
    result = jnp.zeros((tile_rows, tile_cols, weight.shape[2]), jnp.float32)
    kernel_rows = []
    for tap_row in range(3):
        kernel_row = []
        for tap_col in range(3):
            grad_piece = grad_pad[
                2 - tap_row : 2 - tap_row + tile_rows, 2 - tap_col : 2 - tap_col + tile_cols
            ]
            result = result + jnp.einsum(
                "hwo,io->hwi",
                grad_piece,
                weight[tap_row, tap_col],
                preferred_element_type=jnp.float32,
            )
            kernel_row.append(
                jnp.einsum("hwi,hwo->io", source, grad_piece, preferred_element_type=jnp.float32)
            )
        kernel_rows.append(jnp.stack(kernel_row))
    return (result, jnp.stack(kernel_rows))


def local(
    feature_one,
    feature_two,
    feature_three,
    feature_four,
    output_one,
    output_two,
    output_three,
    upstream_one,
    upstream_two,
    upstream_three,
    kernel_one,
    kernel_two,
    kernel_three,
    stride_one_two,
    stride_two_three,
    mixer_two_one,
    mixer_three_one,
    mixer_four_one,
    mixer_three_two,
    mixer_four_two,
    mixer_four_three,
):
    width_one = kernel_one.shape[2]
    width_two = kernel_two.shape[2]
    width_three = kernel_three.shape[2]
    width_four = mixer_four_one.shape[0]
    cells_one = as_cells(feature_one, width_one)
    cells_two = as_cells(feature_two, width_two)
    cells_three = as_cells(feature_three, width_three)
    cells_four = as_cells(feature_four, width_four)
    saved_one = as_cells(output_one, width_one)
    saved_two = as_cells(output_two, width_two)
    saved_three = as_cells(output_three, width_three)
    incoming_one = as_cells(upstream_one, width_one)
    incoming_two = as_cells(upstream_two, width_two)
    incoming_three = as_cells(upstream_three, width_three)
    framed_two = extend_next(incoming_two)
    framed_three = extend_next(incoming_three)
    spread_one, stride_grad_one = down_backward(saved_one, framed_two, stride_one_two)
    spread_two, stride_grad_two = down_backward(saved_two, framed_three, stride_two_three)
    half_one = pool_sum(incoming_one, 2)
    quarter_one = pool_sum(half_one, 2)
    eighth_one = pool_sum(quarter_one, 2)
    half_two = pool_sum(incoming_two, 2)
    quarter_two = pool_sum(half_two, 2)
    half_three = pool_sum(incoming_three, 2)
    pooled_one_two = half_one.astype(jnp.bfloat16)
    pooled_one_three = quarter_one.astype(jnp.bfloat16)
    pooled_one_four = eighth_one.astype(jnp.bfloat16)
    pooled_two_three = half_two.astype(jnp.bfloat16)
    pooled_two_four = quarter_two.astype(jnp.bfloat16)
    pooled_three_four = half_three.astype(jnp.bfloat16)
    delta_one = (incoming_one + spread_one).astype(jnp.bfloat16)
    delta_two = (incoming_two + project(pooled_one_two, mixer_two_one) + spread_two).astype(
        jnp.bfloat16
    )
    delta_three = (
        incoming_three
        + project(pooled_one_three, mixer_three_one)
        + project(pooled_two_three, mixer_three_two)
    ).astype(jnp.bfloat16)
    back_four = (
        project(pooled_one_four, mixer_four_one)
        + project(pooled_two_four, mixer_four_two)
        + project(pooled_three_four, mixer_four_three)
    )
    back_one, kernel_grad_one = conv_backward(cells_one, with_frame(delta_one), kernel_one)
    back_two, kernel_grad_two = conv_backward(cells_two, with_frame(delta_two), kernel_two)
    back_three, kernel_grad_three = conv_backward(
        cells_three, with_frame(delta_three), kernel_three
    )
    pieces = (
        kernel_grad_one,
        kernel_grad_two,
        kernel_grad_three,
        stride_grad_one,
        stride_grad_two,
        mixer_grad(saved_two, pooled_one_two),
        mixer_grad(saved_three, pooled_one_three),
        mixer_grad(cells_four, pooled_one_four),
        mixer_grad(saved_three, pooled_two_three),
        mixer_grad(cells_four, pooled_two_four),
        mixer_grad(cells_four, pooled_three_four),
    )
    partial_value = jnp.concatenate([piece_grad.reshape(-1) for piece_grad in pieces])
    total_count = partial_value.shape[0]
    share_length = total_count // lax.axis_size(("row", "col"))
    summed = lax.psum(partial_value, ("branch", "row", "col"))
    squares = jnp.sum(summed * summed)
    start = lax.axis_index(("row", "col")) * share_length
    share = lax.dynamic_slice_in_dim(summed, start, share_length)
    spread_rms = jnp.sqrt(squares / total_count + EPSILON)
    weight_grads = share * jnp.minimum(jnp.float32(1.0), 1.0 / spread_rms)
    return (
        back_one.astype(jnp.bfloat16).reshape(feature_one.shape),
        back_two.astype(jnp.bfloat16).reshape(feature_two.shape),
        back_three.astype(jnp.bfloat16).reshape(feature_three.shape),
        back_four.astype(jnp.bfloat16).reshape(feature_four.shape),
        weight_grads,
    )


def solution(mesh):
    in_specs = (
        P(("branch", "row"), "col"),
        P(("branch", "row"), "col"),
        P(("branch", "row"), "col"),
        P(("branch", "row"), "col"),
        P(("branch", "row"), "col"),
        P(("branch", "row"), "col"),
        P(("branch", "row"), "col"),
        P(("branch", "row"), "col"),
        P(("branch", "row"), "col"),
        P(("branch", "row"), "col"),
        P(),
        P(),
        P(),
        P(),
        P(),
        P(),
        P(),
        P(),
        P(),
        P(),
        P(),
    )
    out_specs = (
        P(("branch", "row"), "col"),
        P(("branch", "row"), "col"),
        P(("branch", "row"), "col"),
        P(("branch", "row"), "col"),
        P(("row", "col")),
    )
    return jax.shard_map(local, mesh=mesh, in_specs=in_specs, out_specs=out_specs, check_vma=False)
```

profile of v0, /device:TPU:1, one launch (start us, length us, event | category | flops | bytes accessed | tf_op | source)
XLA Modules:
  0.0 752.0 jit_solution(4519271185764531634)
XLA Ops:
  9.0 8.8 %collective-permute-start = (bf16[1,96,96]{2,1,0:T(8,128)(2,1)}, bf16[1,96,96]{2,1,0:T(8,128)(2,1)}, u32[]{:S(2)}, u32[]{:S(2)}) collective-permute-start(bf16[1,96,96]{2,1,0:T(8,128)(2,1)} %slice.343), channel_id=1, source_target_pairs={{8,0},{16,8},{24,16},{32,24},{40,32},{48,40},{56,48},{64,56},{72,6... | collective-permute-start | bytes 55304 | tf_op jit(solution)/shard_map/ppermute | solution.py:13
  19.4 1.9 collective-permute-start.6
  23.2 2.2 reshape.192
  28.9 1.9 collective-permute-start.13
  30.9 12.4 %collective-permute-start.12 = (bf16[1,48,192]{2,1,0:T(8,128)(2,1)}, bf16[1,48,192]{2,1,0:T(8,128)(2,1)}, u32[]{:S(2)}, u32[]{:S(2)}) collective-permute-start(bf16[1,48,192]{2,1,0:T(8,128)(2,1)} %get-tuple-element.31), channel_id=1, source_target_pairs={{0,8},{8,16},{16,24},{24,32},{32,40},{40,48},{48,56},{56,64},{64,7... | collective-permute-start | bytes 55304 | tf_op jit(solution)/shard_map/ppermute | solution.py:24
  103.2 5.2 collective-permute-start.15
  108.5 1.7 fusion.69
  110.2 1.7 fusion.80
  123.5 1.9 collective-permute-start.3
  125.4 12.5 %collective-permute-start.2 = (bf16[1,192,48]{1,2,0:T(8,128)(2,1)}, bf16[1,192,48]{1,2,0:T(8,128)(2,1)}, u32[]{:S(2)}, u32[]{:S(2)}) collective-permute-start(bf16[1,192,48]{1,2,0:T(8,128)(2,1)} %get-tuple-element.15), channel_id=1, source_target_pairs={{0,8},{8,16},{16,24},{24,32},{32,40},{40,48},{48,56},{56,64},{64,7... | collective-permute-start | bytes 55304 | tf_op jit(solution)/shard_map/ppermute | solution.py:24
  148.2 1.9 collective-permute-start.9
  155.5 12.5 %collective-permute-start.8 = (bf16[1,96,96]{2,1,0:T(8,128)(2,1)}, bf16[1,96,96]{2,1,0:T(8,128)(2,1)S(1)}, u32[]{:S(2)}, u32[]{:S(2)}) collective-permute-start(bf16[1,96,96]{2,1,0:T(8,128)(2,1)} %get-tuple-element.29), channel_id=1, source_target_pairs={{0,8},{8,16},{16,24},{24,32},{32,40},{40,48},{48,56},{56,64},{64,7... | collective-permute-start | bytes 55304 | tf_op jit(solution)/shard_map/ppermute | solution.py:24
  177.7 1.8 copy.356
  179.5 3.1 reshape.179
  184.8 4.0 collective-permute-start.5
  194.7 4.0 collective-permute-start.11
  209.9 1.8 fusion.5
  217.1 1.7 constant_dynamic-update-slice_fusion.13
  218.9 11.9 %dynamic-update-slice.2 = f32[804096]{0:T(1024)} dynamic-update-slice(f32[804096]{0:T(1024)} %constant_dynamic-update-slice_fusion.13, f32[331776]{0:T(1024)S(1)} %copy-done.1, s32[]{} %constant.44) | dynamic-update-slice | bytes 2654212
  230.8 1.8 constant_dynamic-update-slice_fusion.12
  232.6 2.0 constant_dynamic-update-slice_fusion.11
  242.0 1.8 constant_dynamic-update-slice_fusion.5
  252.7 487.0 %all-reduce.2.cloned.1.call-done = f32[804096]{0:T(1024)} async-done(((f32[804096]{0:T(1024)}), f32[804096]{0:T(1024)}) %all-reduce.2.cloned.1.call-update) | async-done | bytes 3216400 | tf_op jit(solution)/shard_map/psum | solution.py:211
  739.7 3.3 multiply_reduce_fusion
  (361 shorter events, 146.8 us)
Async XLA Ops:
  7.2 66.5 %copy-start = (bf16[384,192]{0,1:T(8,128)(2,1)S(1)}, bf16[384,192]{0,1:T(8,128)(2,1)}, u32[]{:S(2)}) copy-start(bf16[384,192]{0,1:T(8,128)(2,1)} %param.41) | copy-start | bytes 442372
  7.2 48.9 %copy-start.34 = (bf16[2,9216]{1,0:T(2,128)(2,1)S(1)}, bf16[2,9216]{1,0:T(2,128)(2,1)}, u32[]{:S(2)}) copy-start(bf16[2,9216]{1,0:T(2,128)(2,1)} %param.30) | copy-start | bytes 110596
  7.2 48.6 %copy-start.7 = (bf16[8,9216]{1,0:T(8,128)(2,1)S(1)}, bf16[8,9216]{1,0:T(8,128)(2,1)}, u32[]{:S(2)}) copy-start(bf16[8,9216]{1,0:T(8,128)(2,1)} %param.28) | copy-start | bytes 442372
  7.2 49.0 %copy-start.37 = (bf16[4,9216]{1,0:T(4,128)(2,1)S(1)}, bf16[4,9216]{1,0:T(4,128)(2,1)}, u32[]{:S(2)}) copy-start(bf16[4,9216]{1,0:T(4,128)(2,1)} %param.26) | copy-start | bytes 221188
  7.2 49.2 %copy-start.58 = (bf16[2,9216]{1,0:T(2,128)(2,1)S(1)}, bf16[2,9216]{1,0:T(2,128)(2,1)}, u32[]{:S(2)}) copy-start(bf16[2,9216]{1,0:T(2,128)(2,1)} %param.27) | copy-start | bytes 110596
  7.2 732.5 %all-reduce.2.cloned.1.call-start = ((), (), s32[]{:S(2)}) async-start(), calls=%async_computation | async-start | bytes 6438912 | tf_op jit(solution)/shard_map/psum | solution.py:211
  9.0 79.5 %collective-permute-start = (bf16[1,96,96]{2,1,0:T(8,128)(2,1)}, bf16[1,96,96]{2,1,0:T(8,128)(2,1)}, u32[]{:S(2)}, u32[]{:S(2)}) collective-permute-start(bf16[1,96,96]{2,1,0:T(8,128)(2,1)} %slice.343), channel_id=1, source_target_pairs={{8,0},{16,8},{24,16},{32,24},{40,32},{48,40},{56,48},{64,56},{72,6... | collective-permute-start | bytes 55304 | tf_op jit(solution)/shard_map/ppermute | solution.py:13
  19.4 72.4 %collective-permute-start.6 = (bf16[1,48,192]{2,1,0:T(8,128)(2,1)}, bf16[1,48,192]{2,1,0:T(8,128)(2,1)}, u32[]{:S(2)}, u32[]{:S(2)}) collective-permute-start(bf16[1,48,192]{2,1,0:T(8,128)(2,1)} %slice.379), channel_id=1, source_target_pairs={{8,0},{16,8},{24,16},{32,24},{40,32},{48,40},{56,48},{64,56},{72,6... | collective-permute-start | bytes 55304 | tf_op jit(solution)/shard_map/ppermute | solution.py:13
  23.2 37.5 %copy-start.59 = (bf16[2,9216]{1,0:T(2,128)(2,1)S(1)}, bf16[2,9216]{1,0:T(2,128)(2,1)}, u32[]{:S(2)}) copy-start(bf16[2,9216]{1,0:T(2,128)(2,1)} %param.23) | copy-start | bytes 110596
  28.9 71.7 %collective-permute-start.13 = (bf16[1,48,192]{2,1,0:T(8,128)(2,1)}, bf16[1,48,192]{2,1,0:T(8,128)(2,1)}, u32[]{:S(2)}, u32[]{:S(2)}) collective-permute-start(bf16[1,48,192]{2,1,0:T(8,128)(2,1)} %get-tuple-element.32), channel_id=1, source_target_pairs={{8,0},{16,8},{24,16},{32,24},{40,32},{48,40},{56,48},{64,56},{72,6... | collective-permute-start | bytes 55304 | tf_op jit(solution)/shard_map/ppermute | solution.py:26
  30.9 69.8 %collective-permute-start.12 = (bf16[1,48,192]{2,1,0:T(8,128)(2,1)}, bf16[1,48,192]{2,1,0:T(8,128)(2,1)}, u32[]{:S(2)}, u32[]{:S(2)}) collective-permute-start(bf16[1,48,192]{2,1,0:T(8,128)(2,1)} %get-tuple-element.31), channel_id=1, source_target_pairs={{0,8},{8,16},{16,24},{24,32},{32,40},{40,48},{48,56},{56,64},{64,7... | collective-permute-start | bytes 55304 | tf_op jit(solution)/shard_map/ppermute | solution.py:24
  77.7 37.4 %copy-start.40 = (f32[2,48,96]{2,1,0:T(8,128)S(1)}, f32[2,48,96]{2,1,0:T(8,128)}, u32[]{:S(2)}) copy-start(f32[2,48,96]{2,1,0:T(8,128)} %fusion.120) | copy-start | bytes 110596
  96.5 20.2 %collective-permute-start.1 = (bf16[5,1,96]{2,1,0:T(2,128)(2,1)S(1)}, bf16[5,1,96]{2,1,0:T(2,128)(2,1)S(1)}, u32[]{:S(2)}, u32[]{:S(2)}) collective-permute-start(bf16[5,1,96]{2,1,0:T(2,128)(2,1)S(1)} %slice.442), channel_id=1, source_target_pairs={{1,0},{2,1},{3,2},{4,3},{5,4},{6,5},{7,6},{9,8},{10,9},{11,10},{12... | collective-permute-start | bytes 2888 | tf_op jit(solution)/shard_map/ppermute | solution.py:13
  99.3 43.6 %collective-permute-start.7 = (bf16[3,1,192]{2,1,0:T(2,128)(2,1)}, bf16[3,1,192]{2,1,0:T(2,128)(2,1)S(1)}, u32[]{:S(2)}, u32[]{:S(2)}) collective-permute-start(bf16[3,1,192]{2,1,0:T(2,128)(2,1)} %slice.455), channel_id=1, source_target_pairs={{1,0},{2,1},{3,2},{4,3},{5,4},{6,5},{7,6},{9,8},{10,9},{11,10},{12... | collective-permute-start | bytes 3464 | tf_op jit(solution)/shard_map/ppermute | solution.py:13
  101.9 53.6 %collective-permute-start.14 = (bf16[4,1,192]{2,1,0:T(2,128)(2,1)}, bf16[4,1,192]{2,1,0:T(2,128)(2,1)S(1)}, u32[]{:S(2)}, u32[]{:S(2)}) collective-permute-start(bf16[4,1,192]{2,1,0:T(2,128)(2,1)} %get-tuple-element.27), channel_id=1, source_target_pairs={{1,0},{2,1},{3,2},{4,3},{5,4},{6,5},{7,6},{9,8},{10,9},{11,10},{12... | collective-permute-start | bytes 4616 | tf_op jit(solution)/shard_map/ppermute | solution.py:26
  103.2 64.8 %collective-permute-start.15 = (bf16[4,1,192]{2,1,0:T(2,128)(2,1)}, bf16[4,1,192]{2,1,0:T(2,128)(2,1)S(1)}, u32[]{:S(2)}, u32[]{:S(2)}) collective-permute-start(bf16[4,1,192]{2,1,0:T(2,128)(2,1)} %get-tuple-element.28), channel_id=1, source_target_pairs={{0,1},{1,2},{2,3},{3,4},{4,5},{5,6},{6,7},{8,9},{9,10},{10,11},{11... | collective-permute-start | bytes 4616 | tf_op jit(solution)/shard_map/ppermute | solution.py:24
  123.5 59.1 %collective-permute-start.3 = (bf16[1,192,48]{1,2,0:T(8,128)(2,1)}, bf16[1,192,48]{1,2,0:T(8,128)(2,1)}, u32[]{:S(2)}, u32[]{:S(2)}) collective-permute-start(bf16[1,192,48]{1,2,0:T(8,128)(2,1)} %get-tuple-element.16), channel_id=1, source_target_pairs={{8,0},{16,8},{24,16},{32,24},{40,32},{48,40},{56,48},{64,56},{72,6... | collective-permute-start | bytes 55304 | tf_op jit(solution)/shard_map/ppermute | solution.py:26
  125.4 57.2 %collective-permute-start.2 = (bf16[1,192,48]{1,2,0:T(8,128)(2,1)}, bf16[1,192,48]{1,2,0:T(8,128)(2,1)}, u32[]{:S(2)}, u32[]{:S(2)}) collective-permute-start(bf16[1,192,48]{1,2,0:T(8,128)(2,1)} %get-tuple-element.15), channel_id=1, source_target_pairs={{0,8},{8,16},{16,24},{24,32},{32,40},{40,48},{48,56},{56,64},{64,7... | collective-permute-start | bytes 55304 | tf_op jit(solution)/shard_map/ppermute | solution.py:24
  148.2 45.2 %collective-permute-start.9 = (bf16[1,96,96]{2,1,0:T(8,128)(2,1)}, bf16[1,96,96]{2,1,0:T(8,128)(2,1)S(1)}, u32[]{:S(2)}, u32[]{:S(2)}) collective-permute-start(bf16[1,96,96]{2,1,0:T(8,128)(2,1)} %get-tuple-element.30), channel_id=1, source_target_pairs={{8,0},{16,8},{24,16},{32,24},{40,32},{48,40},{56,48},{64,56},{72,6... | collective-permute-start | bytes 55304 | tf_op jit(solution)/shard_map/ppermute | solution.py:26
  155.5 37.9 %collective-permute-start.8 = (bf16[1,96,96]{2,1,0:T(8,128)(2,1)}, bf16[1,96,96]{2,1,0:T(8,128)(2,1)S(1)}, u32[]{:S(2)}, u32[]{:S(2)}) collective-permute-start(bf16[1,96,96]{2,1,0:T(8,128)(2,1)} %get-tuple-element.29), channel_id=1, source_target_pairs={{0,8},{8,16},{16,24},{24,32},{32,40},{40,48},{48,56},{56,64},{64,7... | collective-permute-start | bytes 55304 | tf_op jit(solution)/shard_map/ppermute | solution.py:24
  183.5 20.1 %collective-permute-start.4 = (bf16[10,1,48]{1,2,0:T(8,128)(2,1)S(1)}, bf16[10,1,48]{1,2,0:T(8,128)(2,1)S(1)}, u32[]{:S(2)}, u32[]{:S(2)}) collective-permute-start(bf16[10,1,48]{1,2,0:T(8,128)(2,1)S(1)} %get-tuple-element.13), channel_id=1, source_target_pairs={{1,0},{2,1},{3,2},{4,3},{5,4},{6,5},{7,6},{9,8},{10,9},{11,10},{12... | collective-permute-start | bytes 2888 | tf_op jit(solution)/shard_map/ppermute | solution.py:26
  184.8 18.8 %collective-permute-start.5 = (bf16[10,1,48]{1,2,0:T(8,128)(2,1)S(1)}, bf16[10,1,48]{1,2,0:T(8,128)(2,1)S(1)}, u32[]{:S(2)}, u32[]{:S(2)}) collective-permute-start(bf16[10,1,48]{1,2,0:T(8,128)(2,1)S(1)} %get-tuple-element.14), channel_id=1, source_target_pairs={{0,1},{1,2},{2,3},{3,4},{4,5},{5,6},{6,7},{8,9},{9,10},{10,11},{11... | collective-permute-start | bytes 2888 | tf_op jit(solution)/shard_map/ppermute | solution.py:24
  193.4 19.9 %collective-permute-start.10 = (bf16[6,1,96]{2,1,0:T(2,128)(2,1)S(1)}, bf16[6,1,96]{2,1,0:T(2,128)(2,1)S(1)}, u32[]{:S(2)}, u32[]{:S(2)}) collective-permute-start(bf16[6,1,96]{2,1,0:T(2,128)(2,1)S(1)} %get-tuple-element.19), channel_id=1, source_target_pairs={{1,0},{2,1},{3,2},{4,3},{5,4},{6,5},{7,6},{9,8},{10,9},{11,10},{12... | collective-permute-start | bytes 3464 | tf_op jit(solution)/shard_map/ppermute | solution.py:26
  194.7 18.6 %collective-permute-start.11 = (bf16[6,1,96]{2,1,0:T(2,128)(2,1)S(1)}, bf16[6,1,96]{2,1,0:T(2,128)(2,1)S(1)}, u32[]{:S(2)}, u32[]{:S(2)}) collective-permute-start(bf16[6,1,96]{2,1,0:T(2,128)(2,1)S(1)} %get-tuple-element.20), channel_id=1, source_target_pairs={{0,1},{1,2},{2,3},{3,4},{4,5},{5,6},{6,7},{8,9},{9,10},{10,11},{11... | collective-permute-start | bytes 3464 | tf_op jit(solution)/shard_map/ppermute | solution.py:24
  (54 other events, 925.3 us)
Sparse Core Ops, SparseCore 0:
  243.9 495.7 all-reduce.1
where the time goes:
time: 757 us; the launch traced here: 752 us
  waiting for transfers between devices  487 us (64%)
  matrix products  89.3 us (12%)
  starting transfers between devices  73.5 us (10%)
  local copies, waits for them, and re-layouts  71.3 us (9%)
  between operations  16.4 us (2%)
  other arithmetic  14.6 us (2%)
    psum x1, waiting for transfers between devices, local(): summed = lax.psum(partial_value, ('branch', 'row', 'col'))  487 us
    ppermute x6, starting transfers between devices, with_halo(): lax.ppermute(tail, axis, [(i, (i + 1) % count) for i in range(ends)])  50.6 us
    dot_general x27, matrix products, conv_backward(): jnp.einsum('hwo,io->hwi', grad_piece, weight[tap_row, tap_col], preferred...  31.5 us
    unnamed x139, local copies, waits for them, and re-layouts  28.5 us
    dot_general x18, matrix products, down_backward(): jnp.einsum('hwo,io->hwi', grad_piece, weight[tap_row, tap_col], preferred...  22.8 us
  transfers between devices with their start and end apart: 17, of which 1 were waited for; matrix products, arithmetic and copies ran while one was open for 18% of the time, Pallas kernels for 0%

commit v1 on v0

--- a/solution.py
+++ b/solution.py
@@ -1,9 +1,278 @@
+import functools
+
 import jax
 import jax.numpy as jnp
 from jax import lax
+from jax.experimental import pallas as pl
+from jax.experimental.pallas import tpu as pltpu
 from jax.sharding import PartitionSpec as P
 
 EPSILON = 1e-06
+MESH = pl.DeviceIdType.MESH
+TOTAL = 804096
+SHARE = 6282
+WINDOW = 64
+FLAT_ROWS = 6296
+
+
+def share_place(share):
+    row, col = divmod(share, 8)
+    core, z_hi, y = row % 2, (row // 2) % 2, row // 4
+    half, quarter = divmod(col, 4)
+    return ((core * 4 + y) * 4 + quarter) * 4 + z_hi * 2 + half
+
+
+def pack_shares(flat_ref, packed_ref):
+    for share in range(128):
+        start = SHARE * share // 1024 * 8
+        place = share_place(share) * WINDOW
+        packed_ref[place : place + WINDOW, :] = flat_ref[start : start + WINDOW, :].astype(jnp.bfloat16)
+
+
+def reduce_kernel(
+    packed_ref,
+    out_ref,
+    from_core,
+    sum_core,
+    from_plane,
+    sum_plane,
+    from_line,
+    share_buf,
+    square_buf,
+    from_near,
+    near_buf,
+    from_far,
+    core_sems,
+    plane_send,
+    plane_recv,
+    line_send,
+    line_recv,
+    share_send,
+    share_recv,
+    near_send,
+    near_recv,
+    far_send,
+    far_recv,
+):
+    x = lax.axis_index("branch")
+    row = lax.axis_index("row")
+    col = lax.axis_index("col")
+    core, z_hi, y = row % 2, (row // 2) % 2, row // 4
+    z = z_hi * 8 + col
+    partner = (x, row + 1 - 2 * core, col)
+
+    def plane_peer(step):
+        there = (x * 4 + y + step) % 16
+        return there, (there // 4, (there % 4) * 4 + z_hi * 2 + core, col)
+
+    def line_peer(step):
+        there = (z + step) % 16
+        return (x, y * 4 + (there // 8) * 2 + core, there % 8)
+
+    def near_peer(step):
+        there = (y * 2 + core + step) % 8
+        return (x, (there // 2) * 4 + z_hi * 2 + there % 2, col)
+
+    def greet(peer):
+        pl.semaphore_signal(barrier, inc=1, device_id=peer, device_id_type=MESH)
+
+    barrier = pltpu.get_barrier_semaphore()
+    greet(partner)
+
+    @pl.loop(1, 16)
+    def _(step):
+        greet(plane_peer(step)[1])
+        greet(line_peer(step))
+
+    @pl.loop(1, 8)
+    def _(step):
+        greet(near_peer(step))
+
+    pl.semaphore_wait(barrier, 38)
+
+    def remote(src, dst, send_sem, recv_sem, peer):
+        return pltpu.make_async_remote_copy(
+            src_ref=src, dst_ref=dst, send_sem=send_sem, recv_sem=recv_sem,
+            device_id=peer, device_id_type=MESH,
+        )
+
+    half = 64 * WINDOW
+    across = remote(
+        packed_ref.at[pl.ds(pl.multiple_of((1 - core) * half, half), half)],
+        from_core, core_sems.at[0], core_sems.at[1], partner,
+    )
+    across.start()
+    across.wait()
+
+    @pl.loop(0, 16)
+    def _(block):
+        start = pl.multiple_of(block * 256, 256)
+        mine = packed_ref[pl.ds(pl.multiple_of(core * half, half) + start, 256), :]
+        theirs = from_core[pl.ds(start, 256), :]
+        sum_core[pl.ds(start, 256), :] = (mine.astype(jnp.float32) + theirs.astype(jnp.float32)).astype(jnp.bfloat16)
+
+    def plane_copy(step):
+        there, peer = plane_peer(step)
+        place = (there % 4) * 4 + there // 4
+        return remote(
+            sum_core.at[pl.ds(pl.multiple_of(place * 256, 256), 256)],
+            from_plane.at[step - 1], plane_send.at[step - 1], plane_recv.at[step - 1], peer,
+        )
+
+    @pl.loop(1, 16)
+    def _(step):
+        plane_copy(step).start()
+
+    @pl.loop(1, 16)
+    def _(step):
+        plane_copy(step).wait()
+
+    @pl.loop(0, 4)
+    def _(block):
+        start = pl.multiple_of(block * WINDOW, WINDOW)
+        own = pl.multiple_of((y * 4 + x) * 256 + start, WINDOW)
+        total = sum_core[pl.ds(own, WINDOW), :].astype(jnp.float32)
+        for step in range(15):
+            total = total + from_plane[step, pl.ds(start, WINDOW), :].astype(jnp.float32)
+        sum_plane[pl.ds(start, WINDOW), :] = total.astype(jnp.bfloat16)
+
+    def line_copy(block):
+        target = (block // 2) * 8 + (block % 2) * 4 + x
+        step = (z - target + 16) % 16
+        slot = (step + 15) % 16
+        return step, remote(
+            sum_plane.at[pl.ds(pl.multiple_of(block * WINDOW, WINDOW), WINDOW)],
+            from_line.at[slot], line_send.at[block], line_recv.at[slot],
+            (x, y * 4 + (target // 8) * 2 + core, target % 8),
+        )
+
+    for block in range(4):
+        step, copy = line_copy(block)
+
+        @pl.when(step != 0)
+        def _():
+            copy.start()
+
+    owner_x = col % 4
+    owner = owner_x == x
+
+    def share_copy(step):
+        return remote(
+            share_buf, share_buf, share_send.at[step - 1], share_recv.at[0],
+            ((x + step) % 4, row, col),
+        )
+
+    @pl.when(owner)
+    def _():
+        @pl.loop(0, 15)
+        def _(slot):
+            remote(
+                sum_plane.at[pl.ds(0, WINDOW)], from_line.at[slot], line_send.at[0], line_recv.at[slot], partner
+            ).wait_recv()
+
+        own = pl.multiple_of((z_hi * 2 + col // 4) * WINDOW, WINDOW)
+        total = sum_plane[pl.ds(own, WINDOW), :].astype(jnp.float32)
+        for slot in range(15):
+            total = total + from_line[slot].astype(jnp.float32)
+        share_buf[...] = total
+        for step in range(1, 4):
+            share_copy(step).start()
+
+    @pl.when(jnp.logical_not(owner))
+    def _():
+        share_copy(1).wait_recv()
+
+    offset = (SHARE * (row * 8 + col)) % 1024
+    place = lax.broadcasted_iota(jnp.int32, (WINDOW, 128), 0) * 128 + lax.broadcasted_iota(jnp.int32, (WINDOW, 128), 1)
+    inside = jnp.logical_and(place >= offset, place < offset + SHARE)
+    share = share_buf[...]
+    squares = jnp.where(inside, share * share, 0.0)
+    square_buf[...] = squares.reshape(8, 8, 128).sum(axis=0)
+
+    def near_copy(step):
+        return remote(
+            square_buf, from_near.at[step - 1], near_send.at[step - 1], near_recv.at[step - 1], near_peer(step)
+        )
+
+    @pl.loop(1, 8)
+    def _(step):
+        near_copy(step).start()
+
+    @pl.loop(1, 8)
+    def _(step):
+        near_copy(step).wait()
+
+    near_buf[...] = square_buf[...] + from_near[...].sum(axis=0)
+
+    def far_copy(step):
+        return remote(
+            near_buf, from_far.at[step - 1], far_send.at[step - 1], far_recv.at[step - 1], line_peer(step)
+        )
+
+    @pl.loop(1, 16)
+    def _(step):
+        far_copy(step).start()
+
+    @pl.loop(1, 16)
+    def _(step):
+        far_copy(step).wait()
+
+    total_squares = jnp.sum(near_buf[...] + from_far[...].sum(axis=0), keepdims=True)
+    spread_rms = jnp.sqrt(total_squares / TOTAL + EPSILON)
+    out_ref[...] = share_buf[...] * jnp.minimum(jnp.float32(1.0), 1.0 / spread_rms)
+
+    for block in range(4):
+        step, copy = line_copy(block)
+
+        @pl.when(step != 0)
+        def _():
+            copy.wait_send()
+
+    @pl.when(owner)
+    def _():
+        for step in range(1, 4):
+            share_copy(step).wait_send()
+
+
+def reduce_shares(packed):
+    dma = pltpu.SemaphoreType.DMA
+    window = pl.pallas_call(
+        reduce_kernel,
+        out_shape=jax.ShapeDtypeStruct((WINDOW, 128), jnp.float32),
+        in_specs=[pl.BlockSpec(memory_space=pltpu.VMEM)],
+        out_specs=pl.BlockSpec(memory_space=pltpu.VMEM),
+        scratch_shapes=[
+            pltpu.VMEM((64 * WINDOW, 128), jnp.bfloat16),
+            pltpu.VMEM((64 * WINDOW, 128), jnp.bfloat16),
+            pltpu.VMEM((15, 4 * WINDOW, 128), jnp.bfloat16),
+            pltpu.VMEM((4 * WINDOW, 128), jnp.bfloat16),
+            pltpu.VMEM((15, WINDOW, 128), jnp.bfloat16),
+            pltpu.VMEM((WINDOW, 128), jnp.float32),
+            pltpu.VMEM((8, 128), jnp.float32),
+            pltpu.VMEM((7, 8, 128), jnp.float32),
+            pltpu.VMEM((8, 128), jnp.float32),
+            pltpu.VMEM((15, 8, 128), jnp.float32),
+            dma((2,)),
+            dma((15,)),
+            dma((15,)),
+            dma((4,)),
+            dma((15,)),
+            dma((3,)),
+            dma((1,)),
+            dma((7,)),
+            dma((7,)),
+            dma((15,)),
+            dma((15,)),
+        ],
+        compiler_params=pltpu.CompilerParams(
+            collective_id=0, has_side_effects=True, vmem_limit_bytes=32 * 1024 * 1024
+        ),
+        name="reduce_shares",
+    )(packed)
+    offset = (SHARE * lax.axis_index(("row", "col"))) % 1024
+    return lax.dynamic_slice(window.reshape(WINDOW * 128), (offset,), (SHARE,))
+
+
 PARITY = ((1, 1), (0, 0), (1, 0))
 
 
@@ -205,15 +474,19 @@
         mixer_grad(cells_four, pooled_two_four),
         mixer_grad(cells_four, pooled_three_four),
     )
-    partial_value = jnp.concatenate([piece_grad.reshape(-1) for piece_grad in pieces])
-    total_count = partial_value.shape[0]
-    share_length = total_count // lax.axis_size(("row", "col"))
-    summed = lax.psum(partial_value, ("branch", "row", "col"))
-    squares = jnp.sum(summed * summed)
-    start = lax.axis_index(("row", "col")) * share_length
-    share = lax.dynamic_slice_in_dim(summed, start, share_length)
-    spread_rms = jnp.sqrt(squares / total_count + EPSILON)
-    weight_grads = share * jnp.minimum(jnp.float32(1.0), 1.0 / spread_rms)
+    flat = jnp.concatenate(
+        [piece_grad.reshape(-1) for piece_grad in pieces]
+        + [jnp.zeros((FLAT_ROWS * 128 - TOTAL,), jnp.float32)]
+    ).reshape(FLAT_ROWS, 128)
+    packed = pl.pallas_call(
+        pack_shares,
+        out_shape=jax.ShapeDtypeStruct((128 * WINDOW, 128), jnp.bfloat16),
+        in_specs=[pl.BlockSpec(memory_space=pltpu.VMEM)],
+        out_specs=pl.BlockSpec(memory_space=pltpu.VMEM),
+        compiler_params=pltpu.CompilerParams(vmem_limit_bytes=32 * 1024 * 1024),
+        name="pack_shares",
+    )(flat)
+    weight_grads = reduce_shares(packed)
     return (
         back_one.astype(jnp.bfloat16).reshape(feature_one.shape),
         back_two.astype(jnp.bfloat16).reshape(feature_two.shape),

time: 757 us -> 381 us (0.50)
  waiting for transfers between devices: 487 us -> 0.04 us
  Pallas kernels: 0 us -> 63.7 us
  local copies, waits for them, and re-layouts: 71.3 us -> 102 us
  matrix products: 89.3 us -> 109 us
  between operations: 16.4 us -> 2.01 us
  other arithmetic: 14.6 us -> 22.3 us
    psum x1 -> x0, waiting for transfers between devices: 487 us -> none  [local(): summed = lax.psum(partial_value, ('branch', 'row', 'col'))]
    pallas_call x0 -> x2, Pallas kernels: none -> 63.7 us  [the longest x1 63.5 us: reduce_shares(): pl.pallas_call(reduce_kernel, out_shape=jax.ShapeDtypeStruct((WINDOW, 128...]
    reshape x11, local copies, waits for them, and re-layouts: 11.3 us -> 20.4 us  [local(): piece_grad.reshape(-1)]
    unnamed x139 -> x128, local copies, waits for them, and re-layouts: 28.5 us -> 25 us
  transfers between devices with their start and end apart: 17 -> 16, of which waited for: 1 -> 0; matrix products, arithmetic and copies ran while one was open for 18% -> 51% of each run, Pallas kernels for 0% -> 0%
where the time goes in v1:
time: 381 us; the launch traced here: 374 us
  matrix products  109 us (29%)
  local copies, waits for them, and re-layouts  102 us (27%)
  starting transfers between devices  74.6 us (20%)
  Pallas kernels  63.7 us (17%)
  other arithmetic  22.3 us (6%)
    pallas_call x1, Pallas kernels, reduce_shares(): pl.pallas_call(reduce_kernel, out_shape=jax.ShapeDtypeStruct((WINDOW, 128...  63.5 us
    ppermute x6, starting transfers between devices, with_halo(): lax.ppermute(tail, axis, [(i, (i + 1) % count) for i in range(ends)])  51.8 us
    dot_general x27, matrix products, conv_backward(): jnp.einsum('hwo,io->hwi', grad_piece, weight[tap_row, tap_col], preferred...  38.6 us
    unnamed x128, local copies, waits for them, and re-layouts  25 us
    dot_general x18, matrix products, down_backward(): jnp.einsum('hwo,io->hwi', grad_piece, weight[tap_row, tap_col], preferred...  23.4 us
    reshape x11, local copies, waits for them, and re-layouts, local(): piece_grad.reshape(-1)  20.4 us
    dot_general x27, matrix products, conv_backward(): jnp.einsum('hwi,hwo->io', source, grad_piece, preferred_element_type=jnp....  20.1 us
    dot_general x18, matrix products, down_backward(): jnp.einsum('hwi,hwo->io', parity_part, grad_piece, preferred_element_type...  18.4 us
  transfers between devices with their start and end apart: 16, of which 0 were waited for; matrix products, arithmetic and copies ran while one was open for 51% of the time, Pallas kernels for 0%

profile of v1, /device:TPU:1, one launch (start us, length us, event | category | flops | bytes accessed | tf_op | source)
XLA Modules:
  0.0 373.7 jit_solution(9189452129975154978)
XLA Ops:
  2.5 8.8 %collective-permute-start = (bf16[1,96,96]{2,1,0:T(8,128)(2,1)}, bf16[1,96,96]{2,1,0:T(8,128)(2,1)}, u32[]{:S(2)}, u32[]{:S(2)}) collective-permute-start(bf16[1,96,96]{2,1,0:T(8,128)(2,1)} %slice.343), channel_id=1, source_target_pairs={{8,0},{16,8},{24,16},{32,24},{40,32},{48,40},{56,48},{64,56},{72,6... | collective-permute-start | bytes 55304 | tf_op jit(solution)/shard_map/ppermute | solution.py:282
  16.7 2.2 reshape.200
  24.3 12.4 %collective-permute-start.12 = (bf16[1,48,192]{2,1,0:T(8,128)(2,1)}, bf16[1,48,192]{2,1,0:T(8,128)(2,1)}, u32[]{:S(2)}, u32[]{:S(2)}) collective-permute-start(bf16[1,48,192]{2,1,0:T(8,128)(2,1)} %get-tuple-element.31), channel_id=1, source_target_pairs={{0,8},{8,16},{16,24},{24,32},{32,40},{40,48},{48,56},{56,64},{64,7... | collective-permute-start | bytes 55304 | tf_op jit(solution)/shard_map/ppermute | solution.py:293
  72.4 2.2 copy.322
  76.0 2.1 reshape.180
  120.3 5.8 %collective-permute-start.15 = (bf16[4,1,192]{2,1,0:T(2,128)(2,1)}, bf16[4,1,192]{2,1,0:T(2,128)(2,1)}, u32[]{:S(2)}, u32[]{:S(2)}) collective-permute-start(bf16[4,1,192]{2,1,0:T(2,128)(2,1)} %get-tuple-element.28), channel_id=1, source_target_pairs={{0,1},{1,2},{2,3},{3,4},{4,5},{5,6},{6,7},{8,9},{9,10},{10,11},{11... | collective-permute-start | bytes 4616 | tf_op jit(solution)/shard_map/ppermute | solution.py:293
  140.8 2.0 copy.321
  142.8 2.2 copy.323
  149.4 12.5 %collective-permute-start.2 = (bf16[1,192,48]{1,2,0:T(8,128)(2,1)}, bf16[1,192,48]{1,2,0:T(8,128)(2,1)}, u32[]{:S(2)}, u32[]{:S(2)}) collective-permute-start(bf16[1,192,48]{1,2,0:T(8,128)(2,1)} %get-tuple-element.15), channel_id=1, source_target_pairs={{0,8},{8,16},{16,24},{24,32},{32,40},{40,48},{48,56},{56,64},{64,7... | collective-permute-start | bytes 55304 | tf_op jit(solution)/shard_map/ppermute | solution.py:293
  163.8 2.1 fusion.184
  165.9 2.0 convolution_bitcast_fusion.44
  187.5 2.5 copy.369
  190.0 2.5 reshape.187
  192.5 12.5 %collective-permute-start.8 = (bf16[1,96,96]{2,1,0:T(8,128)(2,1)}, bf16[1,96,96]{2,1,0:T(8,128)(2,1)}, u32[]{:S(2)}, u32[]{:S(2)}) collective-permute-start(bf16[1,96,96]{2,1,0:T(8,128)(2,1)} %get-tuple-element.29), channel_id=1, source_target_pairs={{0,8},{8,16},{16,24},{24,32},{32,40},{40,48},{48,56},{56,64},{64,7... | collective-permute-start | bytes 55304 | tf_op jit(solution)/shard_map/ppermute | solution.py:293
  215.8 2.8 copy.356
  218.6 3.0 reshape.185
  224.1 4.0 %collective-permute-start.5 = (bf16[10,1,48]{1,2,0:T(8,128)(2,1)S(1)}, bf16[10,1,48]{1,2,0:T(8,128)(2,1)S(1)}, u32[]{:S(2)}, u32[]{:S(2)}) collective-permute-start(bf16[10,1,48]{1,2,0:T(8,128)(2,1)S(1)} %get-tuple-element.14), channel_id=1, source_target_pairs={{0,1},{1,2},{2,3},{3,4},{4,5},{5,6},{6,7},{8,9},{9,10},{10,11},{11... | collective-permute-start | bytes 2888 | tf_op jit(solution)/shard_map/ppermute | solution.py:293
  237.2 4.6 %collective-permute-start.11 = (bf16[6,1,96]{2,1,0:T(2,128)(2,1)}, bf16[6,1,96]{2,1,0:T(2,128)(2,1)}, u32[]{:S(2)}, u32[]{:S(2)}) collective-permute-start(bf16[6,1,96]{2,1,0:T(2,128)(2,1)} %get-tuple-element.20), channel_id=1, source_target_pairs={{0,1},{1,2},{2,3},{3,4},{4,5},{5,6},{6,7},{8,9},{9,10},{10,11},{11... | collective-permute-start | bytes 3464 | tf_op jit(solution)/shard_map/ppermute | solution.py:293
  263.2 2.2 fusion.6
  267.4 2.2 reshape.173
  284.8 2.0 copy.355
  286.8 2.0 reshape.183
  289.8 13.0 %dynamic-update-slice.2 = f32[805888]{0:T(1024)S(1)} dynamic-update-slice(f32[805888]{0:T(1024)S(1)} %constant_dynamic-update-slice_fusion.14, f32[331776]{0:T(1024)} %reshape.185, s32[]{} %constant.50) | dynamic-update-slice | bytes 2654212
  309.4 63.5 %reduce_shares.1 = f32[64,128]{1,0:T(8,128)S(1)} custom-call(bf16[8192,128]{1,0:T(8,128)(2,1)S(1)} %pack_shares.1.packed_ref), custom_call_target="tpu_custom_call" | custom-call | tf_op jit(solution)/shard_map/reduce_shares/pallas_call | solution.py:239
  (348 shorter events, 200.7 us)
Async XLA Ops:
  0.6 67.2 %copy-start = (bf16[384,192]{0,1:T(8,128)(2,1)S(1)}, bf16[384,192]{0,1:T(8,128)(2,1)}, u32[]{:S(2)}) copy-start(bf16[384,192]{0,1:T(8,128)(2,1)} %param.41) | copy-start | bytes 442372
  0.7 49.5 %copy-start.44 = (bf16[2,9216]{1,0:T(2,128)(2,1)S(1)}, bf16[2,9216]{1,0:T(2,128)(2,1)}, u32[]{:S(2)}) copy-start(bf16[2,9216]{1,0:T(2,128)(2,1)} %param.30) | copy-start | bytes 110596
  0.7 49.3 %copy-start.15 = (bf16[8,9216]{1,0:T(8,128)(2,1)S(1)}, bf16[8,9216]{1,0:T(8,128)(2,1)}, u32[]{:S(2)}) copy-start(bf16[8,9216]{1,0:T(8,128)(2,1)} %param.28) | copy-start | bytes 442372
  0.7 49.6 %copy-start.45 = (bf16[4,9216]{1,0:T(4,128)(2,1)S(1)}, bf16[4,9216]{1,0:T(4,128)(2,1)}, u32[]{:S(2)}) copy-start(bf16[4,9216]{1,0:T(4,128)(2,1)} %param.26) | copy-start | bytes 221188
  0.7 49.9 %copy-start.53 = (bf16[2,9216]{1,0:T(2,128)(2,1)S(1)}, bf16[2,9216]{1,0:T(2,128)(2,1)}, u32[]{:S(2)}) copy-start(bf16[2,9216]{1,0:T(2,128)(2,1)} %param.27) | copy-start | bytes 110596
  2.5 97.2 %collective-permute-start = (bf16[1,96,96]{2,1,0:T(8,128)(2,1)}, bf16[1,96,96]{2,1,0:T(8,128)(2,1)}, u32[]{:S(2)}, u32[]{:S(2)}) collective-permute-start(bf16[1,96,96]{2,1,0:T(8,128)(2,1)} %slice.343), channel_id=1, source_target_pairs={{8,0},{16,8},{24,16},{32,24},{40,32},{48,40},{56,48},{64,56},{72,6... | collective-permute-start | bytes 55304 | tf_op jit(solution)/shard_map/ppermute | solution.py:282
  12.8 93.6 %collective-permute-start.6 = (bf16[1,48,192]{2,1,0:T(8,128)(2,1)}, bf16[1,48,192]{2,1,0:T(8,128)(2,1)}, u32[]{:S(2)}, u32[]{:S(2)}) collective-permute-start(bf16[1,48,192]{2,1,0:T(8,128)(2,1)} %slice.379), channel_id=1, source_target_pairs={{8,0},{16,8},{24,16},{32,24},{40,32},{48,40},{56,48},{64,56},{72,6... | collective-permute-start | bytes 55304 | tf_op jit(solution)/shard_map/ppermute | solution.py:282
  22.4 95.3 %collective-permute-start.13 = (bf16[1,48,192]{2,1,0:T(8,128)(2,1)}, bf16[1,48,192]{2,1,0:T(8,128)(2,1)S(1)}, u32[]{:S(2)}, u32[]{:S(2)}) collective-permute-start(bf16[1,48,192]{2,1,0:T(8,128)(2,1)} %get-tuple-element.32), channel_id=1, source_target_pairs={{8,0},{16,8},{24,16},{32,24},{40,32},{48,40},{56,48},{64,56},{72,6... | collective-permute-start | bytes 55304 | tf_op jit(solution)/shard_map/ppermute | solution.py:295
  24.3 93.4 %collective-permute-start.12 = (bf16[1,48,192]{2,1,0:T(8,128)(2,1)}, bf16[1,48,192]{2,1,0:T(8,128)(2,1)}, u32[]{:S(2)}, u32[]{:S(2)}) collective-permute-start(bf16[1,48,192]{2,1,0:T(8,128)(2,1)} %get-tuple-element.31), channel_id=1, source_target_pairs={{0,8},{8,16},{16,24},{24,32},{32,40},{40,48},{48,56},{56,64},{64,7... | collective-permute-start | bytes 55304 | tf_op jit(solution)/shard_map/ppermute | solution.py:293
  99.6 39.2 %copy-start.37 = (f32[4,96,48]{1,2,0:T(8,128)S(1)}, f32[4,96,48]{1,2,0:T(8,128)}, u32[]{:S(2)}) copy-start(f32[4,96,48]{1,2,0:T(8,128)} %fusion.190) | copy-start | bytes 221188
  99.6 40.2 %copy-start.42 = (f32[4,96,1,48]{1,3,0,2:T(8,128)S(1)}, f32[4,96,1,48]{1,3,0,2:T(8,128)}, u32[]{:S(2)}) copy-start(f32[4,96,1,48]{1,3,0,2:T(8,128)} %convolution_bitcast_fusion.21) | copy-start | bytes 221188
  99.7 40.2 %copy-start.14 = (f32[4,2,96,2,48]{2,4,0,3,1:T(8,128)S(1)}, f32[4,2,96,2,48]{2,4,0,3,1:T(8,128)}, u32[]{:S(2)}) copy-start(f32[4,2,96,2,48]{2,4,0,3,1:T(8,128)} %copy.324) | copy-start | bytes 884740
  112.7 21.9 %collective-permute-start.1 = (bf16[5,1,96]{2,1,0:T(2,128)(2,1)S(1)}, bf16[5,1,96]{2,1,0:T(2,128)(2,1)S(1)}, u32[]{:S(2)}, u32[]{:S(2)}) collective-permute-start(bf16[5,1,96]{2,1,0:T(2,128)(2,1)S(1)} %slice.442), channel_id=1, source_target_pairs={{1,0},{2,1},{3,2},{4,3},{5,4},{6,5},{7,6},{9,8},{10,9},{11,10},{12... | collective-permute-start | bytes 2888 | tf_op jit(solution)/shard_map/ppermute | solution.py:282
  116.4 56.8 %collective-permute-start.7 = (bf16[3,1,192]{2,1,0:T(2,128)(2,1)}, bf16[3,1,192]{2,1,0:T(2,128)(2,1)S(1)}, u32[]{:S(2)}, u32[]{:S(2)}) collective-permute-start(bf16[3,1,192]{2,1,0:T(2,128)(2,1)} %slice.455), channel_id=1, source_target_pairs={{1,0},{2,1},{3,2},{4,3},{5,4},{6,5},{7,6},{9,8},{10,9},{11,10},{12... | collective-permute-start | bytes 3464 | tf_op jit(solution)/shard_map/ppermute | solution.py:282
  119.0 73.4 %collective-permute-start.14 = (bf16[4,1,192]{2,1,0:T(2,128)(2,1)}, bf16[4,1,192]{2,1,0:T(2,128)(2,1)S(1)}, u32[]{:S(2)}, u32[]{:S(2)}) collective-permute-start(bf16[4,1,192]{2,1,0:T(2,128)(2,1)} %get-tuple-element.27), channel_id=1, source_target_pairs={{1,0},{2,1},{3,2},{4,3},{5,4},{6,5},{7,6},{9,8},{10,9},{11,10},{12... | collective-permute-start | bytes 4616 | tf_op jit(solution)/shard_map/ppermute | solution.py:295
  120.3 84.6 %collective-permute-start.15 = (bf16[4,1,192]{2,1,0:T(2,128)(2,1)}, bf16[4,1,192]{2,1,0:T(2,128)(2,1)}, u32[]{:S(2)}, u32[]{:S(2)}) collective-permute-start(bf16[4,1,192]{2,1,0:T(2,128)(2,1)} %get-tuple-element.28), channel_id=1, source_target_pairs={{0,1},{1,2},{2,3},{3,4},{4,5},{5,6},{6,7},{8,9},{9,10},{10,11},{11... | collective-permute-start | bytes 4616 | tf_op jit(solution)/shard_map/ppermute | solution.py:293
  147.5 74.2 %collective-permute-start.3 = (bf16[1,192,48]{1,2,0:T(8,128)(2,1)}, bf16[1,192,48]{1,2,0:T(8,128)(2,1)}, u32[]{:S(2)}, u32[]{:S(2)}) collective-permute-start(bf16[1,192,48]{1,2,0:T(8,128)(2,1)} %get-tuple-element.16), channel_id=1, source_target_pairs={{8,0},{16,8},{24,16},{32,24},{40,32},{48,40},{56,48},{64,56},{72,6... | collective-permute-start | bytes 55304 | tf_op jit(solution)/shard_map/ppermute | solution.py:295
  149.4 72.3 %collective-permute-start.2 = (bf16[1,192,48]{1,2,0:T(8,128)(2,1)}, bf16[1,192,48]{1,2,0:T(8,128)(2,1)}, u32[]{:S(2)}, u32[]{:S(2)}) collective-permute-start(bf16[1,192,48]{1,2,0:T(8,128)(2,1)} %get-tuple-element.15), channel_id=1, source_target_pairs={{0,8},{8,16},{16,24},{24,32},{32,40},{40,48},{48,56},{56,64},{64,7... | collective-permute-start | bytes 55304 | tf_op jit(solution)/shard_map/ppermute | solution.py:293
  181.8 52.8 %collective-permute-start.9 = (bf16[1,96,96]{2,1,0:T(8,128)(2,1)}, bf16[1,96,96]{2,1,0:T(8,128)(2,1)}, u32[]{:S(2)}, u32[]{:S(2)}) collective-permute-start(bf16[1,96,96]{2,1,0:T(8,128)(2,1)} %get-tuple-element.30), channel_id=1, source_target_pairs={{8,0},{16,8},{24,16},{32,24},{40,32},{48,40},{56,48},{64,56},{72,6... | collective-permute-start | bytes 55304 | tf_op jit(solution)/shard_map/ppermute | solution.py:295
  192.5 42.2 %collective-permute-start.8 = (bf16[1,96,96]{2,1,0:T(8,128)(2,1)}, bf16[1,96,96]{2,1,0:T(8,128)(2,1)}, u32[]{:S(2)}, u32[]{:S(2)}) collective-permute-start(bf16[1,96,96]{2,1,0:T(8,128)(2,1)} %get-tuple-element.29), channel_id=1, source_target_pairs={{0,8},{8,16},{16,24},{24,32},{32,40},{40,48},{48,56},{56,64},{64,7... | collective-permute-start | bytes 55304 | tf_op jit(solution)/shard_map/ppermute | solution.py:293
  222.8 25.4 %collective-permute-start.4 = (bf16[10,1,48]{1,2,0:T(8,128)(2,1)S(1)}, bf16[10,1,48]{1,2,0:T(8,128)(2,1)S(1)}, u32[]{:S(2)}, u32[]{:S(2)}) collective-permute-start(bf16[10,1,48]{1,2,0:T(8,128)(2,1)S(1)} %get-tuple-element.13), channel_id=1, source_target_pairs={{1,0},{2,1},{3,2},{4,3},{5,4},{6,5},{7,6},{9,8},{10,9},{11,10},{12... | collective-permute-start | bytes 2888 | tf_op jit(solution)/shard_map/ppermute | solution.py:295
  224.1 24.1 %collective-permute-start.5 = (bf16[10,1,48]{1,2,0:T(8,128)(2,1)S(1)}, bf16[10,1,48]{1,2,0:T(8,128)(2,1)S(1)}, u32[]{:S(2)}, u32[]{:S(2)}) collective-permute-start(bf16[10,1,48]{1,2,0:T(8,128)(2,1)S(1)} %get-tuple-element.14), channel_id=1, source_target_pairs={{0,1},{1,2},{2,3},{3,4},{4,5},{5,6},{6,7},{8,9},{9,10},{10,11},{11... | collective-permute-start | bytes 2888 | tf_op jit(solution)/shard_map/ppermute | solution.py:293
  235.9 33.6 %collective-permute-start.10 = (bf16[6,1,96]{2,1,0:T(2,128)(2,1)}, bf16[6,1,96]{2,1,0:T(2,128)(2,1)}, u32[]{:S(2)}, u32[]{:S(2)}) collective-permute-start(bf16[6,1,96]{2,1,0:T(2,128)(2,1)} %get-tuple-element.19), channel_id=1, source_target_pairs={{1,0},{2,1},{3,2},{4,3},{5,4},{6,5},{7,6},{9,8},{10,9},{11,10},{12... | collective-permute-start | bytes 3464 | tf_op jit(solution)/shard_map/ppermute | solution.py:295
  237.2 32.3 %collective-permute-start.11 = (bf16[6,1,96]{2,1,0:T(2,128)(2,1)}, bf16[6,1,96]{2,1,0:T(2,128)(2,1)}, u32[]{:S(2)}, u32[]{:S(2)}) collective-permute-start(bf16[6,1,96]{2,1,0:T(2,128)(2,1)} %get-tuple-element.20), channel_id=1, source_target_pairs={{0,1},{1,2},{2,3},{3,4},{4,5},{5,6},{6,7},{8,9},{9,10},{10,11},{11... | collective-permute-start | bytes 3464 | tf_op jit(solution)/shard_map/ppermute | solution.py:293
  (47 other events, 823.1 us)

commit v2 on v1

v2 whole, which is shorter than its diff:
```python
import jax
import jax.numpy as jnp
import numpy as np
from jax import lax
from jax.experimental import pallas as pl
from jax.experimental.pallas import tpu as pltpu
from jax.sharding import PartitionSpec as P

EPSILON = 1e-06
MESH = pl.DeviceIdType.MESH
TOTAL = 804096
SHARE = 6282
WINDOW = 64
FLAT_ROWS = 6296


def share_place(share):
    row, col = divmod(share, 8)
    core, z_hi, y = row % 2, (row // 2) % 2, row // 4
    half, quarter = divmod(col, 4)
    return ((core * 4 + y) * 4 + quarter) * 4 + z_hi * 2 + half


def pack_shares(flat_ref, packed_ref):
    for share in range(128):
        start = SHARE * share // 1024 * 8
        place = share_place(share) * WINDOW
        packed_ref[place : place + WINDOW, :] = flat_ref[start : start + WINDOW, :].astype(jnp.bfloat16)


def reduce_kernel(
    packed_ref,
    out_ref,
    from_core,
    sum_core,
    from_plane,
    sum_plane,
    from_line,
    share_buf,
    square_buf,
    from_near,
    near_buf,
    from_far,
    core_sems,
    plane_send,
    plane_recv,
    line_send,
    line_recv,
    share_send,
    share_recv,
    near_send,
    near_recv,
    far_send,
    far_recv,
):
    x = lax.axis_index("branch")
    row = lax.axis_index("row")
    col = lax.axis_index("col")
    core, z_hi, y = row % 2, (row // 2) % 2, row // 4
    z = z_hi * 8 + col
    partner = (x, row + 1 - 2 * core, col)

    def plane_peer(step):
        there = (x * 4 + y + step) % 16
        return there, (there // 4, (there % 4) * 4 + z_hi * 2 + core, col)

    def line_peer(step):
        there = (z + step) % 16
        return (x, y * 4 + (there // 8) * 2 + core, there % 8)

    def near_peer(step):
        there = (y * 2 + core + step) % 8
        return (x, (there // 2) * 4 + z_hi * 2 + there % 2, col)

    def greet(peer):
        pl.semaphore_signal(barrier, inc=1, device_id=peer, device_id_type=MESH)

    barrier = pltpu.get_barrier_semaphore()
    greet(partner)

    @pl.loop(1, 16)
    def _(step):
        greet(plane_peer(step)[1])
        greet(line_peer(step))

    @pl.loop(1, 8)
    def _(step):
        greet(near_peer(step))

    pl.semaphore_wait(barrier, 38)

    def remote(src, dst, send_sem, recv_sem, peer):
        return pltpu.make_async_remote_copy(
            src_ref=src, dst_ref=dst, send_sem=send_sem, recv_sem=recv_sem,
            device_id=peer, device_id_type=MESH,
        )

    half = 64 * WINDOW
    across = remote(
        packed_ref.at[pl.ds(pl.multiple_of((1 - core) * half, half), half)],
        from_core, core_sems.at[0], core_sems.at[1], partner,
    )
    across.start()
    across.wait()

    @pl.loop(0, 16)
    def _(block):
        start = pl.multiple_of(block * 256, 256)
        mine = packed_ref[pl.ds(pl.multiple_of(core * half, half) + start, 256), :]
        theirs = from_core[pl.ds(start, 256), :]
        sum_core[pl.ds(start, 256), :] = (mine.astype(jnp.float32) + theirs.astype(jnp.float32)).astype(jnp.bfloat16)

    def plane_copy(step):
        there, peer = plane_peer(step)
        place = (there % 4) * 4 + there // 4
        return remote(
            sum_core.at[pl.ds(pl.multiple_of(place * 256, 256), 256)],
            from_plane.at[step - 1], plane_send.at[step - 1], plane_recv.at[step - 1], peer,
        )

    @pl.loop(1, 16)
    def _(step):
        plane_copy(step).start()

    @pl.loop(1, 16)
    def _(step):
        plane_copy(step).wait()

    @pl.loop(0, 4)
    def _(block):
        start = pl.multiple_of(block * WINDOW, WINDOW)
        own = pl.multiple_of((y * 4 + x) * 256 + start, WINDOW)
        total = sum_core[pl.ds(own, WINDOW), :].astype(jnp.float32)
        for step in range(15):
            total = total + from_plane[step, pl.ds(start, WINDOW), :].astype(jnp.float32)
        sum_plane[pl.ds(start, WINDOW), :] = total.astype(jnp.bfloat16)

    def line_copy(block):
        target = (block // 2) * 8 + (block % 2) * 4 + x
        step = (z - target + 16) % 16
        slot = (step + 15) % 16
        return step, remote(
            sum_plane.at[pl.ds(pl.multiple_of(block * WINDOW, WINDOW), WINDOW)],
            from_line.at[slot], line_send.at[block], line_recv.at[slot],
            (x, y * 4 + (target // 8) * 2 + core, target % 8),
        )

    for block in range(4):
        step, copy = line_copy(block)

        @pl.when(step != 0)
        def _():
            copy.start()

    owner_x = col % 4
    owner = owner_x == x

    def share_copy(step):
        return remote(
            share_buf, share_buf, share_send.at[step - 1], share_recv.at[0],
            ((x + step) % 4, row, col),
        )

    @pl.when(owner)
    def _():
        @pl.loop(0, 15)
        def _(slot):
            remote(
                sum_plane.at[pl.ds(0, WINDOW)], from_line.at[slot], line_send.at[0], line_recv.at[slot], partner
            ).wait_recv()

        own = pl.multiple_of((z_hi * 2 + col // 4) * WINDOW, WINDOW)
        total = sum_plane[pl.ds(own, WINDOW), :].astype(jnp.float32)
        for slot in range(15):
            total = total + from_line[slot].astype(jnp.float32)
        share_buf[...] = total
        for step in range(1, 4):
            share_copy(step).start()

    @pl.when(jnp.logical_not(owner))
    def _():
        share_copy(1).wait_recv()

    offset = (SHARE * (row * 8 + col)) % 1024
    place = lax.broadcasted_iota(jnp.int32, (WINDOW, 128), 0) * 128 + lax.broadcasted_iota(jnp.int32, (WINDOW, 128), 1)
    inside = jnp.logical_and(place >= offset, place < offset + SHARE)
    share = share_buf[...]
    squares = jnp.where(inside, share * share, 0.0)
    square_buf[...] = squares.reshape(8, 8, 128).sum(axis=0)

    def near_copy(step):
        return remote(
            square_buf, from_near.at[step - 1], near_send.at[step - 1], near_recv.at[step - 1], near_peer(step)
        )

    @pl.loop(1, 8)
    def _(step):
        near_copy(step).start()

    @pl.loop(1, 8)
    def _(step):
        near_copy(step).wait()

    near_buf[...] = square_buf[...] + from_near[...].sum(axis=0)

    def far_copy(step):
        return remote(
            near_buf, from_far.at[step - 1], far_send.at[step - 1], far_recv.at[step - 1], line_peer(step)
        )

    @pl.loop(1, 16)
    def _(step):
        far_copy(step).start()

    @pl.loop(1, 16)
    def _(step):
        far_copy(step).wait()

    total_squares = jnp.sum(near_buf[...] + from_far[...].sum(axis=0), keepdims=True)
    spread_rms = jnp.sqrt(total_squares / TOTAL + EPSILON)
    out_ref[...] = share_buf[...] * jnp.minimum(jnp.float32(1.0), 1.0 / spread_rms)

    for block in range(4):
        step, copy = line_copy(block)

        @pl.when(step != 0)
        def _():
            copy.wait_send()

    @pl.when(owner)
    def _():
        for step in range(1, 4):
            share_copy(step).wait_send()


def reduce_shares(packed):
    dma = pltpu.SemaphoreType.DMA
    window = pl.pallas_call(
        reduce_kernel,
        out_shape=jax.ShapeDtypeStruct((WINDOW, 128), jnp.float32),
        in_specs=[pl.BlockSpec(memory_space=pltpu.VMEM)],
        out_specs=pl.BlockSpec(memory_space=pltpu.VMEM),
        scratch_shapes=[
            pltpu.VMEM((64 * WINDOW, 128), jnp.bfloat16),
            pltpu.VMEM((64 * WINDOW, 128), jnp.bfloat16),
            pltpu.VMEM((15, 4 * WINDOW, 128), jnp.bfloat16),
            pltpu.VMEM((4 * WINDOW, 128), jnp.bfloat16),
            pltpu.VMEM((15, WINDOW, 128), jnp.bfloat16),
            pltpu.VMEM((WINDOW, 128), jnp.float32),
            pltpu.VMEM((8, 128), jnp.float32),
            pltpu.VMEM((7, 8, 128), jnp.float32),
            pltpu.VMEM((8, 128), jnp.float32),
            pltpu.VMEM((15, 8, 128), jnp.float32),
            dma((2,)),
            dma((15,)),
            dma((15,)),
            dma((4,)),
            dma((15,)),
            dma((3,)),
            dma((1,)),
            dma((7,)),
            dma((7,)),
            dma((15,)),
            dma((15,)),
        ],
        compiler_params=pltpu.CompilerParams(
            collective_id=0, has_side_effects=True, vmem_limit_bytes=32 * 1024 * 1024
        ),
        name="reduce_shares",
    )(packed)
    offset = (SHARE * lax.axis_index(("row", "col"))) % 1024
    return lax.dynamic_slice(window.reshape(WINDOW * 128), (offset,), (SHARE,))


GROUP = 384
CELLS = 24
PIECES = (
    (48, 0, 0, 432), (96, 162, 0, 864), (192, 810, 0, 1728), (96, 3402, 864, 432), (192, 3726, 1728, 864),
    (48, 5022, 432, 96), (48, 5058, 528, 192), (48, 5130, 720, 384), (96, 5274, 1296, 192),
    (96, 5418, 1488, 384), (192, 5706, 2592, 384),
)
BF16 = jnp.bfloat16
F32 = jnp.float32


def dot(left, right, left_dim=1, right_dim=0):
    return lax.dot_general(left, right, (((left_dim,), (right_dim,)), ((), ())), preferred_element_type=F32)


def lanes_of(rows, lanes):
    return lax.broadcasted_iota(jnp.int32, (rows, lanes), 1)


def halo_kernel(u1_ref, u2_ref, u3_ref, rows_ref, sides_ref, corners_ref, send_rows, send_sides, send_corners,
                recv_rows, recv_sides, recv_corners, send_sems, recv_sems):
    x = lax.axis_index("branch")
    row = lax.axis_index("row")
    col = lax.axis_index("col")
    line = x * 16 + row

    def peer(down, right):
        there = (line + down + 64) % 64
        return (there // 16, there % 16, (col + right + 8) % 8)

    routes = (
        (0, 1, 0, send_rows.at[0], recv_rows.at[0]),
        (1, -1, 0, send_rows.at[1], recv_rows.at[1]),
        (2, 0, 1, send_sides.at[0], recv_sides.at[0]),
        (3, 0, -1, send_sides.at[1], recv_sides.at[1]),
        (4, 1, 1, send_corners.at[0], recv_corners.at[0]),
        (5, 1, -1, send_corners.at[1], recv_corners.at[1]),
        (6, -1, 1, send_corners.at[2], recv_corners.at[2]),
        (7, -1, -1, send_corners.at[3], recv_corners.at[3]),
    )
    barrier = pltpu.get_barrier_semaphore()
    for slot, down, right, src, dst in routes:
        pl.semaphore_signal(barrier, inc=1, device_id=peer(down, right), device_id_type=MESH)

    u1 = u1_ref[...].astype(F32)
    u2 = u2_ref[...].astype(F32)
    u3 = u3_ref[...].astype(F32)
    wide = CELLS * GROUP
    last = wide - GROUP
    blank = jnp.zeros((1, wide), F32)
    bottom = jnp.concatenate([u1[4:8], u2[2:4], u3[1:2], blank], axis=0)
    top = jnp.concatenate([u2[0:2], u3[0:1], blank, u1[0:4]], axis=0)
    empty = jnp.zeros((8, GROUP), F32)
    for index, part in enumerate((bottom, top)):
        send_rows[index] = jnp.concatenate([part[:, : wide // 2], part[:, wide // 2 :]], axis=0).astype(BF16)
        send_corners[2 * index] = jnp.concatenate([part[:, last:], empty], axis=0).astype(BF16)
        send_corners[2 * index + 1] = jnp.concatenate([part[:, :GROUP], empty], axis=0).astype(BF16)
    for index, start in enumerate((last, 0)):
        send_sides[index] = jnp.concatenate(
            [u1[:, start : start + GROUP], u2[:, start : start + GROUP], u3[:, start : start + GROUP], empty[:2]], axis=0
        ).astype(BF16)

    pl.semaphore_wait(barrier, 8)

    def copy(route):
        slot, down, right, src, dst = route
        return pltpu.make_async_remote_copy(
            src_ref=src, dst_ref=dst, send_sem=send_sems.at[slot], recv_sem=recv_sems.at[slot],
            device_id=peer(down, right), device_id_type=MESH,
        )

    for route in routes:
        copy(route).start()
    for route in routes:
        copy(route).wait()

    above = jnp.where(line > 0, 1.0, 0.0)
    below = jnp.where(line < 63, 1.0, 0.0)
    left = jnp.where(col > 0, 1.0, 0.0)
    right = jnp.where(col < 7, 1.0, 0.0)
    rows_ref[0] = (recv_rows[0].astype(F32) * above).astype(BF16)
    rows_ref[1] = (recv_rows[1].astype(F32) * below).astype(BF16)
    sides_ref[0] = (recv_sides[0].astype(F32) * left).astype(BF16)
    sides_ref[1] = (recv_sides[1].astype(F32) * right).astype(BF16)
    corners_ref[0] = (recv_corners[0].astype(F32) * (above * left)).astype(BF16)
    corners_ref[1] = (recv_corners[1].astype(F32) * (above * right)).astype(BF16)
    corners_ref[2] = (recv_corners[2].astype(F32) * (below * left)).astype(BF16)
    corners_ref[3] = (recv_corners[3].astype(F32) * (below * right)).astype(BF16)


def exchange_halo(u1, u2, u3):
    shapes = ((2, 16, CELLS * GROUP // 2), (2, 16, GROUP), (4, 16, GROUP))
    whole = pl.BlockSpec(memory_space=pltpu.VMEM)
    return pl.pallas_call(
        halo_kernel,
        out_shape=[jax.ShapeDtypeStruct(shape, BF16) for shape in shapes],
        in_specs=[whole] * 3,
        out_specs=[whole] * 3,
        scratch_shapes=[pltpu.VMEM(shape, BF16) for shape in shapes + shapes]
        + [pltpu.SemaphoreType.DMA((8,)), pltpu.SemaphoreType.DMA((8,))],
        compiler_params=pltpu.CompilerParams(
            collective_id=1, has_side_effects=True, vmem_limit_bytes=32 * 1024 * 1024
        ),
        name="exchange_halo",
    )(u1, u2, u3)


def banded(weights, repeat, width, rows, blocks, dst):
    wide = dot(weights, repeat)
    lane = lanes_of(rows, repeat.shape[1])
    for block, pieces in enumerate(blocks):
        value = jnp.zeros((rows, repeat.shape[1]), F32)
        for tap, start in pieces:
            inside = jnp.logical_and(lane >= start, lane < start + width)
            value = jnp.where(inside, wide[tap * rows : (tap + 1) * rows], value)
        dst[block * rows : (block + 1) * rows, :] = value.astype(BF16)


def conv_blocks(tap_row, width, base):
    return [[(tap_row * 3 + tap, base + width * (n + 1 - tap)) for tap in range(3)] for n in range(GROUP // width)]


def down_blocks(tap_row, width):
    blocks = []
    for j in range(2 * (GROUP // width)):
        if j % 2 == 0:
            blocks.append([(tap_row * 3 + 1, width * (j // 2))])
        else:
            blocks.append([(tap_row * 3 + 2, width * (j // 2)), (tap_row * 3, width * (j // 2 + 1))])
    return blocks


def mixer_blocks(width, count):
    return [[(0, width * j)] for j in range(count)]


def window(value, start, width):
    first, end = start // 128, -(-(start + width) // 128)
    part = value[:, first * 128 : end * 128]
    shift = start - first * 128
    if shift:
        part = pltpu.roll(part, (end - first) * 128 - shift, 1)
    return part[:, : -(-width // 128) * 128]


def place(src, flat, width, flat_base, src_base, count):
    stride = GROUP // width
    rows = count // stride
    lane = lanes_of(rows, 128)
    held = {}
    for tile in range(3):
        value = None
        for j in range(stride):
            for part in range(-(-width // 128)):
                low = max(width * j + 128 * part, 128 * tile)
                high = min(width * j + min(width, 128 * part + 128), 128 * tile + 128)
                if low >= high:
                    continue
                if (j, part) not in held:
                    held[j, part] = src[part, pl.ds(src_base + j, rows, stride=stride), :]
                piece = held[j, part]
                shift = (width * j + 128 * part - 128 * tile) % 128
                if shift:
                    piece = pltpu.roll(piece, shift, 1)
                value = piece if value is None else jnp.where(lane >= low - 128 * tile, piece, value)
        flat[pl.ds(flat_base + tile, rows, stride=3), :] = value


def backward_kernel(
    rows_ref, sides_ref, corners_ref, f1_ref, f2_ref, f3_ref, f4_ref, o1_ref, o2_ref, o3_ref, u1_ref, u2_ref, u3_ref,
    k1_ref, k2_ref, k3_ref, s12_ref, s23_ref, m21_ref, m31_ref, m41_ref, m32_ref, m42_ref, m43_ref,
    rep1_ref, rep2_ref, rep3_ref, rep12_ref, rep23_ref, rep48_ref, rep96_ref, pool1_ref, pool2_ref, pool3_ref,
    g1_ref, g2_ref, g3_ref, g4_ref, packed_ref,
    ext1, ext2, ext3, v1, v2, v3, del1, del2, del3, pad_f2, pad_f3, pad_o1, pad_o2, pad_o3, rows_f4,
    band1, band2, band3, band12, band23, band21, band31, band32, res2, res3, w48, w96, w192, flat,
):
    half = CELLS // 2

    def lanes(g):
        return slice(GROUP * g, GROUP * (g + 1))

    u1, u2, u3 = (ref[...].astype(F32) for ref in (u1_ref, u2_ref, u3_ref))
    above, below = rows_ref[0].astype(F32), rows_ref[1].astype(F32)
    sides = [sides_ref[i].astype(F32) for i in range(2)]
    corners = [corners_ref[i].astype(F32) for i in range(4)]
    for g in range(CELLS + 2):
        if g == 0 or g == CELLS + 1:
            side = sides[0 if g == 0 else 1]
            mid = side[0:8], side[8:12], side[12:14]
            up = corners[0 if g == 0 else 1]
            down = corners[2 if g == 0 else 3]
        else:
            at = lanes(g - 1)
            mid = u1[:, at], u2[:, at], u3[:, at]
            row0 = 8 * ((g - 1) // half)
            there = lanes((g - 1) % half)
            up, down = above[row0 : row0 + 8, there], below[row0 : row0 + 8, there]
        ext1[g, 0:4, :] = up[0:4]
        ext1[g, 4:12, :] = mid[0]
        ext1[g, 12:16, :] = down[4:8]
        ext2[8 * g : 8 * g + 2, :] = up[4:6]
        ext2[8 * g + 2 : 8 * g + 6, :] = mid[1]
        ext2[8 * g + 6 : 8 * g + 8, :] = down[0:2]
        ext3[4 * g : 4 * g + 1, :] = up[6:7]
        ext3[4 * g + 1 : 4 * g + 3, :] = mid[2]
        ext3[4 * g + 3 : 4 * g + 4, :] = down[2:3]
    ext2[8 * (CELLS + 2) :, :] = jnp.zeros((8, GROUP), F32)
    ext3[4 * (CELLS + 2) :, :] = jnp.zeros((8, GROUP), F32)

    for ref in (pad_f2, pad_f3, pad_o1, pad_o2, pad_o3):
        ref[...] = jnp.zeros_like(ref)
    f2, f3, o1, o2, o3, f4 = (ref[...].astype(F32) for ref in (f2_ref, f3_ref, o1_ref, o2_ref, o3_ref, f4_ref))
    for g in range(CELLS):
        at = lanes(g)
        pad_f2[8 * g + 2 : 8 * g + 6, :] = f2[:, at]
        pad_f3[4 * g + 1 : 4 * g + 3, :] = f3[:, at]
        for tile in range(3):
            part = slice(GROUP * g + 128 * tile, GROUP * g + 128 * tile + 128)
            pad_o1[tile, 16 * g + 4 : 16 * g + 12, :] = o1[:, part]
            pad_o2[tile, 8 * g + 2 : 8 * g + 6, :] = o2[:, part]
        pad_o3[4 * g + 1 : 4 * g + 3, :] = o3[:, at]
        rows_f4[g : g + 1, :] = f4[:, at]

    for a in range(3):
        banded(k1_ref[...], rep1_ref[...], 48, 48, conv_blocks(a, 48, 128), band1.at[a])
        banded(k2_ref[...], rep2_ref[...], 96, 96, conv_blocks(a, 96, 128), band2.at[a])
        banded(k3_ref[...], rep3_ref[...], 192, 192, conv_blocks(a, 192, 256), band3.at[a])
        banded(s12_ref[...], rep12_ref[...], 96, 48, down_blocks(a, 96), band12.at[a])
        banded(s23_ref[...], rep23_ref[...], 192, 96, down_blocks(a, 192), band23.at[a])
    banded(m21_ref[...], rep48_ref[...], 48, 96, mixer_blocks(48, 4), band21)
    banded(m31_ref[...], rep48_ref[:, :128], 48, 192, mixer_blocks(48, 2), band31)
    banded(m32_ref[...], rep96_ref[...], 96, 192, mixer_blocks(96, 2), band32)

    tall1, tall2, tall3 = 16 * (CELLS + 2), 8 * (CELLS + 2), 4 * (CELLS + 2)
    def tiled_store(ref, value, rows=slice(None)):
        for tile in range(value.shape[1] // 128):
            ref[tile, rows, :] = value[:, 128 * tile : 128 * tile + 128]

    def strided(ref, tiles, start, count, stride):
        parts = [ref[tile, pl.ds(start, count, stride=stride), :] for tile in tiles]
        return parts[0] if len(parts) == 1 else jnp.concatenate(parts, axis=1)

    tiled_store(v1, dot(ext1[...].reshape(tall1, GROUP).astype(BF16), pool1_ref[...]))
    tiled_store(v2, dot(ext2[0:tall2, :].astype(BF16), pool2_ref[...]))
    tiled_store(v3, dot(ext3[0:tall3, :].astype(BF16), pool3_ref[...]))

    def strided_sum(ref, picks, count, stride, tiles):
        total = None
        for pick in picks:
            piece = strided(ref, tiles, pick, count, stride)
            total = piece if total is None else total + piece
        return total.astype(BF16)

    p12 = strided_sum(v1, range(2), tall2, 2, (0, 1))
    p13 = strided_sum(v1, range(4), tall3, 4, (2,))
    p14 = strided_sum(v1, range(16 + 4, 16 + 12), CELLS, 16, (3,))
    p23 = strided_sum(v2, range(2), tall3, 2, (0, 1))
    p24 = strided_sum(v2, range(8 + 2, 8 + 6), CELLS, 8, (2,))
    p34 = strided_sum(v3, range(4 + 1, 4 + 3), CELLS, 4, (0, 1))

    line = lax.axis_index("branch") * 16 + lax.axis_index("row")
    col = lax.axis_index("col")
    top, bottom = jnp.where(line > 0, 1.0, 0.0), jnp.where(line < 63, 1.0, 0.0)
    left, right = jnp.where(col > 0, 1.0, 0.0), jnp.where(col < 7, 1.0, 0.0)

    def rim_mask(rows, inner):
        place_row = lax.broadcasted_iota(jnp.int32, (CELLS + 2, rows, GROUP), 1)
        place_col = lax.broadcasted_iota(jnp.int32, (CELLS + 2, rows, GROUP), 0)
        start, end = (rows - inner) // 2, (rows + inner) // 2
        by_row = jnp.where(place_row == start - 1, top, jnp.where(place_row == end, bottom, 1.0))
        by_row = jnp.where(jnp.logical_and(place_row >= start - 1, place_row <= end), by_row, 0.0)
        by_col = jnp.where(place_col == 0, left, jnp.where(place_col == CELLS + 1, right, 1.0))
        return by_row * by_col

    def rolled(value):
        return pltpu.roll(value, value.shape[0] - 1, 0)

    x2 = jnp.concatenate([ext2[0:tall2, :], ext2[8 : tall2 + 8, 0:128]], axis=1).astype(BF16)
    tiled_store(v1, dot(x2, band12[1], 1, 1), pl.ds(0, tall2, stride=2))
    tiled_store(v1, dot(x2, band12[2], 1, 1) + rolled(dot(x2, band12[0], 1, 1)), pl.ds(1, tall2, stride=2))
    spread1 = jnp.concatenate([v1[tile] for tile in range(3)], axis=1)
    delta1 = ext1[...] + spread1.reshape(CELLS + 2, 16, GROUP)
    del1[...] = (delta1 * rim_mask(16, 8)).astype(BF16).astype(F32)

    x3 = jnp.concatenate([ext3[0:tall3, :], ext3[4 : tall3 + 4, 0:256]], axis=1).astype(BF16)
    tiled_store(v2, dot(x3, band23[1], 1, 1), pl.ds(0, tall3, stride=2))
    tiled_store(v2, dot(x3, band23[2], 1, 1) + rolled(dot(x3, band23[0], 1, 1)), pl.ds(1, tall3, stride=2))
    spread2 = jnp.concatenate([v2[tile] for tile in range(3)], axis=1)
    delta2 = ext2[0:tall2, :] + dot(p12, band21[...], 1, 1) + spread2
    del2[8 : 8 + tall2, :] = (delta2 * rim_mask(8, 4).reshape(tall2, GROUP)).astype(BF16).astype(F32)

    delta3 = ext3[0:tall3, :] + dot(p13, band31[...], 1, 1) + dot(p23, band32[...], 1, 1)
    place_row = lax.broadcasted_iota(jnp.int32, (tall3, GROUP), 0)
    in_group = jnp.bitwise_and(place_row, 3)
    by_row = jnp.where(in_group == 0, top, jnp.where(in_group == 3, bottom, 1.0))
    by_col = jnp.where(place_row < 4, left, jnp.where(place_row >= 4 * (CELLS + 1), right, 1.0))
    del3[8 : 8 + tall3, :] = (delta3 * (by_row * by_col)).astype(BF16).astype(F32)
    for ref in (del2, del3):
        ref[0:8, :] = jnp.zeros((8, GROUP), F32)
        ref[ref.shape[0] - 8 :, :] = jnp.zeros((8, GROUP), F32)

    def fold(grads, width, base, a, dst):
        total = None
        for n in range(GROUP // width):
            part = window(grads[n * width : (n + 1) * width, :], base + width * (n - 1), 3 * width)
            total = part if total is None else total + part
        for tap in range(3):
            start = (a * 3 + tap) * width
            tiled_store(dst, window(total, width * (2 - tap), width), slice(start, start + width))

    f1 = f1_ref[...]
    f1 = jnp.concatenate([f1[:, lanes(g)].astype(F32) for g in range(CELLS)], axis=0).astype(BF16)
    back = None
    for a in range(3):
        at = slice(5 - a, 13 - a)
        x1 = jnp.concatenate(
            [del1[0:CELLS, at, 256:GROUP], del1[1 : CELLS + 1, at, :], del1[2 : CELLS + 2, at, 0:128]], axis=2
        ).reshape(8 * CELLS, 640).astype(BF16)
        part = dot(x1, band1[a], 1, 1)
        back = part if back is None else back + part
        fold(dot(f1, x1, 0, 0), 48, 128, a, w48)
    for g in range(CELLS):
        g1_ref[:, lanes(g)] = back[8 * g : 8 * g + 8].astype(BF16)

    f2x = pad_f2[...].astype(BF16)
    back = None
    for a in range(3):
        at = 8 + 1 - a
        n = 8 * CELLS
        x2d = jnp.concatenate(
            [del2[at : at + n, 256:GROUP], del2[at + 8 : at + 8 + n, :], del2[at + 16 : at + 16 + n, 0:128]], axis=1
        ).astype(BF16)
        part = dot(x2d, band2[a], 1, 1)
        back = part if back is None else back + part
        fold(dot(f2x, x2d, 0, 0), 96, 128, a, w96)
    res2[...] = back
    for g in range(CELLS):
        g2_ref[:, lanes(g)] = res2[8 * g + 2 : 8 * g + 6, :].astype(BF16)

    f3x = pad_f3[...].astype(BF16)
    back = None
    for a in range(3):
        at = 8 + 1 - a
        n = 4 * CELLS
        x3d = jnp.concatenate(
            [del3[at : at + n, 128:GROUP], del3[at + 4 : at + 4 + n, :], del3[at + 8 : at + 8 + n, 0:256]], axis=1
        ).astype(BF16)
        part = dot(x3d, band3[a], 1, 1)
        back = part if back is None else back + part
        fold(dot(f3x, x3d, 0, 0), 192, 256, a, w192)
    res3[...] = back
    for g in range(CELLS):
        g3_ref[:, lanes(g)] = res3[4 * g + 1 : 4 * g + 3, :].astype(BF16)

    def fold_down(grads, width, rows, a, base, dst):
        for b in range(3):
            total = None
            for j in range(1 if b != 1 else 0, 2 * (GROUP // width), 2):
                p = (j + 1 - b) // 2
                part = window(grads[j * rows : (j + 1) * rows, :], width * p, width)
                total = part if total is None else total + part
            start = base + (a * 3 + b) * rows
            tiled_store(dst, total, slice(start, start + rows))

    def down_grads(saved, ext, skip, count, head, width, rows, base, dst):
        even = strided(saved, range(3), 0, count, 2).astype(BF16)
        odd = strided(saved, range(3), 1, count, 2).astype(BF16)
        for a in range(3):
            at = skip + (1 if a == 0 else 0)
            xs = jnp.concatenate(
                [ext[at : at + count, :], ext[at + skip : at + skip + count, 0:head]], axis=1
            ).astype(BF16)
            fold_down(dot(even if a == 1 else odd, xs, 0, 0), width, rows, a, base, dst)

    down_grads(pad_o1, ext2, 8, 8 * CELLS, 128, 96, 48, 864, w96)
    down_grads(pad_o2, ext3, 4, 4 * CELLS, 256, 192, 96, 1728, w192)

    def fold_mixer(grads, width, rows, base, dst):
        total = None
        for j in range(GROUP // rows):
            part = window(grads[j * rows : (j + 1) * rows, :], width * j, width)
            total = part if total is None else total + part
        tiled_store(dst, total, slice(base, base + rows))

    o2x = jnp.concatenate([pad_o2[tile] for tile in range(3)], axis=1).astype(BF16)
    o3x = pad_o3[...].astype(BF16)
    f4x = rows_f4[...].astype(BF16)
    inner2, inner3 = slice(8, 8 + 8 * CELLS), slice(4, 4 + 4 * CELLS)
    fold_mixer(dot(o2x, p12[inner2], 0, 0), 48, 96, 432, w48)
    fold_mixer(dot(o3x, p13[inner3], 0, 0), 48, 192, 528, w48)
    fold_mixer(dot(f4x, p14, 0, 0), 48, 384, 720, w48)
    fold_mixer(dot(o3x, p23[inner3], 0, 0), 96, 192, 1296, w96)
    fold_mixer(dot(f4x, p24, 0, 0), 96, 384, 1488, w96)
    fold_mixer(dot(f4x, p34, 0, 0), 192, 384, 2592, w192)
    back4 = (
        dot(p14[:, 0:48], m41_ref[...], 1, 1) + dot(p24[:, 0:96], m42_ref[...], 1, 1) + dot(p34[:, 0:192], m43_ref[...], 1, 1)
    )
    for g in range(CELLS):
        g4_ref[:, lanes(g)] = back4[g : g + 1].astype(BF16)

    for width, flat_base, src_base, count in PIECES:
        place({48: w48, 96: w96, 192: w192}[width], flat, width, flat_base, src_base, count)
    flat[6282:FLAT_ROWS, :] = jnp.zeros((FLAT_ROWS - 6282, 128), F32)
    pack_shares(flat, packed_ref)


def repeats(width, lanes, base=0):
    lane = np.arange(lanes)[None, :]
    return ((lane - base) % width == np.arange(width)[:, None]).astype(np.float32)


def pools(width, factors, parts):
    blocks = []
    for factor, lanes in zip(factors, parts):
        block = np.zeros((GROUP, lanes), np.float32)
        for lane in range(GROUP):
            block[lane, lane // (width * factor) * width + lane % width] = 1.0
        blocks.append(block)
    return np.concatenate(blocks, axis=1)


def local(f1, f2, f3, f4, o1, o2, o3, u1, u2, u3, k1, k2, k3, s12, s23, m21, m31, m41, m32, m42, m43):
    rows, sides, corners = exchange_halo(u1, u2, u3)
    constants = [
        jnp.asarray(value, BF16)
        for value in (
            repeats(48, 640, 128), repeats(96, 640, 128), repeats(192, 896, 256), repeats(96, 512), repeats(192, 640),
            repeats(48, 256), repeats(96, 256),
            pools(48, (2, 4, 8), (256, 128, 128)), pools(96, (2, 4), (256, 128)), pools(192, (2,), (256,)),
        )
    ]
    whole = pl.BlockSpec(memory_space=pltpu.VMEM)
    inputs = [
        rows, sides, corners, f1, f2, f3, f4, o1, o2, o3, u1, u2, u3,
        k1.reshape(432, 48), k2.reshape(864, 96), k3.reshape(1728, 192), s12.reshape(432, 96), s23.reshape(864, 192),
        m21, m31, m41, m32, m42, m43,
    ] + constants

    def f32(*shape):
        return pltpu.VMEM(shape, F32)

    def bf16(*shape):
        return pltpu.VMEM(shape, BF16)

    ext = CELLS + 2
    grad_one, grad_two, grad_three, grad_four, packed = pl.pallas_call(
        backward_kernel,
        out_shape=[jax.ShapeDtypeStruct(value.shape, BF16) for value in (f1, f2, f3, f4)]
        + [jax.ShapeDtypeStruct((128 * WINDOW, 128), BF16)],
        in_specs=[whole] * len(inputs),
        out_specs=[whole] * 5,
        scratch_shapes=[
            f32(ext, 16, GROUP), f32(8 * ext + 8, GROUP), f32(4 * ext + 8, GROUP),
            f32(4, 16 * ext, 128), f32(3, 8 * ext, 128), f32(2, 4 * ext, 128),
            f32(ext, 16, GROUP), f32(8 * ext + 16, GROUP), f32(4 * ext + 16, GROUP),
            f32(8 * CELLS, GROUP), f32(4 * CELLS, GROUP), f32(3, 16 * CELLS, 128), f32(3, 8 * CELLS, 128),
            f32(4 * CELLS, GROUP), f32(CELLS, GROUP),
            bf16(3, GROUP, 640), bf16(3, GROUP, 640), bf16(3, GROUP, 896), bf16(3, GROUP, 512), bf16(3, GROUP, 640),
            bf16(GROUP, 256), bf16(GROUP, 128), bf16(GROUP, 256),
            f32(8 * CELLS, GROUP), f32(4 * CELLS, GROUP),
            f32(1, 1104, 128), f32(1, 1872, 128), f32(2, 2976, 128), f32(FLAT_ROWS, 128),
        ],
        compiler_params=pltpu.CompilerParams(vmem_limit_bytes=56 * 1024 * 1024),
        name="backward",
    )(*inputs)
    return grad_one, grad_two, grad_three, grad_four, reduce_shares(packed)


def solution(mesh):
    in_specs = (
        P(("branch", "row"), "col"),
        P(("branch", "row"), "col"),
        P(("branch", "row"), "col"),
        P(("branch", "row"), "col"),
        P(("branch", "row"), "col"),
        P(("branch", "row"), "col"),
        P(("branch", "row"), "col"),
        P(("branch", "row"), "col"),
        P(("branch", "row"), "col"),
        P(("branch", "row"), "col"),
        P(),
        P(),
        P(),
        P(),
        P(),
        P(),
        P(),
        P(),
        P(),
        P(),
        P(),
    )
    out_specs = (
        P(("branch", "row"), "col"),
        P(("branch", "row"), "col"),
        P(("branch", "row"), "col"),
        P(("branch", "row"), "col"),
        P(("row", "col")),
    )
    return jax.shard_map(local, mesh=mesh, in_specs=in_specs, out_specs=out_specs, check_vma=False)
```

time: 381 us -> 120 us (0.31); the launches traced: 374 us -> 120 us
  matrix products: 109 us -> 0 us
  local copies, waits for them, and re-layouts: 102 us -> 14.5 us
  starting transfers between devices: 74.6 us -> 0 us
  Pallas kernels: 63.7 us -> 104 us
  other arithmetic: 22.3 us -> 0 us
    dot_general x102 -> x0, matrix products: 109 us -> none  [the longest x27 38.6 us: conv_backward(): jnp.einsum('hwo,io->hwi', grad_piece, weight[tap_row, tap_col], preferred...]
    ppermute x16 -> x0, starting transfers between devices: 74.6 us -> none  [the longest x6 51.8 us: with_halo(): lax.ppermute(tail, axis, [(i, (i + 1) % count) for i in range(ends)])]
    pallas_call x1 -> x2, Pallas kernels: 0.17 us -> 49.8 us  [the longest x1 33.5 us: exchange_halo(): pl.pallas_call(halo_kernel, out_shape=[jax.ShapeDtypeStruct(shape, BF16)...]
    reshape x22 -> x0, local copies, waits for them, and re-layouts: 31.4 us -> none  [the longest x11 20.4 us: local(): piece_grad.reshape(-1)]
    another operation x10 -> x0, local copies, waits for them, and re-layouts: 12.7 us -> none  [the longest x3 6.52 us: conv_backward(): return (result, jnp.stack(kernel_rows))]
    unnamed x128 -> x19, local copies, waits for them, and re-layouts: 25 us -> 13.8 us
    convert_element_type x6 -> x0, local copies, waits for them, and re-layouts: 10.5 us -> none  [the longest x5 8.61 us: local(): delta_one = (incoming_one + spread_one).astype(jnp.bfloat16)]
    dot_general x6 -> x0, local copies, waits for them, and re-layouts: 9.9 us -> none  [mixer_grad(): jnp.einsum('hwj,hwi->ji', source, pooled, preferred_element_type=jnp.floa...]
  transfers between devices with their start and end apart: 16 -> 0, of which waited for: 0 -> 0; matrix products, arithmetic and copies ran while one was open for 51% -> 0% of each run, Pallas kernels for 0% -> 0%
where the time goes in v2:
time: 120 us
  Pallas kernels  104 us (87%)
  local copies, waits for them, and re-layouts  14.5 us (12%)
    pallas_call x1, Pallas kernels, reduce_shares(): pl.pallas_call(reduce_kernel, out_shape=jax.ShapeDtypeStruct((WINDOW, 128...  54.6 us
    pallas_call x1, Pallas kernels, exchange_halo(): pl.pallas_call(halo_kernel, out_shape=[jax.ShapeDtypeStruct(shape, BF16)...  33.5 us
    pallas_call x1, Pallas kernels, local(): pl.pallas_call(backward_kernel, out_shape=[jax.ShapeDtypeStruct(value.sha...  16.3 us
    unnamed x19, local copies, waits for them, and re-layouts  13.8 us

profile of v2, /device:TPU:1, one launch (start us, length us, event | category | flops | bytes accessed | tf_op | source)
XLA Modules:
  0.0 119.6 jit_solution(8901767619693705951)
XLA Ops:
  0.6 0.0 copy-start.1
  0.6 0.9 copy-done.1
  1.5 0.0 copy-start.3
  1.5 0.9 copy-done.3
  2.4 0.0 copy-start.4
  2.4 0.8 copy-done.4
  3.2 33.5 %exchange_halo.1 = (bf16[2,16,4608]{2,1,0:T(8,128)(2,1)S(1)}, bf16[2,16,384]{2,1,0:T(8,128)(2,1)S(1)}, bf16[4,16,384]{2,1,0:T(8,128)(2,1)S(1)}) custom-call(bf16[8,9216]{1,0:T(8,128)(2,1)S(1)} %copy-done.1, bf16[4,9216]{1,0:T(4,128)(2,1)S(1)} %copy-done.3, bf16[2,9216]{1,0:T(2,128)(2,1)S(1)} %copy-done.4), custom_call_target="tpu_custom_call" | custom-call | tf_op jit(solution)/shard_map/exchange_halo/pallas_call | solution.py:368
  36.7 0.0 copy-start.2
  36.7 0.7 copy-done.2
  37.4 0.0 copy-start.5
  37.4 0.6 copy-done.5
  38.0 0.0 copy-start.6
  38.0 0.6 copy-done.6
  38.6 1.4 %copy.36.m21_ref = bf16[96,48]{1,0:T(8,128)(2,1)} copy(bf16[96,48]{0,1:T(8,128)(2,1)} %param.46) | data formatting | bytes 18432 | tf_op args[15]
  40.1 1.4 %copy.37.m31_ref = bf16[192,48]{1,0:T(8,128)(2,1)} copy(bf16[192,48]{0,1:T(8,128)(2,1)} %param.47) | data formatting | bytes 36864 | tf_op args[16]
  41.5 1.5 %copy.38.m41_ref = bf16[384,48]{1,0:T(8,128)(2,1)} copy(bf16[384,48]{0,1:T(8,128)(2,1)} %param.48) | data formatting | bytes 73728 | tf_op args[17]
  43.0 1.6 %copy.39.m42_ref = bf16[384,96]{1,0:T(8,128)(2,1)} copy(bf16[384,96]{0,1:T(8,128)(2,1)} %param.50) | data formatting | bytes 147456 | tf_op args[19]
  44.6 1.7 %copy.40.m43_ref = bf16[384,192]{1,0:T(8,128)(2,1)} copy(bf16[384,192]{0,1:T(8,128)(2,1)} %param.51) | data formatting | bytes 294912 | tf_op args[20]
  46.4 16.3 %backward.1 = (bf16[8,9216]{1,0:T(8,128)(2,1)}, bf16[4,9216]{1,0:T(4,128)(2,1)}, bf16[2,9216]{1,0:T(2,128)(2,1)}, bf16[1,9216]{1,0:T(2,128)(2,1)}, bf16[8192,128]{1,0:T(8,128)(2,1)}) custom-call(bf16[2,16,4608]{2,1,0:T(8,128)(2,1)} %copy-done.2, bf16[2,16,384]{2,1,0:T(8,128)(2,1)} %copy-done.6, bf16[4,16,384]{2,1,0:T(8,128)(2,1)} %copy-done.5, ...), custom_call_target="tpu_custom_call" | custom-call | tf_op jit(solution)/shard_map/backward/pallas_call | solution.py:720
  62.6 0.0 copy-start
  62.6 1.6 %copy-done = bf16[8192,128]{1,0:T(8,128)(2,1)S(1)} copy-done((bf16[8192,128]{1,0:T(8,128)(2,1)S(1)}, bf16[8192,128]{1,0:T(8,128)(2,1)}, u32[]{:S(2)}) %copy-start) | copy-done | bytes 2097176
  64.2 54.6 %reduce_shares.1 = f32[64,128]{1,0:T(8,128)S(1)} custom-call(bf16[8192,128]{1,0:T(8,128)(2,1)S(1)} %copy-done), custom_call_target="tpu_custom_call" | custom-call | tf_op jit(solution)/shard_map/reduce_shares/pallas_call | solution.py:238
  118.9 0.7 dynamic_slice.3
Async XLA Ops:
  0.6 0.9 copy-start.1
  1.5 0.9 copy-start.3
  2.4 0.8 copy-start.4
  36.7 0.7 copy-start.2
  37.4 0.6 copy-start.5
  38.0 0.6 copy-start.6
  62.6 1.6 %copy-start = (bf16[8192,128]{1,0:T(8,128)(2,1)S(1)}, bf16[8192,128]{1,0:T(8,128)(2,1)}, u32[]{:S(2)}) copy-start(bf16[8192,128]{1,0:T(8,128)(2,1)} %get-tuple-element.20.packed_ref) | copy-start | bytes 6291460

commit v3 on v2

v3 whole, which is shorter than its diff:
```python
import jax
import jax.numpy as jnp
import numpy as np
from jax import lax
from jax.experimental import pallas as pl
from jax.experimental.pallas import tpu as pltpu
from jax.sharding import PartitionSpec as P

EPSILON = 1e-06
MESH = pl.DeviceIdType.MESH
TOTAL = 804096
SHARE = 6282
WINDOW = 64
FLAT_ROWS = 6296


def share_place(share):
    row, col = divmod(share, 8)
    core, z_hi, y = row % 2, (row // 2) % 2, row // 4
    half, quarter = divmod(col, 4)
    return ((core * 4 + y) * 4 + quarter) * 4 + z_hi * 2 + half


def pack_shares(flat_ref, packed_ref):
    for share in range(128):
        start = SHARE * share // 1024 * 8
        place = share_place(share) * WINDOW
        packed_ref[place : place + WINDOW, :] = flat_ref[start : start + WINDOW, :].astype(jnp.bfloat16)


def reduce_stages(
    packed_ref,
    out_ref,
    from_core,
    sum_core,
    from_plane,
    sum_plane,
    from_line,
    share_buf,
    square_buf,
    from_near,
    near_buf,
    from_far,
    core_sems,
    plane_send,
    plane_recv,
    line_send,
    line_recv,
    share_send,
    share_recv,
    near_send,
    near_recv,
    far_send,
    far_recv,
):
    x = lax.axis_index("branch")
    row = lax.axis_index("row")
    col = lax.axis_index("col")
    core, z_hi, y = row % 2, (row // 2) % 2, row // 4
    z = z_hi * 8 + col
    partner = (x, row + 1 - 2 * core, col)

    def plane_peer(step):
        there = (x * 4 + y + step) % 16
        return there, (there // 4, (there % 4) * 4 + z_hi * 2 + core, col)

    def line_peer(step):
        there = (z + step) % 16
        return (x, y * 4 + (there // 8) * 2 + core, there % 8)

    def near_peer(step):
        there = (y * 2 + core + step) % 8
        return (x, (there // 2) * 4 + z_hi * 2 + there % 2, col)

    def remote(src, dst, send_sem, recv_sem, peer):
        return pltpu.make_async_remote_copy(
            src_ref=src, dst_ref=dst, send_sem=send_sem, recv_sem=recv_sem,
            device_id=peer, device_id_type=MESH,
        )

    half = 64 * WINDOW
    across = remote(
        packed_ref.at[pl.ds(pl.multiple_of((1 - core) * half, half), half)],
        from_core, core_sems.at[0], core_sems.at[1], partner,
    )
    across.start()
    across.wait()

    @pl.loop(0, 16)
    def _(block):
        start = pl.multiple_of(block * 256, 256)
        mine = packed_ref[pl.ds(pl.multiple_of(core * half, half) + start, 256), :]
        theirs = from_core[pl.ds(start, 256), :]
        sum_core[pl.ds(start, 256), :] = (mine.astype(jnp.float32) + theirs.astype(jnp.float32)).astype(jnp.bfloat16)

    def plane_copy(step):
        there, peer = plane_peer(step)
        place = (there % 4) * 4 + there // 4
        return remote(
            sum_core.at[pl.ds(pl.multiple_of(place * 256, 256), 256)],
            from_plane.at[step - 1], plane_send.at[step - 1], plane_recv.at[step - 1], peer,
        )

    @pl.loop(1, 16)
    def _(step):
        plane_copy(step).start()

    @pl.loop(1, 16)
    def _(step):
        plane_copy(step).wait()

    @pl.loop(0, 4)
    def _(block):
        start = pl.multiple_of(block * WINDOW, WINDOW)
        own = pl.multiple_of((y * 4 + x) * 256 + start, WINDOW)
        total = sum_core[pl.ds(own, WINDOW), :].astype(jnp.float32)
        for step in range(15):
            total = total + from_plane[step, pl.ds(start, WINDOW), :].astype(jnp.float32)
        sum_plane[pl.ds(start, WINDOW), :] = total.astype(jnp.bfloat16)

    def line_copy(block):
        target = (block // 2) * 8 + (block % 2) * 4 + x
        step = (z - target + 16) % 16
        slot = (step + 15) % 16
        return step, remote(
            sum_plane.at[pl.ds(pl.multiple_of(block * WINDOW, WINDOW), WINDOW)],
            from_line.at[slot], line_send.at[block], line_recv.at[slot],
            (x, y * 4 + (target // 8) * 2 + core, target % 8),
        )

    for block in range(4):
        step, copy = line_copy(block)

        @pl.when(step != 0)
        def _():
            copy.start()

    owner_x = col % 4
    owner = owner_x == x

    def share_copy(step):
        return remote(
            share_buf, share_buf, share_send.at[step - 1], share_recv.at[0],
            ((x + step) % 4, row, col),
        )

    @pl.when(owner)
    def _():
        @pl.loop(0, 15)
        def _(slot):
            remote(
                sum_plane.at[pl.ds(0, WINDOW)], from_line.at[slot], line_send.at[0], line_recv.at[slot], partner
            ).wait_recv()

        own = pl.multiple_of((z_hi * 2 + col // 4) * WINDOW, WINDOW)
        total = sum_plane[pl.ds(own, WINDOW), :].astype(jnp.float32)
        for slot in range(15):
            total = total + from_line[slot].astype(jnp.float32)
        share_buf[...] = total
        for step in range(1, 4):
            share_copy(step).start()

    @pl.when(jnp.logical_not(owner))
    def _():
        share_copy(1).wait_recv()

    offset = (SHARE * (row * 8 + col)) % 1024
    place = lax.broadcasted_iota(jnp.int32, (WINDOW, 128), 0) * 128 + lax.broadcasted_iota(jnp.int32, (WINDOW, 128), 1)
    inside = jnp.logical_and(place >= offset, place < offset + SHARE)
    share = share_buf[...]
    squares = jnp.where(inside, share * share, 0.0)
    square_buf[...] = squares.reshape(8, 8, 128).sum(axis=0)

    def near_copy(step):
        return remote(
            square_buf, from_near.at[step - 1], near_send.at[step - 1], near_recv.at[step - 1], near_peer(step)
        )

    @pl.loop(1, 8)
    def _(step):
        near_copy(step).start()

    @pl.loop(1, 8)
    def _(step):
        near_copy(step).wait()

    near_buf[...] = square_buf[...] + from_near[...].sum(axis=0)

    def far_copy(step):
        return remote(
            near_buf, from_far.at[step - 1], far_send.at[step - 1], far_recv.at[step - 1], line_peer(step)
        )

    @pl.loop(1, 16)
    def _(step):
        far_copy(step).start()

    @pl.loop(1, 16)
    def _(step):
        far_copy(step).wait()

    total_squares = jnp.sum(near_buf[...] + from_far[...].sum(axis=0), keepdims=True)
    spread_rms = jnp.sqrt(total_squares / TOTAL + EPSILON)
    out_ref[...] = share_buf[...] * jnp.minimum(jnp.float32(1.0), 1.0 / spread_rms)

    for block in range(4):
        step, copy = line_copy(block)

        @pl.when(step != 0)
        def _():
            copy.wait_send()

    @pl.when(owner)
    def _():
        for step in range(1, 4):
            share_copy(step).wait_send()


GROUP = 384
CELLS = 24
PIECES = (
    (48, 0, 0, 432), (96, 162, 0, 864), (192, 810, 0, 1728), (96, 3402, 864, 432), (192, 3726, 1728, 864),
    (48, 5022, 432, 96), (48, 5058, 528, 192), (48, 5130, 720, 384), (96, 5274, 1296, 192),
    (96, 5418, 1488, 384), (192, 5706, 2592, 384),
)
BF16 = jnp.bfloat16
F32 = jnp.float32


def dot(left, right, left_dim=1, right_dim=0):
    return lax.dot_general(left, right, (((left_dim,), (right_dim,)), ((), ())), preferred_element_type=F32)


def lanes_of(rows, lanes):
    return lax.broadcasted_iota(jnp.int32, (rows, lanes), 1)


def fill_packets(u1, u2, u3, send_rows, send_sides, send_corners):
    wide = CELLS * GROUP
    last = wide - GROUP
    blank = jnp.zeros((1, wide), F32)
    bottom = jnp.concatenate([u1[4:8], u2[2:4], u3[1:2], blank], axis=0)
    top = jnp.concatenate([u2[0:2], u3[0:1], blank, u1[0:4]], axis=0)
    empty = jnp.zeros((8, GROUP), F32)
    for index, part in enumerate((bottom, top)):
        send_rows[index] = jnp.concatenate([part[:, : wide // 2], part[:, wide // 2 :]], axis=0).astype(BF16)
        send_corners[2 * index] = jnp.concatenate([part[:, last:], empty], axis=0).astype(BF16)
        send_corners[2 * index + 1] = jnp.concatenate([part[:, :GROUP], empty], axis=0).astype(BF16)
    for index, start in enumerate((last, 0)):
        send_sides[index] = jnp.concatenate(
            [u1[:, start : start + GROUP], u2[:, start : start + GROUP], u3[:, start : start + GROUP], empty[:2]], axis=0
        ).astype(BF16)


def banded(weights, repeat, width, rows, blocks, dst):
    wide = dot(weights, repeat)
    lane = lanes_of(rows, repeat.shape[1])
    for block, pieces in enumerate(blocks):
        value = jnp.zeros((rows, repeat.shape[1]), F32)
        for tap, start in pieces:
            inside = jnp.logical_and(lane >= start, lane < start + width)
            value = jnp.where(inside, wide[tap * rows : (tap + 1) * rows], value)
        dst[block * rows : (block + 1) * rows, :] = value.astype(BF16)


def conv_blocks(tap_row, width, base):
    return [[(tap_row * 3 + tap, base + width * (n + 1 - tap)) for tap in range(3)] for n in range(GROUP // width)]


def down_blocks(tap_row, width):
    blocks = []
    for j in range(2 * (GROUP // width)):
        if j % 2 == 0:
            blocks.append([(tap_row * 3 + 1, width * (j // 2))])
        else:
            blocks.append([(tap_row * 3 + 2, width * (j // 2)), (tap_row * 3, width * (j // 2 + 1))])
    return blocks


def mixer_blocks(width, count):
    return [[(0, width * j)] for j in range(count)]


def window(value, start, width):
    first, end = start // 128, -(-(start + width) // 128)
    part = value[:, first * 128 : end * 128]
    shift = start - first * 128
    if shift:
        part = pltpu.roll(part, (end - first) * 128 - shift, 1)
    return part[:, : -(-width // 128) * 128]


def place(src, flat, width, flat_base, src_base, count):
    stride = GROUP // width
    rows = count // stride
    lane = lanes_of(rows, 128)
    held = {}
    for tile in range(3):
        value = None
        for j in range(stride):
            for part in range(-(-width // 128)):
                low = max(width * j + 128 * part, 128 * tile)
                high = min(width * j + min(width, 128 * part + 128), 128 * tile + 128)
                if low >= high:
                    continue
                if (j, part) not in held:
                    held[j, part] = src[part, pl.ds(src_base + j, rows, stride=stride), :]
                piece = held[j, part]
                shift = (width * j + 128 * part - 128 * tile) % 128
                if shift:
                    piece = pltpu.roll(piece, shift, 1)
                value = piece if value is None else jnp.where(lane >= low - 128 * tile, piece, value)
        flat[pl.ds(flat_base + tile, rows, stride=3), :] = value


def backward_kernel(
    f1_ref, f2_ref, f3_ref, f4_ref, o1_ref, o2_ref, o3_ref, u1_ref, u2_ref, u3_ref,
    k1_ref, k2_ref, k3_ref, s12_ref, s23_ref, m21_ref, m31_ref, m41_ref, m32_ref, m42_ref, m43_ref,
    rep1_ref, rep2_ref, rep3_ref, rep12_ref, rep23_ref, rep96_ref, rep192_ref, pool1_ref, pool2_ref, pool3_ref,
    g1_ref, g2_ref, g3_ref, g4_ref, share_ref,
    packed_ref, send_rows, send_sides, send_corners, recv_rows, recv_sides, recv_corners, halo_send, halo_recv,
    ext1, ext2, ext3, v1, v2, v3, del1, del2, del3, pad_f2, pad_f3, pad_o1, pad_o2, pad_o3, rows_f4,
    band1, band2, band3, band12, band23, band21, band31, band32, res2, res3, w48, w96, w192, flat, *reduce_refs,
):
    half = CELLS // 2

    def lanes(g):
        return slice(GROUP * g, GROUP * (g + 1))

    x = lax.axis_index("branch")
    row = lax.axis_index("row")
    col = lax.axis_index("col")
    core, z_hi, y = row % 2, (row // 2) % 2, row // 4
    z = z_hi * 8 + col
    line = x * 16 + row

    def peer(down, right):
        there = (line + down + 64) % 64
        return (there // 16, there % 16, (col + right + 8) % 8)

    routes = (
        (0, 1, 0, send_rows.at[0], recv_rows.at[0]),
        (1, -1, 0, send_rows.at[1], recv_rows.at[1]),
        (2, 0, 1, send_sides.at[0], recv_sides.at[0]),
        (3, 0, -1, send_sides.at[1], recv_sides.at[1]),
        (4, 1, 1, send_corners.at[0], recv_corners.at[0]),
        (5, 1, -1, send_corners.at[1], recv_corners.at[1]),
        (6, -1, 1, send_corners.at[2], recv_corners.at[2]),
        (7, -1, -1, send_corners.at[3], recv_corners.at[3]),
    )

    def plane_peer(step):
        there = (x * 4 + y + step) % 16
        return there, (there // 4, (there % 4) * 4 + z_hi * 2 + core, col)

    def line_peer(step):
        there = (z + step) % 16
        return (x, y * 4 + (there // 8) * 2 + core, there % 8)

    def near_peer(step):
        there = (y * 2 + core + step) % 8
        return (x, (there // 2) * 4 + z_hi * 2 + there % 2, col)

    def greet(peer):
        pl.semaphore_signal(barrier, inc=1, device_id=peer, device_id_type=MESH)

    barrier = pltpu.get_barrier_semaphore()
    for route in routes:
        greet(peer(route[1], route[2]))
    greet((x, row + 1 - 2 * core, col))

    @pl.loop(1, 16)
    def _(step):
        greet(plane_peer(step)[1])
        greet(line_peer(step))

    @pl.loop(1, 8)
    def _(step):
        greet(near_peer(step))

    u1, u2, u3 = (ref[...].astype(F32) for ref in (u1_ref, u2_ref, u3_ref))
    fill_packets(u1, u2, u3, send_rows, send_sides, send_corners)
    pl.semaphore_wait(barrier, 46)

    def halo_copy(route):
        slot, down, right, src, dst = route
        return pltpu.make_async_remote_copy(
            src_ref=src, dst_ref=dst, send_sem=halo_send.at[slot], recv_sem=halo_recv.at[slot],
            device_id=peer(down, right), device_id_type=MESH,
        )

    for route in routes:
        halo_copy(route).start()

    for ref in (pad_f2, pad_f3, pad_o1, pad_o2, pad_o3):
        ref[...] = jnp.zeros_like(ref)
    f2, f3, o1, o2, o3, f4 = (ref[...].astype(F32) for ref in (f2_ref, f3_ref, o1_ref, o2_ref, o3_ref, f4_ref))
    for g in range(CELLS):
        at = lanes(g)
        pad_f2[8 * g + 2 : 8 * g + 6, :] = f2[:, at]
        pad_f3[4 * g + 1 : 4 * g + 3, :] = f3[:, at]
        for tile in range(3):
            part = slice(GROUP * g + 128 * tile, GROUP * g + 128 * tile + 128)
            pad_o1[tile, 16 * g + 4 : 16 * g + 12, :] = o1[:, part]
            pad_o2[tile, 8 * g + 2 : 8 * g + 6, :] = o2[:, part]
        pad_o3[4 * g + 1 : 4 * g + 3, :] = o3[:, at]
        rows_f4[g : g + 1, :] = f4[:, at]

    for a in range(3):
        banded(k1_ref[...], rep1_ref[...], 48, 48, conv_blocks(a, 48, 128), band1.at[a])
        banded(k2_ref[...], rep2_ref[...], 96, 96, conv_blocks(a, 96, 128), band2.at[a])
        banded(k3_ref[...], rep3_ref[...], 192, 192, conv_blocks(a, 192, 256), band3.at[a])
        banded(s12_ref[...], rep12_ref[...], 96, 48, down_blocks(a, 96), band12.at[a])
        banded(s23_ref[...], rep23_ref[...], 192, 96, down_blocks(a, 192), band23.at[a])
    banded(m21_ref[...], rep96_ref[...], 96, 48, mixer_blocks(96, 4), band21)
    banded(m31_ref[...], rep192_ref[...], 192, 48, mixer_blocks(192, 2), band31)
    banded(m32_ref[...], rep96_ref[:, :256], 96, 192, mixer_blocks(96, 2), band32)

    for route in routes:
        halo_copy(route).wait()
    top, bottom = jnp.where(line > 0, 1.0, 0.0), jnp.where(line < 63, 1.0, 0.0)
    left, right = jnp.where(col > 0, 1.0, 0.0), jnp.where(col < 7, 1.0, 0.0)
    above, below = recv_rows[0].astype(F32) * top, recv_rows[1].astype(F32) * bottom
    sides = [recv_sides[0].astype(F32) * left, recv_sides[1].astype(F32) * right]
    corners = [
        recv_corners[0].astype(F32) * (top * left), recv_corners[1].astype(F32) * (top * right),
        recv_corners[2].astype(F32) * (bottom * left), recv_corners[3].astype(F32) * (bottom * right),
    ]
    for g in range(CELLS + 2):
        if g == 0 or g == CELLS + 1:
            side = sides[0 if g == 0 else 1]
            mid = side[0:8], side[8:12], side[12:14]
            up = corners[0 if g == 0 else 1]
            down = corners[2 if g == 0 else 3]
        else:
            at = lanes(g - 1)
            mid = u1[:, at], u2[:, at], u3[:, at]
            row0 = 8 * ((g - 1) // half)
            there = lanes((g - 1) % half)
            up, down = above[row0 : row0 + 8, there], below[row0 : row0 + 8, there]
        ext1[g, 0:4, :] = up[0:4]
        ext1[g, 4:12, :] = mid[0]
        ext1[g, 12:16, :] = down[4:8]
        ext2[8 * g : 8 * g + 2, :] = up[4:6]
        ext2[8 * g + 2 : 8 * g + 6, :] = mid[1]
        ext2[8 * g + 6 : 8 * g + 8, :] = down[0:2]
        ext3[4 * g : 4 * g + 1, :] = up[6:7]
        ext3[4 * g + 1 : 4 * g + 3, :] = mid[2]
        ext3[4 * g + 3 : 4 * g + 4, :] = down[2:3]
    ext2[8 * (CELLS + 2) :, :] = jnp.zeros((8, GROUP), F32)
    ext3[4 * (CELLS + 2) :, :] = jnp.zeros((8, GROUP), F32)

    tall1, tall2, tall3 = 16 * (CELLS + 2), 8 * (CELLS + 2), 4 * (CELLS + 2)
    def tiled_store(ref, value, rows=slice(None)):
        for tile in range(value.shape[1] // 128):
            ref[tile, rows, :] = value[:, 128 * tile : 128 * tile + 128]

    def strided(ref, tiles, start, count, stride):
        parts = [ref[tile, pl.ds(start, count, stride=stride), :] for tile in tiles]
        return parts[0] if len(parts) == 1 else jnp.concatenate(parts, axis=1)

    tiled_store(v1, dot(ext1[...].reshape(tall1, GROUP).astype(BF16), pool1_ref[...]))
    tiled_store(v2, dot(ext2[0:tall2, :].astype(BF16), pool2_ref[...]))
    tiled_store(v3, dot(ext3[0:tall3, :].astype(BF16), pool3_ref[...]))

    def strided_sum(ref, picks, count, stride, tiles):
        total = None
        for pick in picks:
            piece = strided(ref, tiles, pick, count, stride)
            total = piece if total is None else total + piece
        return total.astype(BF16)

    p12 = strided_sum(v1, range(2), tall2, 2, (0, 1))
    p13 = strided_sum(v1, range(4), tall3, 4, (2,))
    p14 = strided_sum(v1, range(16 + 4, 16 + 12), CELLS, 16, (3,))
    p23 = strided_sum(v2, range(2), tall3, 2, (0, 1))
    p24 = strided_sum(v2, range(8 + 2, 8 + 6), CELLS, 8, (2,))
    p34 = strided_sum(v3, range(4 + 1, 4 + 3), CELLS, 4, (0, 1))

    def rim_mask(rows, inner):
        place_row = lax.broadcasted_iota(jnp.int32, (CELLS + 2, rows, GROUP), 1)
        place_col = lax.broadcasted_iota(jnp.int32, (CELLS + 2, rows, GROUP), 0)
        start, end = (rows - inner) // 2, (rows + inner) // 2
        by_row = jnp.where(place_row == start - 1, top, jnp.where(place_row == end, bottom, 1.0))
        by_row = jnp.where(jnp.logical_and(place_row >= start - 1, place_row <= end), by_row, 0.0)
        by_col = jnp.where(place_col == 0, left, jnp.where(place_col == CELLS + 1, right, 1.0))
        return by_row * by_col

    def rolled(value):
        return pltpu.roll(value, value.shape[0] - 1, 0)

    x2 = jnp.concatenate([ext2[0:tall2, :], ext2[8 : tall2 + 8, 0:128]], axis=1).astype(BF16)
    tiled_store(v1, dot(x2, band12[1], 1, 1), pl.ds(0, tall2, stride=2))
    tiled_store(v1, dot(x2, band12[2], 1, 1) + rolled(dot(x2, band12[0], 1, 1)), pl.ds(1, tall2, stride=2))
    spread1 = jnp.concatenate([v1[tile] for tile in range(3)], axis=1)
    delta1 = ext1[...] + spread1.reshape(CELLS + 2, 16, GROUP)
    del1[...] = (delta1 * rim_mask(16, 8)).astype(BF16).astype(F32)

    x3 = jnp.concatenate([ext3[0:tall3, :], ext3[4 : tall3 + 4, 0:256]], axis=1).astype(BF16)
    tiled_store(v2, dot(x3, band23[1], 1, 1), pl.ds(0, tall3, stride=2))
    tiled_store(v2, dot(x3, band23[2], 1, 1) + rolled(dot(x3, band23[0], 1, 1)), pl.ds(1, tall3, stride=2))
    spread2 = jnp.concatenate([v2[tile] for tile in range(3)], axis=1)
    delta2 = ext2[0:tall2, :] + dot(p12[:, 0:192], band21[...]) + spread2
    del2[8 : 8 + tall2, :] = (delta2 * rim_mask(8, 4).reshape(tall2, GROUP)).astype(BF16).astype(F32)

    delta3 = ext3[0:tall3, :] + dot(p13[:, 0:96], band31[...]) + dot(p23, band32[...], 1, 1)
    place_row = lax.broadcasted_iota(jnp.int32, (tall3, GROUP), 0)
    in_group = jnp.bitwise_and(place_row, 3)
    by_row = jnp.where(in_group == 0, top, jnp.where(in_group == 3, bottom, 1.0))
    by_col = jnp.where(place_row < 4, left, jnp.where(place_row >= 4 * (CELLS + 1), right, 1.0))
    del3[8 : 8 + tall3, :] = (delta3 * (by_row * by_col)).astype(BF16).astype(F32)
    for ref in (del2, del3):
        ref[0:8, :] = jnp.zeros((8, GROUP), F32)
        ref[ref.shape[0] - 8 :, :] = jnp.zeros((8, GROUP), F32)

    def fold(grads, width, base, a, dst):
        total = None
        for n in range(GROUP // width):
            part = window(grads[n * width : (n + 1) * width, :], base + width * (n - 1), 3 * width)
            total = part if total is None else total + part
        for tap in range(3):
            start = (a * 3 + tap) * width
            tiled_store(dst, window(total, width * (2 - tap), width), slice(start, start + width))

    f1 = f1_ref[...]
    f1 = jnp.concatenate([f1[:, lanes(g)].astype(F32) for g in range(CELLS)], axis=0).astype(BF16)
    back = None
    for a in range(3):
        at = slice(5 - a, 13 - a)
        x1 = jnp.concatenate(
            [del1[0:CELLS, at, 256:GROUP], del1[1 : CELLS + 1, at, :], del1[2 : CELLS + 2, at, 0:128]], axis=2
        ).reshape(8 * CELLS, 640).astype(BF16)
        part = dot(x1, band1[a], 1, 1)
        back = part if back is None else back + part
        fold(dot(f1, x1, 0, 0), 48, 128, a, w48)
    for g in range(CELLS):
        g1_ref[:, lanes(g)] = back[8 * g : 8 * g + 8].astype(BF16)

    f2x = pad_f2[...].astype(BF16)
    back = None
    for a in range(3):
        at = 8 + 1 - a
        n = 8 * CELLS
        x2d = jnp.concatenate(
            [del2[at : at + n, 256:GROUP], del2[at + 8 : at + 8 + n, :], del2[at + 16 : at + 16 + n, 0:128]], axis=1
        ).astype(BF16)
        part = dot(x2d, band2[a], 1, 1)
        back = part if back is None else back + part
        fold(dot(f2x, x2d, 0, 0), 96, 128, a, w96)
    res2[...] = back
    for g in range(CELLS):
        g2_ref[:, lanes(g)] = res2[8 * g + 2 : 8 * g + 6, :].astype(BF16)

    f3x = pad_f3[...].astype(BF16)
    back = None
    for a in range(3):
        at = 8 + 1 - a
        n = 4 * CELLS
        x3d = jnp.concatenate(
            [del3[at : at + n, 128:GROUP], del3[at + 4 : at + 4 + n, :], del3[at + 8 : at + 8 + n, 0:256]], axis=1
        ).astype(BF16)
        part = dot(x3d, band3[a], 1, 1)
        back = part if back is None else back + part
        fold(dot(f3x, x3d, 0, 0), 192, 256, a, w192)
    res3[...] = back
    for g in range(CELLS):
        g3_ref[:, lanes(g)] = res3[4 * g + 1 : 4 * g + 3, :].astype(BF16)

    def fold_down(grads, width, rows, a, base, dst):
        for b in range(3):
            total = None
            for j in range(1 if b != 1 else 0, 2 * (GROUP // width), 2):
                p = (j + 1 - b) // 2
                part = window(grads[j * rows : (j + 1) * rows, :], width * p, width)
                total = part if total is None else total + part
            start = base + (a * 3 + b) * rows
            tiled_store(dst, total, slice(start, start + rows))

    def down_grads(saved, ext, skip, count, head, width, rows, base, dst):
        even = strided(saved, range(3), 0, count, 2).astype(BF16)
        odd = strided(saved, range(3), 1, count, 2).astype(BF16)
        for a in range(3):
            at = skip + (1 if a == 0 else 0)
            xs = jnp.concatenate(
                [ext[at : at + count, :], ext[at + skip : at + skip + count, 0:head]], axis=1
            ).astype(BF16)
            fold_down(dot(even if a == 1 else odd, xs, 0, 0), width, rows, a, base, dst)

    down_grads(pad_o1, ext2, 8, 8 * CELLS, 128, 96, 48, 864, w96)
    down_grads(pad_o2, ext3, 4, 4 * CELLS, 256, 192, 96, 1728, w192)

    def fold_mixer(grads, width, rows, base, dst):
        total = None
        for j in range(GROUP // rows):
            part = window(grads[j * rows : (j + 1) * rows, :], width * j, width)
            total = part if total is None else total + part
        tiled_store(dst, total, slice(base, base + rows))

    o2x = jnp.concatenate([pad_o2[tile] for tile in range(3)], axis=1).astype(BF16)
    o3x = pad_o3[...].astype(BF16)
    f4x = rows_f4[...].astype(BF16)
    inner2, inner3 = slice(8, 8 + 8 * CELLS), slice(4, 4 + 4 * CELLS)
    fold_mixer(dot(o2x, p12[inner2], 0, 0), 48, 96, 432, w48)
    fold_mixer(dot(o3x, p13[inner3], 0, 0), 48, 192, 528, w48)
    fold_mixer(dot(f4x, p14, 0, 0), 48, 384, 720, w48)
    fold_mixer(dot(o3x, p23[inner3], 0, 0), 96, 192, 1296, w96)
    fold_mixer(dot(f4x, p24, 0, 0), 96, 384, 1488, w96)
    fold_mixer(dot(f4x, p34, 0, 0), 192, 384, 2592, w192)
    back4 = (
        dot(p14[:, 0:48], m41_ref[...]) + dot(p24[:, 0:96], m42_ref[...]) + dot(p34[:, 0:192], m43_ref[...])
    )
    for g in range(CELLS):
        g4_ref[:, lanes(g)] = back4[g : g + 1].astype(BF16)

    for width, flat_base, src_base, count in PIECES:
        place({48: w48, 96: w96, 192: w192}[width], flat, width, flat_base, src_base, count)
    flat[6282:FLAT_ROWS, :] = jnp.zeros((FLAT_ROWS - 6282, 128), F32)
    pack_shares(flat, packed_ref)
    reduce_stages(packed_ref, share_ref, *reduce_refs)


def repeats(width, lanes, base=0):
    lane = np.arange(lanes)[None, :]
    return ((lane - base) % width == np.arange(width)[:, None]).astype(np.float32)


def pools(width, factors, parts):
    blocks = []
    for factor, lanes in zip(factors, parts):
        block = np.zeros((GROUP, lanes), np.float32)
        for lane in range(GROUP):
            block[lane, lane // (width * factor) * width + lane % width] = 1.0
        blocks.append(block)
    return np.concatenate(blocks, axis=1)


def local(f1, f2, f3, f4, o1, o2, o3, u1, u2, u3, k1, k2, k3, s12, s23, m21, m31, m41, m32, m42, m43):
    constants = [
        jnp.asarray(value, BF16)
        for value in (
            repeats(48, 640, 128), repeats(96, 640, 128), repeats(192, 896, 256), repeats(96, 512), repeats(192, 640),
            repeats(96, 384), repeats(192, 384),
            pools(48, (2, 4, 8), (256, 128, 128)), pools(96, (2, 4), (256, 128)), pools(192, (2,), (256,)),
        )
    ]
    whole = pl.BlockSpec(memory_space=pltpu.VMEM)
    inputs = [
        f1, f2, f3, f4, o1, o2, o3, u1, u2, u3,
        k1.reshape(432, 48), k2.reshape(864, 96), k3.reshape(1728, 192), s12.reshape(432, 96), s23.reshape(864, 192),
        m21.T, m31.T, m41.T, m32, m42.T, m43.T,
    ] + constants

    def f32(*shape):
        return pltpu.VMEM(shape, F32)

    def bf16(*shape):
        return pltpu.VMEM(shape, BF16)

    ext = CELLS + 2
    dma = pltpu.SemaphoreType.DMA
    packets = ((2, 16, CELLS * GROUP // 2), (2, 16, GROUP), (4, 16, GROUP))
    grad_one, grad_two, grad_three, grad_four, share = pl.pallas_call(
        backward_kernel,
        out_shape=[jax.ShapeDtypeStruct(value.shape, BF16) for value in (f1, f2, f3, f4)]
        + [jax.ShapeDtypeStruct((WINDOW, 128), F32)],
        in_specs=[whole] * len(inputs),
        out_specs=[whole] * 5,
        scratch_shapes=[
            bf16(128 * WINDOW, 128), *(bf16(*shape) for shape in packets + packets), dma((8,)), dma((8,)),
            f32(ext, 16, GROUP), f32(8 * ext + 8, GROUP), f32(4 * ext + 8, GROUP),
            f32(4, 16 * ext, 128), f32(3, 8 * ext, 128), f32(2, 4 * ext, 128),
            f32(ext, 16, GROUP), f32(8 * ext + 16, GROUP), f32(4 * ext + 16, GROUP),
            f32(8 * CELLS, GROUP), f32(4 * CELLS, GROUP), f32(3, 16 * CELLS, 128), f32(3, 8 * CELLS, 128),
            f32(4 * CELLS, GROUP), f32(CELLS, GROUP),
            bf16(3, GROUP, 640), bf16(3, GROUP, 640), bf16(3, GROUP, 896), bf16(3, GROUP, 512), bf16(3, GROUP, 640),
            bf16(192, GROUP), bf16(96, GROUP), bf16(GROUP, 256),
            f32(8 * CELLS, GROUP), f32(4 * CELLS, GROUP),
            f32(1, 1104, 128), f32(1, 1872, 128), f32(2, 2976, 128), f32(FLAT_ROWS, 128),
            pltpu.VMEM((64 * WINDOW, 128), jnp.bfloat16),
            pltpu.VMEM((64 * WINDOW, 128), jnp.bfloat16),
            pltpu.VMEM((15, 4 * WINDOW, 128), jnp.bfloat16),
            pltpu.VMEM((4 * WINDOW, 128), jnp.bfloat16),
            pltpu.VMEM((15, WINDOW, 128), jnp.bfloat16),
            pltpu.VMEM((WINDOW, 128), jnp.float32),
            pltpu.VMEM((8, 128), jnp.float32),
            pltpu.VMEM((7, 8, 128), jnp.float32),
            pltpu.VMEM((8, 128), jnp.float32),
            pltpu.VMEM((15, 8, 128), jnp.float32),
            dma((2,)),
            dma((15,)),
            dma((15,)),
            dma((4,)),
            dma((15,)),
            dma((3,)),
            dma((1,)),
            dma((7,)),
            dma((7,)),
            dma((15,)),
            dma((15,)),
        ],
        compiler_params=pltpu.CompilerParams(
            collective_id=0, has_side_effects=True, vmem_limit_bytes=48 * 1024 * 1024
        ),
        name="backward",
    )(*inputs)
    offset = (SHARE * lax.axis_index(("row", "col"))) % 1024
    weight_grads = lax.dynamic_slice(share.reshape(WINDOW * 128), (offset,), (SHARE,))
    return grad_one, grad_two, grad_three, grad_four, weight_grads


def solution(mesh):
    in_specs = (
        P(("branch", "row"), "col"),
        P(("branch", "row"), "col"),
        P(("branch", "row"), "col"),
        P(("branch", "row"), "col"),
        P(("branch", "row"), "col"),
        P(("branch", "row"), "col"),
        P(("branch", "row"), "col"),
        P(("branch", "row"), "col"),
        P(("branch", "row"), "col"),
        P(("branch", "row"), "col"),
        P(),
        P(),
        P(),
        P(),
        P(),
        P(),
        P(),
        P(),
        P(),
        P(),
        P(),
    )
    out_specs = (
        P(("branch", "row"), "col"),
        P(("branch", "row"), "col"),
        P(("branch", "row"), "col"),
        P(("branch", "row"), "col"),
        P(("row", "col")),
    )
    return jax.shard_map(local, mesh=mesh, in_specs=in_specs, out_specs=out_specs, check_vma=False)
```

time: 120 us -> 120 us (level); the launches traced: 120 us -> 118 us
  Pallas kernels: 104 us -> 87 us
  local copies, waits for them, and re-layouts: 14.5 us -> 29.9 us
    pallas_call x2 -> x0, Pallas kernels: 88.1 us -> none  [the longest x1 54.6 us: reduce_shares(): pl.pallas_call(reduce_kernel, out_shape=jax.ShapeDtypeStruct((WINDOW, 128...]
    pallas_call x1, Pallas kernels: 16.3 us -> 87 us  [local(): pl.pallas_call(backward_kernel, out_shape=[jax.ShapeDtypeStruct(value.sha...]
    unnamed x19 -> x66, local copies, waits for them, and re-layouts: 13.8 us -> 29.2 us
where the time goes in v3:
time: 120 us; the launch traced here: 118 us
  Pallas kernels  87 us (72%)
  local copies, waits for them, and re-layouts  29.9 us (25%)
    pallas_call x1, Pallas kernels, local(): pl.pallas_call(backward_kernel, out_shape=[jax.ShapeDtypeStruct(value.sha...  87 us
    unnamed x66, local copies, waits for them, and re-layouts  29.2 us

profile of v3, /device:TPU:1, one launch (start us, length us, event | category | flops | bytes accessed | tf_op | source)
XLA Modules:
  0.0 117.6 jit_solution(9177351107804830102)
XLA Ops:
  1.5 1.2 copy-done
  2.6 1.0 copy-done.1
  3.7 1.0 copy-done.2
  4.7 1.0 copy-done.3
  5.6 1.0 copy-done.4
  6.6 0.9 copy-done.5
  7.5 0.9 copy-done.6
  8.5 0.9 copy-done.7
  9.4 0.9 copy-done.8
  10.3 0.9 copy-done.9
  11.2 0.9 copy-done.10
  12.1 0.9 copy-done.11
  13.0 0.9 copy-done.12
  14.0 0.9 copy-done.13
  14.9 0.9 copy-done.14
  15.8 0.9 copy-done.15
  16.7 0.9 copy-done.16
  17.5 0.9 copy-done.17
  18.4 0.9 copy-done.18
  19.3 0.9 copy-done.19
  20.2 0.9 copy-done.20
  21.1 0.9 copy-done.21
  22.0 0.8 copy-done.23
  27.3 87.0 %backward.1 = (bf16[8,9216]{1,0:T(8,128)(2,1)S(1)}, bf16[4,9216]{1,0:T(4,128)(2,1)S(1)}, bf16[2,9216]{1,0:T(2,128)(2,1)S(1)}, bf16[1,9216]{1,0:T(2,128)(2,1)S(1)}, f32[64,128]{1,0:T(8,128)S(1)}) custom-call(bf16[8,9216]{1,0:T(8,128)(2,1)S(1)} %copy-done.8, bf16[4,9216]{1,0:T(4,128)(2,1)S(1)} %copy-done.17, bf16[2,9216]{1,0:T(2,128)(2,1)S(1)} %copy-done.24, ...), custom_call_target="tpu_custom_call" | custom-call | tf_op jit(solution)/shard_map/backward/pallas_call | solution.py:662
  (44 shorter events, 8.6 us)
Async XLA Ops:
  0.6 0.8 copy-start.22
  0.7 0.8 copy-start.30
  1.5 1.2 copy-start
  2.6 1.0 copy-start.1
  3.7 1.0 copy-start.2
  4.7 1.0 copy-start.3
  5.6 1.0 copy-start.4
  6.6 0.9 copy-start.5
  7.5 0.9 copy-start.6
  8.5 0.9 copy-start.7
  9.4 0.9 copy-start.8
  10.3 0.9 copy-start.9
  11.2 0.9 copy-start.10
  12.1 0.9 copy-start.11
  13.0 0.9 copy-start.12
  14.0 0.9 copy-start.13
  14.9 0.9 copy-start.14
  15.8 0.9 copy-start.15
  16.7 0.9 copy-start.16
  17.5 0.9 copy-start.17
  18.4 0.9 copy-start.18
  19.3 0.9 copy-start.19
  20.2 0.9 copy-start.20
  21.1 0.9 copy-start.21
  (7 other events, 5.4 us)

commit v4 on v3

--- a/solution.py
+++ b/solution.py
@@ -8,6 +8,8 @@
 
 EPSILON = 1e-06
 MESH = pl.DeviceIdType.MESH
+BF16 = jnp.bfloat16
+F32 = jnp.float32
 TOTAL = 804096
 SHARE = 6282
 WINDOW = 64
@@ -18,22 +20,110 @@
     row, col = divmod(share, 8)
     core, z_hi, y = row % 2, (row // 2) % 2, row // 4
     half, quarter = divmod(col, 4)
-    return ((core * 4 + y) * 4 + quarter) * 4 + z_hi * 2 + half
-
-
-def pack_shares(flat_ref, packed_ref):
-    for share in range(128):
+    return ((y * 2 + core) * 4 + quarter) * 4 + z_hi * 2 + half
+
+
+def pack_shares(flat_ref, packed_ref, block):
+    for share in range(32 * block, 32 * block + 32):
         start = SHARE * share // 1024 * 8
         place = share_place(share) * WINDOW
         packed_ref[place : place + WINDOW, :] = flat_ref[start : start + WINDOW, :].astype(jnp.bfloat16)
 
 
-def reduce_stages(
-    packed_ref,
+BLOCK = 16 * WINDOW
+PART = 4 * WINDOW
+
+
+class Reduction:
+    def __init__(self, packed, where, from_core, sum_core, from_x, sum_x, from_y, core_send, core_recv, x_send, x_recv, y_send, y_recv):
+        self.packed, self.where = packed, where
+        self.from_core, self.sum_core, self.from_x, self.sum_x, self.from_y = from_core, sum_core, from_x, sum_x, from_y
+        self.core_send, self.core_recv = core_send, core_recv
+        self.x_send, self.x_recv, self.y_send, self.y_recv = x_send, x_recv, y_send, y_recv
+
+    def core_copy(self, block):
+        x, row, col = self.where
+        core = row % 2
+        start = pl.multiple_of((block * 2 + 1 - core) * BLOCK, BLOCK)
+        return remote(
+            self.packed.at[pl.ds(start, BLOCK)], self.from_core.at[pl.ds(block * BLOCK, BLOCK)],
+            self.core_send.at[block], self.core_recv.at[block], (x, row + 1 - 2 * core, col),
+        )
+
+    def x_copy(self, block, step):
+        x, row, col = self.where
+        there = (x + step) % 4
+        start = pl.multiple_of(block * BLOCK + there * PART, PART)
+        slot = block * 3 + step - 1
+        return remote(
+            self.sum_core.at[pl.ds(start, PART)], self.from_x.at[slot], self.x_send.at[slot], self.x_recv.at[slot],
+            (there, row, col),
+        )
+
+    def y_copy(self, block):
+        x, row, col = self.where
+        y = row // 4
+        step = (block - y + 4) % 4
+        return remote(
+            self.sum_x.at[pl.ds(block * PART, PART)], self.from_y.at[step], self.y_send.at[step], self.y_recv.at[step],
+            (x, block * 4 + row % 4, col),
+        )
+
+    def leave(self, block):
+        self.core_copy(block).start()
+
+    def along_x(self, block):
+        core = self.where[1] % 2
+        self.core_copy(block).wait()
+
+        @pl.loop(0, 4)
+        def _(part):
+            mine = pl.multiple_of((block * 2 + core) * BLOCK + part * PART, PART)
+            place = pl.multiple_of(block * BLOCK + part * PART, PART)
+            total = self.packed[pl.ds(mine, PART), :].astype(F32) + self.from_core[pl.ds(place, PART), :].astype(F32)
+            self.sum_core[pl.ds(place, PART), :] = total.astype(BF16)
+
+        for step in range(1, 4):
+            self.x_copy(block, step).start()
+
+    def along_y(self, block):
+        x, row, col = self.where
+        for step in range(1, 4):
+            self.x_copy(block, step).wait()
+        own = pl.multiple_of(block * BLOCK + x * PART, PART)
+        total = self.sum_core[pl.ds(own, PART), :].astype(F32)
+        for step in range(3):
+            total = total + self.from_x[block * 3 + step].astype(F32)
+        self.sum_x[block * PART : (block + 1) * PART, :] = total.astype(BF16)
+
+        @pl.when(row // 4 != block)
+        def _():
+            self.y_copy(block).start()
+
+    def plane_sum(self, sum_plane):
+        y = self.where[1] // 4
+        for step in range(1, 4):
+            remote(
+                self.sum_x.at[pl.ds(0, PART)], self.from_y.at[step], self.y_send.at[step], self.y_recv.at[step], self.where
+            ).wait_recv()
+        total = self.sum_x[pl.ds(pl.multiple_of(y * PART, PART), PART), :].astype(F32)
+        for step in range(1, 4):
+            total = total + self.from_y[step].astype(F32)
+        sum_plane[...] = total.astype(BF16)
+        for step in range(1, 4):
+            remote(
+                self.sum_x.at[pl.ds(0, PART)], self.from_y.at[step], self.y_send.at[step], self.y_recv.at[step], self.where
+            ).wait_send()
+
+
+def remote(src, dst, send_sem, recv_sem, peer):
+    return pltpu.make_async_remote_copy(
+        src_ref=src, dst_ref=dst, send_sem=send_sem, recv_sem=recv_sem, device_id=peer, device_id_type=MESH
+    )
+
+
+def finish_shares(
     out_ref,
-    from_core,
-    sum_core,
-    from_plane,
     sum_plane,
     from_line,
     share_buf,
@@ -41,9 +131,6 @@
     from_near,
     near_buf,
     from_far,
-    core_sems,
-    plane_send,
-    plane_recv,
     line_send,
     line_recv,
     share_send,
@@ -60,10 +147,6 @@
     z = z_hi * 8 + col
     partner = (x, row + 1 - 2 * core, col)
 
-    def plane_peer(step):
-        there = (x * 4 + y + step) % 16
-        return there, (there // 4, (there % 4) * 4 + z_hi * 2 + core, col)
-
     def line_peer(step):
         there = (z + step) % 16
         return (x, y * 4 + (there // 8) * 2 + core, there % 8)
@@ -71,52 +154,6 @@
     def near_peer(step):
         there = (y * 2 + core + step) % 8
         return (x, (there // 2) * 4 + z_hi * 2 + there % 2, col)
-
-    def remote(src, dst, send_sem, recv_sem, peer):
-        return pltpu.make_async_remote_copy(
-            src_ref=src, dst_ref=dst, send_sem=send_sem, recv_sem=recv_sem,
-            device_id=peer, device_id_type=MESH,
-        )
-
-    half = 64 * WINDOW
-    across = remote(
-        packed_ref.at[pl.ds(pl.multiple_of((1 - core) * half, half), half)],
-        from_core, core_sems.at[0], core_sems.at[1], partner,
-    )
-    across.start()
-    across.wait()
-
-    @pl.loop(0, 16)
-    def _(block):
-        start = pl.multiple_of(block * 256, 256)
-        mine = packed_ref[pl.ds(pl.multiple_of(core * half, half) + start, 256), :]
-        theirs = from_core[pl.ds(start, 256), :]
-        sum_core[pl.ds(start, 256), :] = (mine.astype(jnp.float32) + theirs.astype(jnp.float32)).astype(jnp.bfloat16)
-
-    def plane_copy(step):
-        there, peer = plane_peer(step)
-        place = (there % 4) * 4 + there // 4
-        return remote(
-            sum_core.at[pl.ds(pl.multiple_of(place * 256, 256), 256)],
-            from_plane.at[step - 1], plane_send.at[step - 1], plane_recv.at[step - 1], peer,
-        )
-
-    @pl.loop(1, 16)
-    def _(step):
-        plane_copy(step).start()
-
-    @pl.loop(1, 16)
-    def _(step):
-        plane_copy(step).wait()
-
-    @pl.loop(0, 4)
-    def _(block):
-        start = pl.multiple_of(block * WINDOW, WINDOW)
-        own = pl.multiple_of((y * 4 + x) * 256 + start, WINDOW)
-        total = sum_core[pl.ds(own, WINDOW), :].astype(jnp.float32)
-        for step in range(15):
-            total = total + from_plane[step, pl.ds(start, WINDOW), :].astype(jnp.float32)
-        sum_plane[pl.ds(start, WINDOW), :] = total.astype(jnp.bfloat16)
 
     def line_copy(block):
         target = (block // 2) * 8 + (block % 2) * 4 + x
@@ -223,8 +260,6 @@
     (48, 5022, 432, 96), (48, 5058, 528, 192), (48, 5130, 720, 384), (96, 5274, 1296, 192),
     (96, 5418, 1488, 384), (192, 5706, 2592, 384),
 )
-BF16 = jnp.bfloat16
-F32 = jnp.float32
 
 
 def dot(left, right, left_dim=1, right_dim=0):
@@ -263,17 +298,17 @@
         dst[block * rows : (block + 1) * rows, :] = value.astype(BF16)
 
 
-def conv_blocks(tap_row, width, base):
-    return [[(tap_row * 3 + tap, base + width * (n + 1 - tap)) for tap in range(3)] for n in range(GROUP // width)]
-
-
-def down_blocks(tap_row, width):
+def conv_blocks(width, base):
+    return [[(tap, base + width * (n + 1 - tap)) for tap in range(3)] for n in range(GROUP // width)]
+
+
+def down_blocks(width):
     blocks = []
     for j in range(2 * (GROUP // width)):
         if j % 2 == 0:
-            blocks.append([(tap_row * 3 + 1, width * (j // 2))])
+            blocks.append([(1, width * (j // 2))])
         else:
-            blocks.append([(tap_row * 3 + 2, width * (j // 2)), (tap_row * 3, width * (j // 2 + 1))])
+            blocks.append([(2, width * (j // 2)), (0, width * (j // 2 + 1))])
     return blocks
 
 
@@ -349,10 +384,6 @@
         (7, -1, -1, send_corners.at[3], recv_corners.at[3]),
     )
 
-    def plane_peer(step):
-        there = (x * 4 + y + step) % 16
-        return there, (there // 4, (there % 4) * 4 + z_hi * 2 + core, col)
-
     def line_peer(step):
         there = (z + step) % 16
         return (x, y * 4 + (there // 8) * 2 + core, there % 8)
@@ -367,11 +398,11 @@
     barrier = pltpu.get_barrier_semaphore()
     for route in routes:
         greet(peer(route[1], route[2]))
-    greet((x, row + 1 - 2 * core, col))
+    for step in range(1, 4):
+        greet(((x + step) % 4, row, col))
 
     @pl.loop(1, 16)
     def _(step):
-        greet(plane_peer(step)[1])
         greet(line_peer(step))
 
     @pl.loop(1, 8)
@@ -380,7 +411,7 @@
 
     u1, u2, u3 = (ref[...].astype(F32) for ref in (u1_ref, u2_ref, u3_ref))
     fill_packets(u1, u2, u3, send_rows, send_sides, send_corners)
-    pl.semaphore_wait(barrier, 46)
+    pl.semaphore_wait(barrier, 33)
 
     def halo_copy(route):
         slot, down, right, src, dst = route
@@ -391,6 +422,14 @@
 
     for route in routes:
         halo_copy(route).start()
+
+    for ref in (ext1, ext2, ext3):
+        ref[...] = jnp.zeros_like(ref)
+    for g in range(CELLS):
+        at = lanes(g)
+        ext1[g + 1, 4:12, :] = u1[:, at]
+        ext2[8 * g + 10 : 8 * g + 14, :] = u2[:, at]
+        ext3[4 * g + 5 : 4 * g + 7, :] = u3[:, at]
 
     for ref in (pad_f2, pad_f3, pad_o1, pad_o2, pad_o3):
         ref[...] = jnp.zeros_like(ref)
@@ -407,48 +446,14 @@
         rows_f4[g : g + 1, :] = f4[:, at]
 
     for a in range(3):
-        banded(k1_ref[...], rep1_ref[...], 48, 48, conv_blocks(a, 48, 128), band1.at[a])
-        banded(k2_ref[...], rep2_ref[...], 96, 96, conv_blocks(a, 96, 128), band2.at[a])
-        banded(k3_ref[...], rep3_ref[...], 192, 192, conv_blocks(a, 192, 256), band3.at[a])
-        banded(s12_ref[...], rep12_ref[...], 96, 48, down_blocks(a, 96), band12.at[a])
-        banded(s23_ref[...], rep23_ref[...], 192, 96, down_blocks(a, 192), band23.at[a])
+        banded(k1_ref[144 * a : 144 * a + 144, :], rep1_ref[...], 48, 48, conv_blocks(48, 128), band1.at[a])
+        banded(k2_ref[288 * a : 288 * a + 288, :], rep2_ref[...], 96, 96, conv_blocks(96, 128), band2.at[a])
+        banded(k3_ref[576 * a : 576 * a + 576, :], rep3_ref[...], 192, 192, conv_blocks(192, 256), band3.at[a])
+        banded(s12_ref[144 * a : 144 * a + 144, :], rep12_ref[...], 96, 48, down_blocks(96), band12.at[a])
+        banded(s23_ref[288 * a : 288 * a + 288, :], rep23_ref[...], 192, 96, down_blocks(192), band23.at[a])
     banded(m21_ref[...], rep96_ref[...], 96, 48, mixer_blocks(96, 4), band21)
     banded(m31_ref[...], rep192_ref[...], 192, 48, mixer_blocks(192, 2), band31)
     banded(m32_ref[...], rep96_ref[:, :256], 96, 192, mixer_blocks(96, 2), band32)
-
-    for route in routes:
-        halo_copy(route).wait()
-    top, bottom = jnp.where(line > 0, 1.0, 0.0), jnp.where(line < 63, 1.0, 0.0)
-    left, right = jnp.where(col > 0, 1.0, 0.0), jnp.where(col < 7, 1.0, 0.0)
-    above, below = recv_rows[0].astype(F32) * top, recv_rows[1].astype(F32) * bottom
-    sides = [recv_sides[0].astype(F32) * left, recv_sides[1].astype(F32) * right]
-    corners = [
-        recv_corners[0].astype(F32) * (top * left), recv_corners[1].astype(F32) * (top * right),
-        recv_corners[2].astype(F32) * (bottom * left), recv_corners[3].astype(F32) * (bottom * right),
-    ]
-    for g in range(CELLS + 2):
-        if g == 0 or g == CELLS + 1:
-            side = sides[0 if g == 0 else 1]
-            mid = side[0:8], side[8:12], side[12:14]
-            up = corners[0 if g == 0 else 1]
-            down = corners[2 if g == 0 else 3]
-        else:
-            at = lanes(g - 1)
-            mid = u1[:, at], u2[:, at], u3[:, at]
-            row0 = 8 * ((g - 1) // half)
-            there = lanes((g - 1) % half)
-            up, down = above[row0 : row0 + 8, there], below[row0 : row0 + 8, there]
-        ext1[g, 0:4, :] = up[0:4]
-        ext1[g, 4:12, :] = mid[0]
-        ext1[g, 12:16, :] = down[4:8]
-        ext2[8 * g : 8 * g + 2, :] = up[4:6]
-        ext2[8 * g + 2 : 8 * g + 6, :] = mid[1]
-        ext2[8 * g + 6 : 8 * g + 8, :] = down[0:2]
-        ext3[4 * g : 4 * g + 1, :] = up[6:7]
-        ext3[4 * g + 1 : 4 * g + 3, :] = mid[2]
-        ext3[4 * g + 3 : 4 * g + 4, :] = down[2:3]
-    ext2[8 * (CELLS + 2) :, :] = jnp.zeros((8, GROUP), F32)
-    ext3[4 * (CELLS + 2) :, :] = jnp.zeros((8, GROUP), F32)
 
     tall1, tall2, tall3 = 16 * (CELLS + 2), 8 * (CELLS + 2), 4 * (CELLS + 2)
     def tiled_store(ref, value, rows=slice(None)):
@@ -458,10 +463,6 @@
     def strided(ref, tiles, start, count, stride):
         parts = [ref[tile, pl.ds(start, count, stride=stride), :] for tile in tiles]
         return parts[0] if len(parts) == 1 else jnp.concatenate(parts, axis=1)
-
-    tiled_store(v1, dot(ext1[...].reshape(tall1, GROUP).astype(BF16), pool1_ref[...]))
-    tiled_store(v2, dot(ext2[0:tall2, :].astype(BF16), pool2_ref[...]))
-    tiled_store(v3, dot(ext3[0:tall3, :].astype(BF16), pool3_ref[...]))
 
     def strided_sum(ref, picks, count, stride, tiles):
         total = None
@@ -470,124 +471,16 @@
             total = piece if total is None else total + piece
         return total.astype(BF16)
 
+    tiled_store(v1, dot(ext1[...].reshape(tall1, GROUP).astype(BF16), pool1_ref[...]))
+    tiled_store(v2, dot(ext2[0:tall2, :].astype(BF16), pool2_ref[...]))
+    tiled_store(v3, dot(ext3[0:tall3, :].astype(BF16), pool3_ref[...]))
+
     p12 = strided_sum(v1, range(2), tall2, 2, (0, 1))
     p13 = strided_sum(v1, range(4), tall3, 4, (2,))
     p14 = strided_sum(v1, range(16 + 4, 16 + 12), CELLS, 16, (3,))
     p23 = strided_sum(v2, range(2), tall3, 2, (0, 1))
     p24 = strided_sum(v2, range(8 + 2, 8 + 6), CELLS, 8, (2,))
     p34 = strided_sum(v3, range(4 + 1, 4 + 3), CELLS, 4, (0, 1))
-
-    def rim_mask(rows, inner):
-        place_row = lax.broadcasted_iota(jnp.int32, (CELLS + 2, rows, GROUP), 1)
-        place_col = lax.broadcasted_iota(jnp.int32, (CELLS + 2, rows, GROUP), 0)
-        start, end = (rows - inner) // 2, (rows + inner) // 2
-        by_row = jnp.where(place_row == start - 1, top, jnp.where(place_row == end, bottom, 1.0))
-        by_row = jnp.where(jnp.logical_and(place_row >= start - 1, place_row <= end), by_row, 0.0)
-        by_col = jnp.where(place_col == 0, left, jnp.where(place_col == CELLS + 1, right, 1.0))
-        return by_row * by_col
-
-    def rolled(value):
-        return pltpu.roll(value, value.shape[0] - 1, 0)
-
-    x2 = jnp.concatenate([ext2[0:tall2, :], ext2[8 : tall2 + 8, 0:128]], axis=1).astype(BF16)
-    tiled_store(v1, dot(x2, band12[1], 1, 1), pl.ds(0, tall2, stride=2))
-    tiled_store(v1, dot(x2, band12[2], 1, 1) + rolled(dot(x2, band12[0], 1, 1)), pl.ds(1, tall2, stride=2))
-    spread1 = jnp.concatenate([v1[tile] for tile in range(3)], axis=1)
-    delta1 = ext1[...] + spread1.reshape(CELLS + 2, 16, GROUP)
-    del1[...] = (delta1 * rim_mask(16, 8)).astype(BF16).astype(F32)
-
-    x3 = jnp.concatenate([ext3[0:tall3, :], ext3[4 : tall3 + 4, 0:256]], axis=1).astype(BF16)
-    tiled_store(v2, dot(x3, band23[1], 1, 1), pl.ds(0, tall3, stride=2))
-    tiled_store(v2, dot(x3, band23[2], 1, 1) + rolled(dot(x3, band23[0], 1, 1)), pl.ds(1, tall3, stride=2))
-    spread2 = jnp.concatenate([v2[tile] for tile in range(3)], axis=1)
-    delta2 = ext2[0:tall2, :] + dot(p12[:, 0:192], band21[...]) + spread2
-    del2[8 : 8 + tall2, :] = (delta2 * rim_mask(8, 4).reshape(tall2, GROUP)).astype(BF16).astype(F32)
-
-    delta3 = ext3[0:tall3, :] + dot(p13[:, 0:96], band31[...]) + dot(p23, band32[...], 1, 1)
-    place_row = lax.broadcasted_iota(jnp.int32, (tall3, GROUP), 0)
-    in_group = jnp.bitwise_and(place_row, 3)
-    by_row = jnp.where(in_group == 0, top, jnp.where(in_group == 3, bottom, 1.0))
-    by_col = jnp.where(place_row < 4, left, jnp.where(place_row >= 4 * (CELLS + 1), right, 1.0))
-    del3[8 : 8 + tall3, :] = (delta3 * (by_row * by_col)).astype(BF16).astype(F32)
-    for ref in (del2, del3):
-        ref[0:8, :] = jnp.zeros((8, GROUP), F32)
-        ref[ref.shape[0] - 8 :, :] = jnp.zeros((8, GROUP), F32)
-
-    def fold(grads, width, base, a, dst):
-        total = None
-        for n in range(GROUP // width):
-            part = window(grads[n * width : (n + 1) * width, :], base + width * (n - 1), 3 * width)
-            total = part if total is None else total + part
-        for tap in range(3):
-            start = (a * 3 + tap) * width
-            tiled_store(dst, window(total, width * (2 - tap), width), slice(start, start + width))
-
-    f1 = f1_ref[...]
-    f1 = jnp.concatenate([f1[:, lanes(g)].astype(F32) for g in range(CELLS)], axis=0).astype(BF16)
-    back = None
-    for a in range(3):
-        at = slice(5 - a, 13 - a)
-        x1 = jnp.concatenate(
-            [del1[0:CELLS, at, 256:GROUP], del1[1 : CELLS + 1, at, :], del1[2 : CELLS + 2, at, 0:128]], axis=2
-        ).reshape(8 * CELLS, 640).astype(BF16)
-        part = dot(x1, band1[a], 1, 1)
-        back = part if back is None else back + part
-        fold(dot(f1, x1, 0, 0), 48, 128, a, w48)
-    for g in range(CELLS):
-        g1_ref[:, lanes(g)] = back[8 * g : 8 * g + 8].astype(BF16)
-
-    f2x = pad_f2[...].astype(BF16)
-    back = None
-    for a in range(3):
-        at = 8 + 1 - a
-        n = 8 * CELLS
-        x2d = jnp.concatenate(
-            [del2[at : at + n, 256:GROUP], del2[at + 8 : at + 8 + n, :], del2[at + 16 : at + 16 + n, 0:128]], axis=1
-        ).astype(BF16)
-        part = dot(x2d, band2[a], 1, 1)
-        back = part if back is None else back + part
-        fold(dot(f2x, x2d, 0, 0), 96, 128, a, w96)
-    res2[...] = back
-    for g in range(CELLS):
-        g2_ref[:, lanes(g)] = res2[8 * g + 2 : 8 * g + 6, :].astype(BF16)
-
-    f3x = pad_f3[...].astype(BF16)
-    back = None
-    for a in range(3):
-        at = 8 + 1 - a
-        n = 4 * CELLS
-        x3d = jnp.concatenate(
-            [del3[at : at + n, 128:GROUP], del3[at + 4 : at + 4 + n, :], del3[at + 8 : at + 8 + n, 0:256]], axis=1
-        ).astype(BF16)
-        part = dot(x3d, band3[a], 1, 1)
-        back = part if back is None else back + part
-        fold(dot(f3x, x3d, 0, 0), 192, 256, a, w192)
-    res3[...] = back
-    for g in range(CELLS):
-        g3_ref[:, lanes(g)] = res3[4 * g + 1 : 4 * g + 3, :].astype(BF16)
-
-    def fold_down(grads, width, rows, a, base, dst):
-        for b in range(3):
-            total = None
-            for j in range(1 if b != 1 else 0, 2 * (GROUP // width), 2):
-                p = (j + 1 - b) // 2
-                part = window(grads[j * rows : (j + 1) * rows, :], width * p, width)
-                total = part if total is None else total + part
-            start = base + (a * 3 + b) * rows
-            tiled_store(dst, total, slice(start, start + rows))
-
-    def down_grads(saved, ext, skip, count, head, width, rows, base, dst):
-        even = strided(saved, range(3), 0, count, 2).astype(BF16)
-        odd = strided(saved, range(3), 1, count, 2).astype(BF16)
-        for a in range(3):
-            at = skip + (1 if a == 0 else 0)
-            xs = jnp.concatenate(
-                [ext[at : at + count, :], ext[at + skip : at + skip + count, 0:head]], axis=1
-            ).astype(BF16)
-            fold_down(dot(even if a == 1 else odd, xs, 0, 0), width, rows, a, base, dst)
-
-    down_grads(pad_o1, ext2, 8, 8 * CELLS, 128, 96, 48, 864, w96)
-    down_grads(pad_o2, ext3, 4, 4 * CELLS, 256, 192, 96, 1728, w192)
 
     def fold_mixer(grads, width, rows, base, dst):
         total = None
@@ -612,11 +505,180 @@
     for g in range(CELLS):
         g4_ref[:, lanes(g)] = back4[g : g + 1].astype(BF16)
 
-    for width, flat_base, src_base, count in PIECES:
-        place({48: w48, 96: w96, 192: w192}[width], flat, width, flat_base, src_base, count)
+    for route in routes:
+        halo_copy(route).wait()
+    top, bottom = jnp.where(line > 0, 1.0, 0.0), jnp.where(line < 63, 1.0, 0.0)
+    left, right = jnp.where(col > 0, 1.0, 0.0), jnp.where(col < 7, 1.0, 0.0)
+    above, below = recv_rows[0].astype(F32) * top, recv_rows[1].astype(F32) * bottom
+    sides = [recv_sides[0].astype(F32) * left, recv_sides[1].astype(F32) * right]
+    corners = [
+        recv_corners[0].astype(F32) * (top * left), recv_corners[1].astype(F32) * (top * right),
+        recv_corners[2].astype(F32) * (bottom * left), recv_corners[3].astype(F32) * (bottom * right),
+    ]
+    for g in range(CELLS + 2):
+        if g == 0 or g == CELLS + 1:
+            side = sides[0 if g == 0 else 1]
+            ext1[g, 4:12, :] = side[0:8]
+            ext2[8 * g + 2 : 8 * g + 6, :] = side[8:12]
+            ext3[4 * g + 1 : 4 * g + 3, :] = side[12:14]
+            up = corners[0 if g == 0 else 1]
+            down = corners[2 if g == 0 else 3]
+        else:
+            row0 = 8 * ((g - 1) // half)
+            there = lanes((g - 1) % half)
+            up, down = above[row0 : row0 + 8, there], below[row0 : row0 + 8, there]
+        ext1[g, 0:4, :] = up[0:4]
+        ext1[g, 12:16, :] = down[4:8]
+        ext2[8 * g : 8 * g + 2, :] = up[4:6]
+        ext2[8 * g + 6 : 8 * g + 8, :] = down[0:2]
+        ext3[4 * g : 4 * g + 1, :] = up[6:7]
+        ext3[4 * g + 3 : 4 * g + 4, :] = down[2:3]
+
+
+    tiled_store(v1, dot(ext1[...].reshape(tall1, GROUP).astype(BF16), pool1_ref[...]))
+    tiled_store(v2, dot(ext2[0:tall2, :].astype(BF16), pool2_ref[...]))
+    p12 = strided_sum(v1, range(2), tall2, 2, (0, 1))
+    p13 = strided_sum(v1, range(4), tall3, 4, (2,))
+    p23 = strided_sum(v2, range(2), tall3, 2, (0, 1))
+
+    def fold_down(grads, width, rows, a, base, dst):
+        for b in range(3):
+            total = None
+            for j in range(1 if b != 1 else 0, 2 * (GROUP // width), 2):
+                p = (j + 1 - b) // 2
+                part = window(grads[j * rows : (j + 1) * rows, :], width * p, width)
+                total = part if total is None else total + part
+            start = base + (a * 3 + b) * rows
+            tiled_store(dst, total, slice(start, start + rows))
+
+    def down_grads(saved, ext, skip, count, head, width, rows, base, dst):
+        even = strided(saved, range(3), 0, count, 2).astype(BF16)
+        odd = strided(saved, range(3), 1, count, 2).astype(BF16)
+        for a in range(3):
+            at = skip + (1 if a == 0 else 0)
+            xs = jnp.concatenate(
+                [ext[at : at + count, :], ext[at + skip : at + skip + count, 0:head]], axis=1
+            ).astype(BF16)
+            fold_down(dot(even if a == 1 else odd, xs, 0, 0), width, rows, a, base, dst)
+
+    down_grads(pad_o1, ext2, 8, 8 * CELLS, 128, 96, 48, 864, w96)
+    down_grads(pad_o2, ext3, 4, 4 * CELLS, 256, 192, 96, 1728, w192)
+
+    reduction = Reduction(packed_ref, (x, row, col), *reduce_refs[:11])
     flat[6282:FLAT_ROWS, :] = jnp.zeros((FLAT_ROWS - 6282, 128), F32)
-    pack_shares(flat, packed_ref)
-    reduce_stages(packed_ref, share_ref, *reduce_refs)
+
+    def settle(pieces, blocks):
+        for piece in pieces:
+            width, flat_base, src_base, count = PIECES[piece]
+            place({48: w48, 96: w96, 192: w192}[width], flat, width, flat_base, src_base, count)
+        for block in blocks:
+            pack_shares(flat, packed_ref, block)
+            reduction.leave(block)
+
+    settle((3, 4, 5, 6, 7, 8, 9, 10), (3,))
+
+    def rim_mask(rows, inner):
+        place_row = lax.broadcasted_iota(jnp.int32, (CELLS + 2, rows, GROUP), 1)
+        place_col = lax.broadcasted_iota(jnp.int32, (CELLS + 2, rows, GROUP), 0)
+        start, end = (rows - inner) // 2, (rows + inner) // 2
+        by_row = jnp.where(place_row == start - 1, top, jnp.where(place_row == end, bottom, 1.0))
+        by_row = jnp.where(jnp.logical_and(place_row >= start - 1, place_row <= end), by_row, 0.0)
+        by_col = jnp.where(place_col == 0, left, jnp.where(place_col == CELLS + 1, right, 1.0))
+        return by_row * by_col
+
+    def rolled(value):
+        return pltpu.roll(value, value.shape[0] - 1, 0)
+
+    x2 = jnp.concatenate([ext2[0:tall2, :], ext2[8 : tall2 + 8, 0:128]], axis=1).astype(BF16)
+    tiled_store(v1, dot(x2, band12[1], 1, 1), pl.ds(0, tall2, stride=2))
+    tiled_store(v1, dot(x2, band12[2], 1, 1) + rolled(dot(x2, band12[0], 1, 1)), pl.ds(1, tall2, stride=2))
+    spread1 = jnp.concatenate([v1[tile] for tile in range(3)], axis=1)
+    delta1 = ext1[...] + spread1.reshape(CELLS + 2, 16, GROUP)
+    del1[...] = (delta1 * rim_mask(16, 8)).astype(BF16).astype(F32)
+
+    x3 = jnp.concatenate([ext3[0:tall3, :], ext3[4 : tall3 + 4, 0:256]], axis=1).astype(BF16)
+    tiled_store(v2, dot(x3, band23[1], 1, 1), pl.ds(0, tall3, stride=2))
+    tiled_store(v2, dot(x3, band23[2], 1, 1) + rolled(dot(x3, band23[0], 1, 1)), pl.ds(1, tall3, stride=2))
+    spread2 = jnp.concatenate([v2[tile] for tile in range(3)], axis=1)
+    delta2 = ext2[0:tall2, :] + dot(p12[:, 0:192], band21[...]) + spread2
+    del2[8 : 8 + tall2, :] = (delta2 * rim_mask(8, 4).reshape(tall2, GROUP)).astype(BF16).astype(F32)
+
+    delta3 = ext3[0:tall3, :] + dot(p13[:, 0:96], band31[...]) + dot(p23, band32[...], 1, 1)
+    place_row = lax.broadcasted_iota(jnp.int32, (tall3, GROUP), 0)
+    in_group = jnp.bitwise_and(place_row, 3)
+    by_row = jnp.where(in_group == 0, top, jnp.where(in_group == 3, bottom, 1.0))
+    by_col = jnp.where(place_row < 4, left, jnp.where(place_row >= 4 * (CELLS + 1), right, 1.0))
+    del3[8 : 8 + tall3, :] = (delta3 * (by_row * by_col)).astype(BF16).astype(F32)
+    for ref in (del2, del3):
+        ref[0:8, :] = jnp.zeros((8, GROUP), F32)
+        ref[ref.shape[0] - 8 :, :] = jnp.zeros((8, GROUP), F32)
+
+    reduction.along_x(3)
+
+    def fold(grads, width, base, a, dst):
+        total = None
+        for n in range(GROUP // width):
+            part = window(grads[n * width : (n + 1) * width, :], base + width * (n - 1), 3 * width)
+            total = part if total is None else total + part
+        for tap in range(3):
+            start = (a * 3 + tap) * width
+            tiled_store(dst, window(total, width * (2 - tap), width), slice(start, start + width))
+
+    f3x = pad_f3[...].astype(BF16)
+    back = None
+    for a in range(3):
+        at = 8 + 1 - a
+        n = 4 * CELLS
+        x3d = jnp.concatenate(
+            [del3[at : at + n, 128:GROUP], del3[at + 4 : at + 4 + n, :], del3[at + 8 : at + 8 + n, 0:256]], axis=1
+        ).astype(BF16)
+        part = dot(x3d, band3[a], 1, 1)
+        back = part if back is None else back + part
+        fold(dot(f3x, x3d, 0, 0), 192, 256, a, w192)
+    res3[...] = back
+    for g in range(CELLS):
+        g3_ref[:, lanes(g)] = res3[4 * g + 1 : 4 * g + 3, :].astype(BF16)
+
+    settle((2,), (2, 1))
+
+    f2x = pad_f2[...].astype(BF16)
+    back = None
+    for a in range(3):
+        at = 8 + 1 - a
+        n = 8 * CELLS
+        x2d = jnp.concatenate(
+            [del2[at : at + n, 256:GROUP], del2[at + 8 : at + 8 + n, :], del2[at + 16 : at + 16 + n, 0:128]], axis=1
+        ).astype(BF16)
+        part = dot(x2d, band2[a], 1, 1)
+        back = part if back is None else back + part
+        fold(dot(f2x, x2d, 0, 0), 96, 128, a, w96)
+    res2[...] = back
+    for g in range(CELLS):
+        g2_ref[:, lanes(g)] = res2[8 * g + 2 : 8 * g + 6, :].astype(BF16)
+
+    reduction.along_x(2)
+    reduction.along_x(1)
+
+    f1 = f1_ref[...]
+    f1 = jnp.concatenate([f1[:, lanes(g)].astype(F32) for g in range(CELLS)], axis=0).astype(BF16)
+    back = None
+    for a in range(3):
+        at = slice(5 - a, 13 - a)
+        x1 = jnp.concatenate(
+            [del1[0:CELLS, at, 256:GROUP], del1[1 : CELLS + 1, at, :], del1[2 : CELLS + 2, at, 0:128]], axis=2
+        ).reshape(8 * CELLS, 640).astype(BF16)
+        part = dot(x1, band1[a], 1, 1)
+        back = part if back is None else back + part
+        fold(dot(f1, x1, 0, 0), 48, 128, a, w48)
+    for g in range(CELLS):
+        g1_ref[:, lanes(g)] = back[8 * g : 8 * g + 8].astype(BF16)
+
+    settle((0, 1), (0,))
+    reduction.along_x(0)
+    for block in (3, 2, 1, 0):
+        reduction.along_y(block)
+    reduction.plane_sum(reduce_refs[11])
+    finish_shares(share_ref, *reduce_refs[11:])
 
 
 def repeats(width, lanes, base=0):
@@ -676,30 +738,13 @@
             bf16(192, GROUP), bf16(96, GROUP), bf16(GROUP, 256),
             f32(8 * CELLS, GROUP), f32(4 * CELLS, GROUP),
             f32(1, 1104, 128), f32(1, 1872, 128), f32(2, 2976, 128), f32(FLAT_ROWS, 128),
-            pltpu.VMEM((64 * WINDOW, 128), jnp.bfloat16),
-            pltpu.VMEM((64 * WINDOW, 128), jnp.bfloat16),
-            pltpu.VMEM((15, 4 * WINDOW, 128), jnp.bfloat16),
-            pltpu.VMEM((4 * WINDOW, 128), jnp.bfloat16),
-            pltpu.VMEM((15, WINDOW, 128), jnp.bfloat16),
-            pltpu.VMEM((WINDOW, 128), jnp.float32),
-            pltpu.VMEM((8, 128), jnp.float32),
-            pltpu.VMEM((7, 8, 128), jnp.float32),
-            pltpu.VMEM((8, 128), jnp.float32),
-            pltpu.VMEM((15, 8, 128), jnp.float32),
-            dma((2,)),
-            dma((15,)),
-            dma((15,)),
-            dma((4,)),
-            dma((15,)),
-            dma((3,)),
-            dma((1,)),
-            dma((7,)),
-            dma((7,)),
-            dma((15,)),
-            dma((15,)),
+            bf16(4 * BLOCK, 128), bf16(4 * BLOCK, 128), bf16(12, PART, 128), bf16(4 * PART, 128), bf16(4, PART, 128),
+            dma((4,)), dma((4,)), dma((12,)), dma((12,)), dma((4,)), dma((4,)),
+            bf16(PART, 128), bf16(15, WINDOW, 128), f32(WINDOW, 128), f32(8, 128), f32(7, 8, 128), f32(8, 128), f32(15, 8, 128),
+            dma((4,)), dma((15,)), dma((3,)), dma((1,)), dma((7,)), dma((7,)), dma((15,)), dma((15,)),
         ],
         compiler_params=pltpu.CompilerParams(
-            collective_id=0, has_side_effects=True, vmem_limit_bytes=48 * 1024 * 1024
+            collective_id=0, has_side_effects=True, vmem_limit_bytes=56 * 1024 * 1024
         ),
         name="backward",
     )(*inputs)

time: 120 us -> 90 us (0.75)
  local copies, waits for them, and re-layouts: 29.9 us -> 5.23 us
  Pallas kernels: 87 us -> 82.6 us
    unnamed x66 -> x10, local copies, waits for them, and re-layouts: 29.2 us -> 3.78 us
    pallas_call x1, Pallas kernels: 87 us -> 82.6 us  [local(): pl.pallas_call(backward_kernel, out_shape=[jax.ShapeDtypeStruct(value.sha...]
where the time goes in v4:
time: 90 us; the launch traced here: 88.5 us
  Pallas kernels  82.6 us (92%)
  local copies, waits for them, and re-layouts  5.23 us (6%)
    pallas_call x1, Pallas kernels, local(): pl.pallas_call(backward_kernel, out_shape=[jax.ShapeDtypeStruct(value.sha...  82.6 us
    unnamed x10, local copies, waits for them, and re-layouts  3.78 us

profile of v4, /device:TPU:1, one launch (start us, length us, event | category | flops | bytes accessed | tf_op | source)
XLA Modules:
  0.0 88.5 jit_solution(13036185004364434642)
XLA Ops:
  0.7 82.6 %backward.1 = (bf16[8,9216]{1,0:T(8,128)(2,1)}, bf16[4,9216]{1,0:T(4,128)(2,1)}, bf16[2,9216]{1,0:T(2,128)(2,1)}, bf16[1,9216]{1,0:T(2,128)(2,1)}, f32[64,128]{1,0:T(8,128)}) custom-call(bf16[8,9216]{1,0:T(8,128)(2,1)} %f1_ref.1, bf16[4,9216]{1,0:T(4,128)(2,1)} %f2_ref.1, bf16[2,9216]{1,0:T(2,128)(2,1)} %f3_ref.1, bf16[1,9216]{1,0:T(2,128)(2,1)} %f4_ref.1, ...), custom_call_target="tpu_custom_call" | custom-call | tf_op jit(solution)/shard_map/backward/pallas_call | solution.py:724
  83.2 1.5 %dynamic_slice.3 = f32[6282]{0:T(1024)} dynamic-slice(f32[8192]{0:T(1024)} %bitcast.19, s32[]{:T(128)S(6)} %select_n.11), dynamic_slice_sizes={6282} | dynamic-slice | bytes 50260 | tf_op jit(solution)/shard_map/dynamic_slice | solution.py:752
  84.7 0.0 copy-start
  84.7 1.6 %copy.40 = bf16[8,9216]{1,0:T(8,128)(2,1)} copy(bf16[8,9216]{1,0:T(8,128)(2,1)} %get-tuple-element.20) | data formatting | bytes 294912
  86.3 0.0 copy-done
  86.3 0.0 copy-start.2
  86.3 0.6 copy.41
  87.0 0.1 copy-done.2
  87.1 0.0 copy-start.1
  87.1 0.6 copy.42
  87.7 0.2 copy-done.1
  87.9 0.6 copy.43
Async XLA Ops:
  84.7 1.6 %copy-start = (bf16[4,9216]{1,0:T(4,128)(2,1)S(1)}, bf16[4,9216]{1,0:T(4,128)(2,1)}, u32[]{:S(2)}) copy-start(bf16[4,9216]{1,0:T(4,128)(2,1)} %get-tuple-element.21) | copy-start | bytes 221188
  86.3 0.8 copy-start.2
  87.1 0.8 copy-start.1

commit v5 on v4

--- a/solution.py
+++ b/solution.py
@@ -20,7 +20,7 @@
     row, col = divmod(share, 8)
     core, z_hi, y = row % 2, (row // 2) % 2, row // 4
     half, quarter = divmod(col, 4)
-    return ((y * 2 + core) * 4 + quarter) * 4 + z_hi * 2 + half
+    return (((y * 2 + core) * 2 + z_hi) * 4 + quarter) * 2 + half
 
 
 def pack_shares(flat_ref, packed_ref, block):
@@ -31,89 +31,142 @@
 
 
 BLOCK = 16 * WINDOW
-PART = 4 * WINDOW
+HALF = 8 * WINDOW
+PART = 2 * WINDOW
 
 
 class Reduction:
-    def __init__(self, packed, where, from_core, sum_core, from_x, sum_x, from_y, core_send, core_recv, x_send, x_recv, y_send, y_recv):
-        self.packed, self.where = packed, where
-        self.from_core, self.sum_core, self.from_x, self.sum_x, self.from_y = from_core, sum_core, from_x, sum_x, from_y
-        self.core_send, self.core_recv = core_send, core_recv
-        self.x_send, self.x_recv, self.y_send, self.y_recv = x_send, x_recv, y_send, y_recv
+    def __init__(self, packed, where, from_core, sum_core, x_first, sum_x, y_second, y_first, sum_y, x_second, sems):
+        self.packed, self.where, self.from_core, self.sum_core = packed, where, from_core, sum_core
+        self.x_first, self.sum_x, self.y_second = x_first, sum_x, y_second
+        self.y_first, self.sum_y, self.x_second = y_first, sum_y, x_second
+        self.sems = sems
 
     def core_copy(self, block):
         x, row, col = self.where
-        core = row % 2
-        start = pl.multiple_of((block * 2 + 1 - core) * BLOCK, BLOCK)
+        start = pl.multiple_of((block * 2 + 1 - row % 2) * BLOCK, BLOCK)
+        send, recv = self.sems[0:2]
         return remote(
             self.packed.at[pl.ds(start, BLOCK)], self.from_core.at[pl.ds(block * BLOCK, BLOCK)],
-            self.core_send.at[block], self.core_recv.at[block], (x, row + 1 - 2 * core, col),
-        )
-
-    def x_copy(self, block, step):
+            send.at[block], recv.at[block], (x, row + 1 - 2 * (row % 2), col),
+        )
+
+    def x_first_copy(self, block, step):
         x, row, col = self.where
         there = (x + step) % 4
         start = pl.multiple_of(block * BLOCK + there * PART, PART)
         slot = block * 3 + step - 1
+        send, recv = self.sems[2:4]
         return remote(
-            self.sum_core.at[pl.ds(start, PART)], self.from_x.at[slot], self.x_send.at[slot], self.x_recv.at[slot],
-            (there, row, col),
-        )
-
-    def y_copy(self, block):
+            self.sum_core.at[pl.ds(start, PART)], self.x_first.at[slot], send.at[slot], recv.at[slot], (there, row, col)
+        )
+
+    def y_first_copy(self, block):
         x, row, col = self.where
-        y = row // 4
-        step = (block - y + 4) % 4
+        step = (block - row // 4 + 4) % 4
+        send, recv = self.sems[4:6]
         return remote(
-            self.sum_x.at[pl.ds(block * PART, PART)], self.from_y.at[step], self.y_send.at[step], self.y_recv.at[step],
+            self.sum_core.at[pl.ds(block * BLOCK + HALF, HALF)], self.y_first.at[step], send.at[step], recv.at[step],
             (x, block * 4 + row % 4, col),
+        )
+
+    def y_second_copy(self, block):
+        x, row, col = self.where
+        step = (block - row // 4 + 4) % 4
+        send, recv = self.sems[6:8]
+        return remote(
+            self.sum_x.at[pl.ds(block * PART, PART)], self.y_second.at[step], send.at[step], recv.at[step],
+            (x, block * 4 + row % 4, col),
+        )
+
+    def x_second_copy(self, step):
+        x, row, col = self.where
+        there = (x + step) % 4
+        send, recv = self.sems[8:10]
+        return remote(
+            self.sum_y.at[pl.ds(pl.multiple_of(there * PART, PART), PART)], self.x_second.at[step - 1],
+            send.at[step - 1], recv.at[step - 1], (there, row, col),
         )
 
     def leave(self, block):
         self.core_copy(block).start()
 
-    def along_x(self, block):
-        core = self.where[1] % 2
+    def spread(self, block):
+        core, y = self.where[1] % 2, self.where[1] // 4
         self.core_copy(block).wait()
-
-        @pl.loop(0, 4)
-        def _(part):
-            mine = pl.multiple_of((block * 2 + core) * BLOCK + part * PART, PART)
-            place = pl.multiple_of(block * BLOCK + part * PART, PART)
-            total = self.packed[pl.ds(mine, PART), :].astype(F32) + self.from_core[pl.ds(place, PART), :].astype(F32)
-            self.sum_core[pl.ds(place, PART), :] = total.astype(BF16)
-
-        for step in range(1, 4):
-            self.x_copy(block, step).start()
-
-    def along_y(self, block):
+        for half in range(2):
+
+            @pl.loop(0, 2)
+            def _(part):
+                mine = pl.multiple_of((block * 2 + core) * BLOCK + half * HALF + part * (HALF // 2), HALF // 2)
+                place = pl.multiple_of(block * BLOCK + half * HALF + part * (HALF // 2), HALF // 2)
+                total = self.packed[pl.ds(mine, HALF // 2), :].astype(F32)
+                total = total + self.from_core[pl.ds(place, HALF // 2), :].astype(F32)
+                self.sum_core[pl.ds(place, HALF // 2), :] = total.astype(BF16)
+
+            if half == 0:
+                for step in range(1, 4):
+                    self.x_first_copy(block, step).start()
+            else:
+
+                @pl.when(y != block)
+                def _():
+                    self.y_first_copy(block).start()
+
+    def turn_to_y(self, block):
         x, row, col = self.where
         for step in range(1, 4):
-            self.x_copy(block, step).wait()
+            self.x_first_copy(block, step).wait()
         own = pl.multiple_of(block * BLOCK + x * PART, PART)
         total = self.sum_core[pl.ds(own, PART), :].astype(F32)
         for step in range(3):
-            total = total + self.from_x[block * 3 + step].astype(F32)
+            total = total + self.x_first[block * 3 + step].astype(F32)
         self.sum_x[block * PART : (block + 1) * PART, :] = total.astype(BF16)
 
         @pl.when(row // 4 != block)
         def _():
-            self.y_copy(block).start()
-
-    def plane_sum(self, sum_plane):
+            self.y_second_copy(block).start()
+
+    def waiting(self, src, slots, step, sems):
+        send, recv = sems
+        return remote(src, slots.at[step], send.at[step], recv.at[step], self.where)
+
+    def turn_to_x(self):
         y = self.where[1] // 4
         for step in range(1, 4):
-            remote(
-                self.sum_x.at[pl.ds(0, PART)], self.from_y.at[step], self.y_send.at[step], self.y_recv.at[step], self.where
-            ).wait_recv()
+            self.waiting(self.sum_core.at[pl.ds(0, HALF)], self.y_first, step, self.sems[4:6]).wait_recv()
+
+        @pl.loop(0, 4)
+        def _(part):
+            own = pl.multiple_of(y * BLOCK + HALF + part * PART, PART)
+            at = pl.ds(pl.multiple_of(part * PART, PART), PART)
+            total = self.sum_core[pl.ds(own, PART), :].astype(F32)
+            for step in range(1, 4):
+                total = total + self.y_first[step, at, :].astype(F32)
+            self.sum_y[at, :] = total.astype(BF16)
+
+        for step in range(1, 4):
+            self.x_second_copy(step).start()
+
+    def plane_sum(self, sum_plane):
+        x, y = self.where[0], self.where[1] // 4
+        for step in range(1, 4):
+            self.waiting(self.sum_x.at[pl.ds(0, PART)], self.y_second, step, self.sems[6:8]).wait_recv()
         total = self.sum_x[pl.ds(pl.multiple_of(y * PART, PART), PART), :].astype(F32)
         for step in range(1, 4):
-            total = total + self.from_y[step].astype(F32)
-        sum_plane[...] = total.astype(BF16)
+            total = total + self.y_second[step].astype(F32)
+        sum_plane[0:PART, :] = total.astype(BF16)
         for step in range(1, 4):
-            remote(
-                self.sum_x.at[pl.ds(0, PART)], self.from_y.at[step], self.y_send.at[step], self.y_recv.at[step], self.where
-            ).wait_send()
+            self.x_second_copy(step).wait()
+        total = self.sum_y[pl.ds(pl.multiple_of(x * PART, PART), PART), :].astype(F32)
+        for step in range(3):
+            total = total + self.x_second[step].astype(F32)
+        sum_plane[PART:, :] = total.astype(BF16)
+
+    def close(self):
+        for step in range(1, 4):
+            self.waiting(self.sum_core.at[pl.ds(0, HALF)], self.y_first, step, self.sems[4:6]).wait_send()
+            self.waiting(self.sum_x.at[pl.ds(0, PART)], self.y_second, step, self.sems[6:8]).wait_send()
 
 
 def remote(src, dst, send_sem, recv_sem, peer):
@@ -128,17 +181,17 @@
     from_line,
     share_buf,
     square_buf,
-    from_near,
-    near_buf,
     from_far,
+    far_buf,
+    from_plane,
     line_send,
     line_recv,
     share_send,
     share_recv,
-    near_send,
-    near_recv,
     far_send,
     far_recv,
+    plane_send,
+    plane_recv,
 ):
     x = lax.axis_index("branch")
     row = lax.axis_index("row")
@@ -151,9 +204,12 @@
         there = (z + step) % 16
         return (x, y * 4 + (there // 8) * 2 + core, there % 8)
 
-    def near_peer(step):
-        there = (y * 2 + core + step) % 8
-        return (x, (there // 2) * 4 + z_hi * 2 + there % 2, col)
+    def plane_peer(step):
+        there = (x * 8 + y * 2 + core + step) % 32
+        return (there // 8, (there % 8) // 2 * 4 + z_hi * 2 + there % 2, col)
+
+    def far_copy(step):
+        return remote(square_buf, from_far.at[step - 1], far_send.at[step - 1], far_recv.at[step - 1], line_peer(step))
 
     def line_copy(block):
         target = (block // 2) * 8 + (block % 2) * 4 + x
@@ -194,49 +250,51 @@
         for slot in range(15):
             total = total + from_line[slot].astype(jnp.float32)
         share_buf[...] = total
+        offset = (SHARE * (row * 8 + col)) % 1024
+        place = lax.broadcasted_iota(jnp.int32, (WINDOW, 128), 0) * 128 + lax.broadcasted_iota(
+            jnp.int32, (WINDOW, 128), 1
+        )
+        inside = jnp.logical_and(place >= offset, place < offset + SHARE)
+        square_buf[...] = jnp.where(inside, total * total, 0.0).reshape(8, 8, 128).sum(axis=0)
+
+        @pl.loop(1, 16)
+        def _(step):
+            far_copy(step).start()
+
         for step in range(1, 4):
             share_copy(step).start()
+
+    @pl.when(jnp.logical_not(owner))
+    def _():
+        square_buf[...] = jnp.zeros((8, 128), F32)
+
+    far_buf[...] = square_buf[...]
+    for index in range(4):
+        source = 4 * index + x
+        step = (z - source + 16) % 16
+
+        @pl.when(step != 0)
+        def _():
+            slot = (step + 15) % 16
+            remote(square_buf, from_far.at[slot], far_send.at[0], far_recv.at[slot], partner).wait_recv()
+            far_buf[...] += from_far[slot]
+
+    def plane_copy(step):
+        return remote(far_buf, from_plane.at[step - 1], plane_send.at[step - 1], plane_recv.at[step - 1], plane_peer(step))
+
+    @pl.loop(1, 32)
+    def _(step):
+        plane_copy(step).start()
 
     @pl.when(jnp.logical_not(owner))
     def _():
         share_copy(1).wait_recv()
 
-    offset = (SHARE * (row * 8 + col)) % 1024
-    place = lax.broadcasted_iota(jnp.int32, (WINDOW, 128), 0) * 128 + lax.broadcasted_iota(jnp.int32, (WINDOW, 128), 1)
-    inside = jnp.logical_and(place >= offset, place < offset + SHARE)
-    share = share_buf[...]
-    squares = jnp.where(inside, share * share, 0.0)
-    square_buf[...] = squares.reshape(8, 8, 128).sum(axis=0)
-
-    def near_copy(step):
-        return remote(
-            square_buf, from_near.at[step - 1], near_send.at[step - 1], near_recv.at[step - 1], near_peer(step)
-        )
-
-    @pl.loop(1, 8)
+    @pl.loop(1, 32)
     def _(step):
-        near_copy(step).start()
-
-    @pl.loop(1, 8)
-    def _(step):
-        near_copy(step).wait()
-
-    near_buf[...] = square_buf[...] + from_near[...].sum(axis=0)
-
-    def far_copy(step):
-        return remote(
-            near_buf, from_far.at[step - 1], far_send.at[step - 1], far_recv.at[step - 1], line_peer(step)
-        )
-
-    @pl.loop(1, 16)
-    def _(step):
-        far_copy(step).start()
-
-    @pl.loop(1, 16)
-    def _(step):
-        far_copy(step).wait()
-
-    total_squares = jnp.sum(near_buf[...] + from_far[...].sum(axis=0), keepdims=True)
+        plane_copy(step).wait()
+
+    total_squares = jnp.sum(far_buf[...] + from_plane[...].sum(axis=0), keepdims=True)
     spread_rms = jnp.sqrt(total_squares / TOTAL + EPSILON)
     out_ref[...] = share_buf[...] * jnp.minimum(jnp.float32(1.0), 1.0 / spread_rms)
 
@@ -249,11 +307,16 @@
 
     @pl.when(owner)
     def _():
+        @pl.loop(1, 16)
+        def _(step):
+            far_copy(step).wait_send()
+
         for step in range(1, 4):
             share_copy(step).wait_send()
 
 
 GROUP = 384
+LATE = 28
 CELLS = 24
 PIECES = (
     (48, 0, 0, 432), (96, 162, 0, 864), (192, 810, 0, 1728), (96, 3402, 864, 432), (192, 3726, 1728, 864),
@@ -270,21 +333,32 @@
     return lax.broadcasted_iota(jnp.int32, (rows, lanes), 1)
 
 
-def fill_packets(u1, u2, u3, send_rows, send_sides, send_corners):
-    wide = CELLS * GROUP
-    last = wide - GROUP
-    blank = jnp.zeros((1, wide), F32)
-    bottom = jnp.concatenate([u1[4:8], u2[2:4], u3[1:2], blank], axis=0)
-    top = jnp.concatenate([u2[0:2], u3[0:1], blank, u1[0:4]], axis=0)
-    empty = jnp.zeros((8, GROUP), F32)
-    for index, part in enumerate((bottom, top)):
-        send_rows[index] = jnp.concatenate([part[:, : wide // 2], part[:, wide // 2 :]], axis=0).astype(BF16)
-        send_corners[2 * index] = jnp.concatenate([part[:, last:], empty], axis=0).astype(BF16)
-        send_corners[2 * index + 1] = jnp.concatenate([part[:, :GROUP], empty], axis=0).astype(BF16)
-    for index, start in enumerate((last, 0)):
-        send_sides[index] = jnp.concatenate(
-            [u1[:, start : start + GROUP], u2[:, start : start + GROUP], u3[:, start : start + GROUP], empty[:2]], axis=0
-        ).astype(BF16)
+def packet_rows(up):
+    maps = (
+        (0, 3, 16, (11, 4), (3, 12)), (1, 3, 8, (5, 2), (1, 6)), (2, 3, 4, (2, 1), (0, 3)),
+        (3, 2, 8, (5, 2), (1, 6)), (4, 1, 4, (2, 1), (0, 3)), (5, 2, 4, (2, 1), (0, 3)),
+    )
+    return [
+        (index, tile, rows, leaves[up], lands[up]) for index, tiles, rows, leaves, lands in maps for tile in range(tiles)
+    ]
+
+
+def fill_packets(maps, send_rows, send_corners):
+    for up in range(2):
+        parts = [
+            maps[index][tile, pl.ds(rows + leaves, CELLS, stride=rows), :]
+            for index, tile, rows, leaves, lands in packet_rows(up)
+        ]
+        send_rows[up] = jnp.concatenate(parts, axis=0).astype(BF16)
+        blank = [jnp.zeros((2, 128), F32)]
+        send_corners[2 * up] = jnp.concatenate([part[CELLS - 1 : CELLS] for part in parts] + blank, axis=0).astype(BF16)
+        send_corners[2 * up + 1] = jnp.concatenate([part[0:1] for part in parts] + blank, axis=0).astype(BF16)
+
+
+def fill_sides(u1, u2, u3, send_sides):
+    for index, start in enumerate(((CELLS - 1) * GROUP, 0)):
+        parts = [value[:, start : start + GROUP] for value in (u1, u2, u3)] + [jnp.zeros((2, GROUP), F32)]
+        send_sides[index] = jnp.concatenate(parts, axis=0).astype(BF16)
 
 
 def banded(weights, repeat, width, rows, blocks, dst):
@@ -349,16 +423,25 @@
 
 
 def backward_kernel(
-    f1_ref, f2_ref, f3_ref, f4_ref, o1_ref, o2_ref, o3_ref, u1_ref, u2_ref, u3_ref,
+    u1_ref, u2_ref, u3_ref, *refs,
+):
+    far = refs[:LATE]
+    outs, near, (late_sems, *rest) = refs[LATE : LATE + 5], refs[LATE + 5 : 2 * LATE + 5], refs[2 * LATE + 5 :]
+    copies = [pltpu.make_async_copy(src, dst, late_sems.at[i]) for i, (src, dst) in enumerate(zip(far, near))]
+    for copy in copies:
+        copy.start()
+    backward_stages(copies, u1_ref, u2_ref, u3_ref, *near, *outs, *rest)
+
+
+def backward_stages(
+    late_copies, u1_ref, u2_ref, u3_ref, f1_ref, f2_ref, f3_ref, f4_ref, o1_ref, o2_ref, o3_ref,
     k1_ref, k2_ref, k3_ref, s12_ref, s23_ref, m21_ref, m31_ref, m41_ref, m32_ref, m42_ref, m43_ref,
     rep1_ref, rep2_ref, rep3_ref, rep12_ref, rep23_ref, rep96_ref, rep192_ref, pool1_ref, pool2_ref, pool3_ref,
     g1_ref, g2_ref, g3_ref, g4_ref, share_ref,
     packed_ref, send_rows, send_sides, send_corners, recv_rows, recv_sides, recv_corners, halo_send, halo_recv,
-    ext1, ext2, ext3, v1, v2, v3, del1, del2, del3, pad_f2, pad_f3, pad_o1, pad_o2, pad_o3, rows_f4,
+    ext1, ext2, ext3, pp12, pp13, pp23, v1, v2, v3, del1, del2, del3, pad_f2, pad_f3, pad_o1, pad_o2, pad_o3, rows_f4,
     band1, band2, band3, band12, band23, band21, band31, band32, res2, res3, w48, w96, w192, flat, *reduce_refs,
 ):
-    half = CELLS // 2
-
     def lanes(g):
         return slice(GROUP * g, GROUP * (g + 1))
 
@@ -388,9 +471,9 @@
         there = (z + step) % 16
         return (x, y * 4 + (there // 8) * 2 + core, there % 8)
 
-    def near_peer(step):
-        there = (y * 2 + core + step) % 8
-        return (x, (there // 2) * 4 + z_hi * 2 + there % 2, col)
+    def plane_peer(step):
+        there = (x * 8 + y * 2 + core + step) % 32
+        return (there // 8, (there % 8) // 2 * 4 + z_hi * 2 + there % 2, col)
 
     def greet(peer):
         pl.semaphore_signal(barrier, inc=1, device_id=peer, device_id_type=MESH)
@@ -398,20 +481,69 @@
     barrier = pltpu.get_barrier_semaphore()
     for route in routes:
         greet(peer(route[1], route[2]))
-    for step in range(1, 4):
-        greet(((x + step) % 4, row, col))
-
     @pl.loop(1, 16)
     def _(step):
         greet(line_peer(step))
 
-    @pl.loop(1, 8)
+    @pl.loop(1, 32)
     def _(step):
-        greet(near_peer(step))
+        greet(plane_peer(step))
 
     u1, u2, u3 = (ref[...].astype(F32) for ref in (u1_ref, u2_ref, u3_ref))
-    fill_packets(u1, u2, u3, send_rows, send_sides, send_corners)
-    pl.semaphore_wait(barrier, 33)
+    fill_sides(u1, u2, u3, send_sides)
+    for ref in (ext1, ext2, ext3):
+        ref[...] = jnp.zeros_like(ref)
+    for g in range(CELLS):
+        for tile in range(3):
+            part = slice(GROUP * g + 128 * tile, GROUP * g + 128 * tile + 128)
+            ext1[tile, 16 * g + 20 : 16 * g + 28, :] = u1[:, part]
+            ext2[tile, 8 * g + 10 : 8 * g + 14, :] = u2[:, part]
+            ext3[tile, 4 * g + 5 : 4 * g + 7, :] = u3[:, part]
+
+    for copy in late_copies:
+        copy.wait()
+
+    tall1, tall2, tall3 = 16 * (CELLS + 2), 8 * (CELLS + 2), 4 * (CELLS + 2)
+    def tiled_store(ref, value, rows=slice(None)):
+        for tile in range(value.shape[1] // 128):
+            ref[tile, rows, :] = value[:, 128 * tile : 128 * tile + 128]
+
+    def strided(ref, tiles, start, count, stride):
+        parts = [ref[tile, pl.ds(start, count, stride=stride), :] for tile in tiles]
+        return parts[0] if len(parts) == 1 else jnp.concatenate(parts, axis=1)
+
+    def strided_sum(ref, picks, count, stride, tiles):
+        total = None
+        for pick in picks:
+            piece = strided(ref, tiles, pick, count, stride)
+            total = piece if total is None else total + piece
+        return total
+
+    def whole_of(ref, rows):
+        return jnp.concatenate([ref[tile, rows, :] for tile in range(ref.shape[0])], axis=1)
+
+    def run_pools():
+        tiled_store(v1, dot(whole_of(ext1, slice(0, tall1)).astype(BF16), pool1_ref[...]))
+        tiled_store(v2, dot(whole_of(ext2, slice(0, tall2)).astype(BF16), pool2_ref[...]))
+        tiled_store(pp12, strided_sum(v1, range(2), tall2, 2, (0, 1)))
+        tiled_store(pp13, strided_sum(v1, range(4), tall3, 4, (2,)))
+        tiled_store(pp23, strided_sum(v2, range(2), tall3, 2, (0, 1)))
+
+    def pooled():
+        return (
+            whole_of(pp12, slice(0, tall2)).astype(BF16),
+            whole_of(pp13, slice(0, tall3)).astype(BF16),
+            whole_of(pp23, slice(0, tall3)).astype(BF16),
+        )
+
+    run_pools()
+    tiled_store(v3, dot(whole_of(ext3, slice(0, tall3)).astype(BF16), pool3_ref[...]))
+    p14 = strided_sum(v1, range(16 + 4, 16 + 12), CELLS, 16, (3,)).astype(BF16)
+    p24 = strided_sum(v2, range(8 + 2, 8 + 6), CELLS, 8, (2,)).astype(BF16)
+    p34 = strided_sum(v3, range(4 + 1, 4 + 3), CELLS, 4, (0, 1)).astype(BF16)
+    p12, p13, p23 = pooled()
+    fill_packets((ext1, ext2, ext3, pp12, pp13, pp23), send_rows, send_corners)
+    pl.semaphore_wait(barrier, 54)
 
     def halo_copy(route):
         slot, down, right, src, dst = route
@@ -422,14 +554,6 @@
 
     for route in routes:
         halo_copy(route).start()
-
-    for ref in (ext1, ext2, ext3):
-        ref[...] = jnp.zeros_like(ref)
-    for g in range(CELLS):
-        at = lanes(g)
-        ext1[g + 1, 4:12, :] = u1[:, at]
-        ext2[8 * g + 10 : 8 * g + 14, :] = u2[:, at]
-        ext3[4 * g + 5 : 4 * g + 7, :] = u3[:, at]
 
     for ref in (pad_f2, pad_f3, pad_o1, pad_o2, pad_o3):
         ref[...] = jnp.zeros_like(ref)
@@ -454,33 +578,6 @@
     banded(m21_ref[...], rep96_ref[...], 96, 48, mixer_blocks(96, 4), band21)
     banded(m31_ref[...], rep192_ref[...], 192, 48, mixer_blocks(192, 2), band31)
     banded(m32_ref[...], rep96_ref[:, :256], 96, 192, mixer_blocks(96, 2), band32)
-
-    tall1, tall2, tall3 = 16 * (CELLS + 2), 8 * (CELLS + 2), 4 * (CELLS + 2)
-    def tiled_store(ref, value, rows=slice(None)):
-        for tile in range(value.shape[1] // 128):
-            ref[tile, rows, :] = value[:, 128 * tile : 128 * tile + 128]
-
-    def strided(ref, tiles, start, count, stride):
-        parts = [ref[tile, pl.ds(start, count, stride=stride), :] for tile in tiles]
-        return parts[0] if len(parts) == 1 else jnp.concatenate(parts, axis=1)
-
-    def strided_sum(ref, picks, count, stride, tiles):
-        total = None
-        for pick in picks:
-            piece = strided(ref, tiles, pick, count, stride)
-            total = piece if total is None else total + piece
-        return total.astype(BF16)
-
-    tiled_store(v1, dot(ext1[...].reshape(tall1, GROUP).astype(BF16), pool1_ref[...]))
-    tiled_store(v2, dot(ext2[0:tall2, :].astype(BF16), pool2_ref[...]))
-    tiled_store(v3, dot(ext3[0:tall3, :].astype(BF16), pool3_ref[...]))
-
-    p12 = strided_sum(v1, range(2), tall2, 2, (0, 1))
-    p13 = strided_sum(v1, range(4), tall3, 4, (2,))
-    p14 = strided_sum(v1, range(16 + 4, 16 + 12), CELLS, 16, (3,))
-    p23 = strided_sum(v2, range(2), tall3, 2, (0, 1))
-    p24 = strided_sum(v2, range(8 + 2, 8 + 6), CELLS, 8, (2,))
-    p34 = strided_sum(v3, range(4 + 1, 4 + 3), CELLS, 4, (0, 1))
 
     def fold_mixer(grads, width, rows, base, dst):
         total = None
@@ -509,37 +606,35 @@
         halo_copy(route).wait()
     top, bottom = jnp.where(line > 0, 1.0, 0.0), jnp.where(line < 63, 1.0, 0.0)
     left, right = jnp.where(col > 0, 1.0, 0.0), jnp.where(col < 7, 1.0, 0.0)
-    above, below = recv_rows[0].astype(F32) * top, recv_rows[1].astype(F32) * bottom
     sides = [recv_sides[0].astype(F32) * left, recv_sides[1].astype(F32) * right]
     corners = [
         recv_corners[0].astype(F32) * (top * left), recv_corners[1].astype(F32) * (top * right),
         recv_corners[2].astype(F32) * (bottom * left), recv_corners[3].astype(F32) * (bottom * right),
     ]
-    for g in range(CELLS + 2):
-        if g == 0 or g == CELLS + 1:
-            side = sides[0 if g == 0 else 1]
-            ext1[g, 4:12, :] = side[0:8]
-            ext2[8 * g + 2 : 8 * g + 6, :] = side[8:12]
-            ext3[4 * g + 1 : 4 * g + 3, :] = side[12:14]
-            up = corners[0 if g == 0 else 1]
-            down = corners[2 if g == 0 else 3]
-        else:
-            row0 = 8 * ((g - 1) // half)
-            there = lanes((g - 1) % half)
-            up, down = above[row0 : row0 + 8, there], below[row0 : row0 + 8, there]
-        ext1[g, 0:4, :] = up[0:4]
-        ext1[g, 12:16, :] = down[4:8]
-        ext2[8 * g : 8 * g + 2, :] = up[4:6]
-        ext2[8 * g + 6 : 8 * g + 8, :] = down[0:2]
-        ext3[4 * g : 4 * g + 1, :] = up[6:7]
-        ext3[4 * g + 3 : 4 * g + 4, :] = down[2:3]
-
-
-    tiled_store(v1, dot(ext1[...].reshape(tall1, GROUP).astype(BF16), pool1_ref[...]))
-    tiled_store(v2, dot(ext2[0:tall2, :].astype(BF16), pool2_ref[...]))
-    p12 = strided_sum(v1, range(2), tall2, 2, (0, 1))
-    p13 = strided_sum(v1, range(4), tall3, 4, (2,))
-    p23 = strided_sum(v2, range(2), tall3, 2, (0, 1))
+    for index, group in enumerate((0, CELLS + 1)):
+        for tile in range(3):
+            part = sides[index][:, 128 * tile : 128 * tile + 128]
+            ext1[tile, 16 * group + 4 : 16 * group + 12, :] = part[0:8]
+            ext2[tile, 8 * group + 2 : 8 * group + 6, :] = part[8:12]
+            ext3[tile, 4 * group + 1 : 4 * group + 3, :] = part[12:14]
+
+    def fill_rims(refs, first):
+        for up, flag in enumerate((top, bottom)):
+            packet = recv_rows[up].astype(F32) * flag
+            for place_in, (index, tile, rows, leaves, lands) in enumerate(packet_rows(up)):
+                if not first <= index < first + 3:
+                    continue
+                ref = refs[index - first]
+                part = packet[CELLS * place_in : CELLS * (place_in + 1)]
+                ref[tile, pl.ds(rows + lands, CELLS, stride=rows), :] = part
+                ref[tile, lands : lands + 1, :] = corners[2 * up][place_in : place_in + 1]
+                last = rows * (CELLS + 1) + lands
+                ref[tile, last : last + 1, :] = corners[2 * up + 1][place_in : place_in + 1]
+
+    fill_rims((ext1, ext2, ext3), 0)
+    run_pools()
+    fill_rims((pp12, pp13, pp23), 3)
+    p12, p13, p23 = pooled()
 
     def fold_down(grads, width, rows, a, base, dst):
         for b in range(3):
@@ -557,14 +652,16 @@
         for a in range(3):
             at = skip + (1 if a == 0 else 0)
             xs = jnp.concatenate(
-                [ext[at : at + count, :], ext[at + skip : at + skip + count, 0:head]], axis=1
+                [ext[tile, at : at + count, :] for tile in range(3)]
+                + [ext[tile, at + skip : at + skip + count, :] for tile in range(head // 128)],
+                axis=1,
             ).astype(BF16)
             fold_down(dot(even if a == 1 else odd, xs, 0, 0), width, rows, a, base, dst)
 
     down_grads(pad_o1, ext2, 8, 8 * CELLS, 128, 96, 48, 864, w96)
     down_grads(pad_o2, ext3, 4, 4 * CELLS, 256, 192, 96, 1728, w192)
 
-    reduction = Reduction(packed_ref, (x, row, col), *reduce_refs[:11])
+    reduction = Reduction(packed_ref, (x, row, col), *reduce_refs[:8], reduce_refs[8:18])
     flat[6282:FLAT_ROWS, :] = jnp.zeros((FLAT_ROWS - 6282, 128), F32)
 
     def settle(pieces, blocks):
@@ -589,21 +686,23 @@
     def rolled(value):
         return pltpu.roll(value, value.shape[0] - 1, 0)
 
-    x2 = jnp.concatenate([ext2[0:tall2, :], ext2[8 : tall2 + 8, 0:128]], axis=1).astype(BF16)
+    x2 = jnp.concatenate([whole_of(ext2, slice(0, tall2)), ext2[0, 8 : tall2 + 8, :]], axis=1).astype(BF16)
     tiled_store(v1, dot(x2, band12[1], 1, 1), pl.ds(0, tall2, stride=2))
     tiled_store(v1, dot(x2, band12[2], 1, 1) + rolled(dot(x2, band12[0], 1, 1)), pl.ds(1, tall2, stride=2))
     spread1 = jnp.concatenate([v1[tile] for tile in range(3)], axis=1)
-    delta1 = ext1[...] + spread1.reshape(CELLS + 2, 16, GROUP)
+    delta1 = (whole_of(ext1, slice(0, tall1)) + spread1).reshape(CELLS + 2, 16, GROUP)
     del1[...] = (delta1 * rim_mask(16, 8)).astype(BF16).astype(F32)
 
-    x3 = jnp.concatenate([ext3[0:tall3, :], ext3[4 : tall3 + 4, 0:256]], axis=1).astype(BF16)
+    x3 = jnp.concatenate(
+        [whole_of(ext3, slice(0, tall3)), ext3[0, 4 : tall3 + 4, :], ext3[1, 4 : tall3 + 4, :]], axis=1
+    ).astype(BF16)
     tiled_store(v2, dot(x3, band23[1], 1, 1), pl.ds(0, tall3, stride=2))
     tiled_store(v2, dot(x3, band23[2], 1, 1) + rolled(dot(x3, band23[0], 1, 1)), pl.ds(1, tall3, stride=2))
     spread2 = jnp.concatenate([v2[tile] for tile in range(3)], axis=1)
-    delta2 = ext2[0:tall2, :] + dot(p12[:, 0:192], band21[...]) + spread2
+    delta2 = whole_of(ext2, slice(0, tall2)) + dot(p12[:, 0:192], band21[...]) + spread2
     del2[8 : 8 + tall2, :] = (delta2 * rim_mask(8, 4).reshape(tall2, GROUP)).astype(BF16).astype(F32)
 
-    delta3 = ext3[0:tall3, :] + dot(p13[:, 0:96], band31[...]) + dot(p23, band32[...], 1, 1)
+    delta3 = whole_of(ext3, slice(0, tall3)) + dot(p13[:, 0:96], band31[...]) + dot(p23, band32[...], 1, 1)
     place_row = lax.broadcasted_iota(jnp.int32, (tall3, GROUP), 0)
     in_group = jnp.bitwise_and(place_row, 3)
     by_row = jnp.where(in_group == 0, top, jnp.where(in_group == 3, bottom, 1.0))
@@ -613,7 +712,7 @@
         ref[0:8, :] = jnp.zeros((8, GROUP), F32)
         ref[ref.shape[0] - 8 :, :] = jnp.zeros((8, GROUP), F32)
 
-    reduction.along_x(3)
+    reduction.spread(3)
 
     def fold(grads, width, base, a, dst):
         total = None
@@ -656,8 +755,8 @@
     for g in range(CELLS):
         g2_ref[:, lanes(g)] = res2[8 * g + 2 : 8 * g + 6, :].astype(BF16)
 
-    reduction.along_x(2)
-    reduction.along_x(1)
+    reduction.spread(2)
+    reduction.spread(1)
 
     f1 = f1_ref[...]
     f1 = jnp.concatenate([f1[:, lanes(g)].astype(F32) for g in range(CELLS)], axis=0).astype(BF16)
@@ -674,11 +773,13 @@
         g1_ref[:, lanes(g)] = back[8 * g : 8 * g + 8].astype(BF16)
 
     settle((0, 1), (0,))
-    reduction.along_x(0)
+    reduction.spread(0)
     for block in (3, 2, 1, 0):
-        reduction.along_y(block)
-    reduction.plane_sum(reduce_refs[11])
-    finish_shares(share_ref, *reduce_refs[11:])
+        reduction.turn_to_y(block)
+    reduction.turn_to_x()
+    reduction.plane_sum(reduce_refs[18])
+    finish_shares(share_ref, *reduce_refs[18:])
+    reduction.close()
 
 
 def repeats(width, lanes, base=0):
@@ -707,7 +808,7 @@
     ]
     whole = pl.BlockSpec(memory_space=pltpu.VMEM)
     inputs = [
-        f1, f2, f3, f4, o1, o2, o3, u1, u2, u3,
+        u1, u2, u3, f1, f2, f3, f4, o1, o2, o3,
         k1.reshape(432, 48), k2.reshape(864, 96), k3.reshape(1728, 192), s12.reshape(432, 96), s23.reshape(864, 192),
         m21.T, m31.T, m41.T, m32, m42.T, m43.T,
     ] + constants
@@ -720,16 +821,18 @@
 
     ext = CELLS + 2
     dma = pltpu.SemaphoreType.DMA
-    packets = ((2, 16, CELLS * GROUP // 2), (2, 16, GROUP), (4, 16, GROUP))
+    packets = ((2, 14 * CELLS, 128), (2, 16, GROUP), (4, 16, 128))
     grad_one, grad_two, grad_three, grad_four, share = pl.pallas_call(
         backward_kernel,
         out_shape=[jax.ShapeDtypeStruct(value.shape, BF16) for value in (f1, f2, f3, f4)]
         + [jax.ShapeDtypeStruct((WINDOW, 128), F32)],
-        in_specs=[whole] * len(inputs),
+        in_specs=[whole] * 3 + [pl.BlockSpec(memory_space=pl.ANY)] * LATE,
         out_specs=[whole] * 5,
         scratch_shapes=[
+            *(pltpu.VMEM(value.shape, BF16) for value in inputs[3:]), dma((LATE,)),
             bf16(128 * WINDOW, 128), *(bf16(*shape) for shape in packets + packets), dma((8,)), dma((8,)),
-            f32(ext, 16, GROUP), f32(8 * ext + 8, GROUP), f32(4 * ext + 8, GROUP),
+            f32(3, 16 * ext, 128), f32(3, 8 * ext + 8, 128), f32(3, 4 * ext + 8, 128),
+            f32(2, 8 * ext, 128), f32(1, 4 * ext, 128), f32(2, 4 * ext, 128),
             f32(4, 16 * ext, 128), f32(3, 8 * ext, 128), f32(2, 4 * ext, 128),
             f32(ext, 16, GROUP), f32(8 * ext + 16, GROUP), f32(4 * ext + 16, GROUP),
             f32(8 * CELLS, GROUP), f32(4 * CELLS, GROUP), f32(3, 16 * CELLS, 128), f32(3, 8 * CELLS, 128),
@@ -739,9 +842,10 @@
             f32(8 * CELLS, GROUP), f32(4 * CELLS, GROUP),
             f32(1, 1104, 128), f32(1, 1872, 128), f32(2, 2976, 128), f32(FLAT_ROWS, 128),
             bf16(4 * BLOCK, 128), bf16(4 * BLOCK, 128), bf16(12, PART, 128), bf16(4 * PART, 128), bf16(4, PART, 128),
-            dma((4,)), dma((4,)), dma((12,)), dma((12,)), dma((4,)), dma((4,)),
-            bf16(PART, 128), bf16(15, WINDOW, 128), f32(WINDOW, 128), f32(8, 128), f32(7, 8, 128), f32(8, 128), f32(15, 8, 128),
-            dma((4,)), dma((15,)), dma((3,)), dma((1,)), dma((7,)), dma((7,)), dma((15,)), dma((15,)),
+            bf16(4, HALF, 128), bf16(HALF, 128), bf16(3, PART, 128),
+            dma((4,)), dma((4,)), dma((12,)), dma((12,)), dma((4,)), dma((4,)), dma((4,)), dma((4,)), dma((3,)), dma((3,)),
+            bf16(2 * PART, 128), bf16(15, WINDOW, 128), f32(WINDOW, 128), f32(8, 128), f32(15, 8, 128), f32(8, 128), f32(31, 8, 128),
+            dma((4,)), dma((15,)), dma((3,)), dma((1,)), dma((15,)), dma((15,)), dma((31,)), dma((31,)),
         ],
         compiler_params=pltpu.CompilerParams(
             collective_id=0, has_side_effects=True, vmem_limit_bytes=56 * 1024 * 1024

time: 90 us -> 81 us (0.900); the launches traced: 88.5 us -> 80.7 us
  Pallas kernels: 82.6 us -> 74.8 us
    pallas_call x1, Pallas kernels: 82.6 us -> 74.8 us  [local(): pl.pallas_call(backward_kernel, out_shape=[jax.ShapeDtypeStruct(value.sha...]
where the time goes in v5:
time: 81 us; the launch traced here: 80.7 us
  Pallas kernels  74.8 us (92%)
  local copies, waits for them, and re-layouts  5.23 us (6%)
    pallas_call x1, Pallas kernels, local(): pl.pallas_call(backward_kernel, out_shape=[jax.ShapeDtypeStruct(value.sha...  74.8 us
    unnamed x10, local copies, waits for them, and re-layouts  3.78 us

profile of v5, /device:TPU:1, one launch (start us, length us, event | category | flops | bytes accessed | tf_op | source)
XLA Modules:
  0.0 80.7 jit_solution(14926898009381595213)
XLA Ops:
  0.7 74.8 %backward.1 = (bf16[8,9216]{1,0:T(8,128)(2,1)}, bf16[4,9216]{1,0:T(4,128)(2,1)}, bf16[2,9216]{1,0:T(2,128)(2,1)}, bf16[1,9216]{1,0:T(2,128)(2,1)}, f32[64,128]{1,0:T(8,128)}) custom-call(bf16[8,9216]{1,0:T(8,128)(2,1)} %u1_ref.1, bf16[4,9216]{1,0:T(4,128)(2,1)} %u2_ref.1, bf16[2,9216]{1,0:T(2,128)(2,1)} %u3_ref.1, bf16[8,9216]{1,0:T(8,128)(2,1)} %refs_0_.1, ...), custom_call_target="tpu_custom_call" | custom-call | tf_op jit(solution)/shard_map/backward/pallas_call | solution.py:825
  75.4 1.5 %dynamic_slice.3 = f32[6282]{0:T(1024)} dynamic-slice(f32[8192]{0:T(1024)} %bitcast.19, s32[]{:T(128)S(6)} %select_n.11), dynamic_slice_sizes={6282} | dynamic-slice | bytes 50260 | tf_op jit(solution)/shard_map/dynamic_slice | solution.py:856
  76.9 0.0 copy-start
  76.9 1.6 %copy.40 = bf16[8,9216]{1,0:T(8,128)(2,1)} copy(bf16[8,9216]{1,0:T(8,128)(2,1)} %get-tuple-element.20) | data formatting | bytes 294912
  78.5 0.0 copy-done
  78.5 0.0 copy-start.2
  78.5 0.6 copy.41
  79.1 0.1 copy-done.2
  79.3 0.0 copy-start.1
  79.3 0.6 copy.42
  79.9 0.2 copy-done.1
  80.0 0.6 copy.43
Async XLA Ops:
  76.9 1.6 %copy-start = (bf16[4,9216]{1,0:T(4,128)(2,1)S(1)}, bf16[4,9216]{1,0:T(4,128)(2,1)}, u32[]{:S(2)}) copy-start(bf16[4,9216]{1,0:T(4,128)(2,1)} %get-tuple-element.21) | copy-start | bytes 221188
  78.5 0.8 copy-start.2
  79.3 0.8 copy-start.1

commit v6 on v5

--- a/solution.py
+++ b/solution.py
@@ -181,17 +181,21 @@
     from_line,
     share_buf,
     square_buf,
+    from_near,
+    near_buf,
     from_far,
     far_buf,
-    from_plane,
+    from_cross,
     line_send,
     line_recv,
     share_send,
     share_recv,
+    near_send,
+    near_recv,
     far_send,
     far_recv,
-    plane_send,
-    plane_recv,
+    cross_send,
+    cross_recv,
 ):
     x = lax.axis_index("branch")
     row = lax.axis_index("row")
@@ -204,12 +208,15 @@
         there = (z + step) % 16
         return (x, y * 4 + (there // 8) * 2 + core, there % 8)
 
-    def plane_peer(step):
-        there = (x * 8 + y * 2 + core + step) % 32
-        return (there // 8, (there % 8) // 2 * 4 + z_hi * 2 + there % 2, col)
+    def near_peer(step):
+        there = (y * 2 + core + step) % 8
+        return (x, there // 2 * 4 + z_hi * 2 + there % 2, col)
+
+    def near_copy(step):
+        return remote(square_buf, from_near.at[step - 1], near_send.at[step - 1], near_recv.at[step - 1], near_peer(step))
 
     def far_copy(step):
-        return remote(square_buf, from_far.at[step - 1], far_send.at[step - 1], far_recv.at[step - 1], line_peer(step))
+        return remote(near_buf, from_far.at[step - 1], far_send.at[step - 1], far_recv.at[step - 1], line_peer(step))
 
     def line_copy(block):
         target = (block // 2) * 8 + (block % 2) * 4 + x
@@ -257,18 +264,25 @@
         inside = jnp.logical_and(place >= offset, place < offset + SHARE)
         square_buf[...] = jnp.where(inside, total * total, 0.0).reshape(8, 8, 128).sum(axis=0)
 
+        for step in range(1, 8):
+            near_copy(step).start()
+        for step in range(1, 4):
+            share_copy(step).start()
+        squares = square_buf[...]
+        for step in range(1, 8):
+            near_copy(step).wait_recv()
+            squares = squares + from_near[step - 1]
+        near_buf[...] = squares
+
         @pl.loop(1, 16)
         def _(step):
             far_copy(step).start()
 
-        for step in range(1, 4):
-            share_copy(step).start()
-
     @pl.when(jnp.logical_not(owner))
     def _():
-        square_buf[...] = jnp.zeros((8, 128), F32)
-
-    far_buf[...] = square_buf[...]
+        near_buf[...] = jnp.zeros((8, 128), F32)
+
+    far_buf[...] = near_buf[...]
     for index in range(4):
         source = 4 * index + x
         step = (z - source + 16) % 16
@@ -276,25 +290,25 @@
         @pl.when(step != 0)
         def _():
             slot = (step + 15) % 16
-            remote(square_buf, from_far.at[slot], far_send.at[0], far_recv.at[slot], partner).wait_recv()
+            remote(near_buf, from_far.at[slot], far_send.at[0], far_recv.at[slot], partner).wait_recv()
             far_buf[...] += from_far[slot]
 
-    def plane_copy(step):
-        return remote(far_buf, from_plane.at[step - 1], plane_send.at[step - 1], plane_recv.at[step - 1], plane_peer(step))
-
-    @pl.loop(1, 32)
-    def _(step):
-        plane_copy(step).start()
+    def cross_copy(step):
+        return remote(
+            far_buf, from_cross.at[step - 1], cross_send.at[step - 1], cross_recv.at[step - 1], ((x + step) % 4, row, col)
+        )
+
+    for step in range(1, 4):
+        cross_copy(step).start()
 
     @pl.when(jnp.logical_not(owner))
     def _():
         share_copy(1).wait_recv()
 
-    @pl.loop(1, 32)
-    def _(step):
-        plane_copy(step).wait()
-
-    total_squares = jnp.sum(far_buf[...] + from_plane[...].sum(axis=0), keepdims=True)
+    for step in range(1, 4):
+        cross_copy(step).wait()
+
+    total_squares = jnp.sum(far_buf[...] + from_cross[...].sum(axis=0), keepdims=True)
     spread_rms = jnp.sqrt(total_squares / TOTAL + EPSILON)
     out_ref[...] = share_buf[...] * jnp.minimum(jnp.float32(1.0), 1.0 / spread_rms)
 
@@ -311,6 +325,8 @@
         def _(step):
             far_copy(step).wait_send()
 
+        for step in range(1, 8):
+            near_copy(step).wait_send()
         for step in range(1, 4):
             share_copy(step).wait_send()
 
@@ -471,9 +487,9 @@
         there = (z + step) % 16
         return (x, y * 4 + (there // 8) * 2 + core, there % 8)
 
-    def plane_peer(step):
-        there = (x * 8 + y * 2 + core + step) % 32
-        return (there // 8, (there % 8) // 2 * 4 + z_hi * 2 + there % 2, col)
+    def near_peer(step):
+        there = (y * 2 + core + step) % 8
+        return (x, there // 2 * 4 + z_hi * 2 + there % 2, col)
 
     def greet(peer):
         pl.semaphore_signal(barrier, inc=1, device_id=peer, device_id_type=MESH)
@@ -485,9 +501,10 @@
     def _(step):
         greet(line_peer(step))
 
-    @pl.loop(1, 32)
-    def _(step):
-        greet(plane_peer(step))
+    for step in range(1, 4):
+        greet(((x + step) % 4, row, col))
+    for step in range(1, 8):
+        greet(near_peer(step))
 
     u1, u2, u3 = (ref[...].astype(F32) for ref in (u1_ref, u2_ref, u3_ref))
     fill_sides(u1, u2, u3, send_sides)
@@ -543,7 +560,7 @@
     p34 = strided_sum(v3, range(4 + 1, 4 + 3), CELLS, 4, (0, 1)).astype(BF16)
     p12, p13, p23 = pooled()
     fill_packets((ext1, ext2, ext3, pp12, pp13, pp23), send_rows, send_corners)
-    pl.semaphore_wait(barrier, 54)
+    pl.semaphore_wait(barrier, 33)
 
     def halo_copy(route):
         slot, down, right, src, dst = route
@@ -795,6 +812,31 @@
             block[lane, lane // (width * factor) * width + lane % width] = 1.0
         blocks.append(block)
     return np.concatenate(blocks, axis=1)
+
+
+def hand_over_kernel(*refs):
+    share_ref, out_ref = refs[4], refs[9]
+    for source, target in zip(refs[0:4], refs[5:9]):
+        target[...] = source[...]
+    offset = (SHARE * (lax.axis_index("row") * 8 + lax.axis_index("col"))) % 1024
+    rows, lanes = offset // 128, offset % 128
+    share = share_ref[...]
+    first = pltpu.roll(pltpu.roll(share, (WINDOW - rows) % WINDOW, 0), (128 - lanes) % 128, 1)
+    then = pltpu.roll(pltpu.roll(share, WINDOW - 1 - rows, 0), (128 - lanes) % 128, 1)
+    out_ref[...] = jnp.where(lanes_of(WINDOW, 128) < 128 - lanes, first, then)[0:56]
+
+
+def hand_over(*results):
+    whole = pl.BlockSpec(memory_space=pltpu.VMEM)
+    return pl.pallas_call(
+        hand_over_kernel,
+        out_shape=[jax.ShapeDtypeStruct(value.shape, BF16) for value in results[:4]]
+        + [jax.ShapeDtypeStruct((56, 128), F32)],
+        in_specs=[whole] * 5,
+        out_specs=[whole] * 5,
+        compiler_params=pltpu.CompilerParams(vmem_limit_bytes=56 * 1024 * 1024),
+        name="hand_over",
+    )(*results)
 
 
 def local(f1, f2, f3, f4, o1, o2, o3, u1, u2, u3, k1, k2, k3, s12, s23, m21, m31, m41, m32, m42, m43):
@@ -844,17 +886,17 @@
             bf16(4 * BLOCK, 128), bf16(4 * BLOCK, 128), bf16(12, PART, 128), bf16(4 * PART, 128), bf16(4, PART, 128),
             bf16(4, HALF, 128), bf16(HALF, 128), bf16(3, PART, 128),
             dma((4,)), dma((4,)), dma((12,)), dma((12,)), dma((4,)), dma((4,)), dma((4,)), dma((4,)), dma((3,)), dma((3,)),
-            bf16(2 * PART, 128), bf16(15, WINDOW, 128), f32(WINDOW, 128), f32(8, 128), f32(15, 8, 128), f32(8, 128), f32(31, 8, 128),
-            dma((4,)), dma((15,)), dma((3,)), dma((1,)), dma((15,)), dma((15,)), dma((31,)), dma((31,)),
+            bf16(2 * PART, 128), bf16(15, WINDOW, 128), f32(WINDOW, 128), f32(8, 128), f32(7, 8, 128), f32(8, 128),
+            f32(15, 8, 128), f32(8, 128), f32(3, 8, 128),
+            dma((4,)), dma((15,)), dma((3,)), dma((1,)), dma((7,)), dma((7,)), dma((15,)), dma((15,)), dma((3,)), dma((3,)),
         ],
         compiler_params=pltpu.CompilerParams(
             collective_id=0, has_side_effects=True, vmem_limit_bytes=56 * 1024 * 1024
         ),
         name="backward",
     )(*inputs)
-    offset = (SHARE * lax.axis_index(("row", "col"))) % 1024
-    weight_grads = lax.dynamic_slice(share.reshape(WINDOW * 128), (offset,), (SHARE,))
-    return grad_one, grad_two, grad_three, grad_four, weight_grads
+    *grads, weight_grads = hand_over(grad_one, grad_two, grad_three, grad_four, share)
+    return *grads, weight_grads.reshape(56 * 128)[:SHARE]
 
 
 def solution(mesh):

time: 81 us -> 77.9 us (0.962)
  the two profiles are of different devices: /device:TPU:1 before, /device:TPU:12 now
where the time goes in v6:
time: 77.9 us; the launch traced here: 77.7 us
  Pallas kernels  77.1 us (99%)
    pallas_call x1, Pallas kernels, local(): pl.pallas_call(backward_kernel, out_shape=[jax.ShapeDtypeStruct(value.sha...  75.4 us
    pallas_call x1, Pallas kernels, hand_over(): pl.pallas_call(hand_over_kernel, out_shape=[jax.ShapeDtypeStruct(value.sh...  1.7 us

profile of v6, /device:TPU:12, one launch (start us, length us, event | category | flops | bytes accessed | tf_op | source)
XLA Modules:
  0.0 77.7 jit_solution(12880219699651097862)
XLA Ops:
  0.6 75.4 %backward.1 = (bf16[8,9216]{1,0:T(8,128)(2,1)}, bf16[4,9216]{1,0:T(4,128)(2,1)}, bf16[2,9216]{1,0:T(2,128)(2,1)}, bf16[1,9216]{1,0:T(2,128)(2,1)}, f32[64,128]{1,0:T(8,128)}) custom-call(bf16[8,9216]{1,0:T(8,128)(2,1)} %u1_ref.1, bf16[4,9216]{1,0:T(4,128)(2,1)} %u2_ref.1, bf16[2,9216]{1,0:T(2,128)(2,1)} %u3_ref.1, bf16[8,9216]{1,0:T(8,128)(2,1)} %refs_0_.1, ...), custom_call_target="tpu_custom_call" | custom-call | tf_op jit(solution)/shard_map/backward/pallas_call | solution.py:867
  76.0 1.7 %hand_over.1 = (bf16[8,9216]{1,0:T(8,128)(2,1)}, bf16[4,9216]{1,0:T(4,128)(2,1)}, bf16[2,9216]{1,0:T(2,128)(2,1)}, bf16[1,9216]{1,0:T(2,128)(2,1)}, f32[56,128]{1,0:T(8,128)}) custom-call(bf16[8,9216]{1,0:T(8,128)(2,1)} %get-tuple-element.15.refs_0_, bf16[4,9216]{1,0:T(4,128)(2,1)} %get-tuple-element.16.refs_1_, bf16[2,9216]{1,0:T(2,128)(2,1)} %get-tuple-element.17.refs_2_, ...), custom_call_target="tpu_custom_call" | custom-call | tf_op jit(solution)/shard_map/hand_over/pallas_call | solution.py:831

commit v7 on v6

--- a/solution.py
+++ b/solution.py
@@ -23,8 +23,8 @@
     return (((y * 2 + core) * 2 + z_hi) * 4 + quarter) * 2 + half
 
 
-def pack_shares(flat_ref, packed_ref, block):
-    for share in range(32 * block, 32 * block + 32):
+def pack_shares(flat_ref, packed_ref, block, half):
+    for share in range(32 * block + 16 * half, 32 * block + 16 * half + 16):
         start = SHARE * share // 1024 * 8
         place = share_place(share) * WINDOW
         packed_ref[place : place + WINDOW, :] = flat_ref[start : start + WINDOW, :].astype(jnp.bfloat16)
@@ -42,13 +42,13 @@
         self.y_first, self.sum_y, self.x_second = y_first, sum_y, x_second
         self.sems = sems
 
-    def core_copy(self, block):
+    def core_copy(self, block, half):
         x, row, col = self.where
-        start = pl.multiple_of((block * 2 + 1 - row % 2) * BLOCK, BLOCK)
+        start = pl.multiple_of((block * 2 + 1 - row % 2) * BLOCK + half * HALF, HALF)
         send, recv = self.sems[0:2]
         return remote(
-            self.packed.at[pl.ds(start, BLOCK)], self.from_core.at[pl.ds(block * BLOCK, BLOCK)],
-            send.at[block], recv.at[block], (x, row + 1 - 2 * (row % 2), col),
+            self.packed.at[pl.ds(start, HALF)], self.from_core.at[pl.ds(block * BLOCK + half * HALF, HALF)],
+            send.at[block * 2 + half], recv.at[block * 2 + half], (x, row + 1 - 2 * (row % 2), col),
         )
 
     def x_first_copy(self, block, step):
@@ -88,30 +88,29 @@
             send.at[step - 1], recv.at[step - 1], (there, row, col),
         )
 
-    def leave(self, block):
-        self.core_copy(block).start()
-
-    def spread(self, block):
+    def leave(self, block, half):
+        self.core_copy(block, half).start()
+
+    def spread(self, block, half):
         core, y = self.where[1] % 2, self.where[1] // 4
-        self.core_copy(block).wait()
-        for half in range(2):
-
-            @pl.loop(0, 2)
-            def _(part):
-                mine = pl.multiple_of((block * 2 + core) * BLOCK + half * HALF + part * (HALF // 2), HALF // 2)
-                place = pl.multiple_of(block * BLOCK + half * HALF + part * (HALF // 2), HALF // 2)
-                total = self.packed[pl.ds(mine, HALF // 2), :].astype(F32)
-                total = total + self.from_core[pl.ds(place, HALF // 2), :].astype(F32)
-                self.sum_core[pl.ds(place, HALF // 2), :] = total.astype(BF16)
-
-            if half == 0:
-                for step in range(1, 4):
-                    self.x_first_copy(block, step).start()
-            else:
-
-                @pl.when(y != block)
-                def _():
-                    self.y_first_copy(block).start()
+        self.core_copy(block, half).wait()
+
+        @pl.loop(0, 2)
+        def _(part):
+            mine = pl.multiple_of((block * 2 + core) * BLOCK + half * HALF + part * (HALF // 2), HALF // 2)
+            place = pl.multiple_of(block * BLOCK + half * HALF + part * (HALF // 2), HALF // 2)
+            total = self.packed[pl.ds(mine, HALF // 2), :].astype(F32)
+            total = total + self.from_core[pl.ds(place, HALF // 2), :].astype(F32)
+            self.sum_core[pl.ds(place, HALF // 2), :] = total.astype(BF16)
+
+        if half == 0:
+            for step in range(1, 4):
+                self.x_first_copy(block, step).start()
+        else:
+
+            @pl.when(y != block)
+            def _():
+                self.y_first_copy(block).start()
 
     def turn_to_y(self, block):
         x, row, col = self.where
@@ -221,7 +220,7 @@
     def line_copy(block):
         target = (block // 2) * 8 + (block % 2) * 4 + x
         step = (z - target + 16) % 16
-        slot = (step + 15) % 16
+        slot = (step + 14) % 15
         return step, remote(
             sum_plane.at[pl.ds(pl.multiple_of(block * WINDOW, WINDOW), WINDOW)],
             from_line.at[slot], line_send.at[block], line_recv.at[slot],
@@ -289,7 +288,7 @@
 
         @pl.when(step != 0)
         def _():
-            slot = (step + 15) % 16
+            slot = (step + 14) % 15
             remote(near_buf, from_far.at[slot], far_send.at[0], far_recv.at[slot], partner).wait_recv()
             far_buf[...] += from_far[slot]
 
@@ -596,6 +595,17 @@
     banded(m31_ref[...], rep192_ref[...], 192, 48, mixer_blocks(192, 2), band31)
     banded(m32_ref[...], rep96_ref[:, :256], 96, 192, mixer_blocks(96, 2), band32)
 
+    reduction = Reduction(packed_ref, (x, row, col), *reduce_refs[:8], reduce_refs[8:18])
+    flat[6282:FLAT_ROWS, :] = jnp.zeros((FLAT_ROWS - 6282, 128), F32)
+
+    def settle(pieces, halves):
+        for piece in pieces:
+            width, flat_base, src_base, count = PIECES[piece]
+            place({48: w48, 96: w96, 192: w192}[width], flat, width, flat_base, src_base, count)
+        for block, half in halves:
+            pack_shares(flat, packed_ref, block, half)
+            reduction.leave(block, half)
+
     def fold_mixer(grads, width, rows, base, dst):
         total = None
         for j in range(GROUP // rows):
@@ -619,6 +629,8 @@
     for g in range(CELLS):
         g4_ref[:, lanes(g)] = back4[g : g + 1].astype(BF16)
 
+    settle((5, 6, 7, 8, 9, 10), ((3, 1),))
+
     for route in routes:
         halo_copy(route).wait()
     top, bottom = jnp.where(line > 0, 1.0, 0.0), jnp.where(line < 63, 1.0, 0.0)
@@ -678,18 +690,8 @@
     down_grads(pad_o1, ext2, 8, 8 * CELLS, 128, 96, 48, 864, w96)
     down_grads(pad_o2, ext3, 4, 4 * CELLS, 256, 192, 96, 1728, w192)
 
-    reduction = Reduction(packed_ref, (x, row, col), *reduce_refs[:8], reduce_refs[8:18])
-    flat[6282:FLAT_ROWS, :] = jnp.zeros((FLAT_ROWS - 6282, 128), F32)
-
-    def settle(pieces, blocks):
-        for piece in pieces:
-            width, flat_base, src_base, count = PIECES[piece]
-            place({48: w48, 96: w96, 192: w192}[width], flat, width, flat_base, src_base, count)
-        for block in blocks:
-            pack_shares(flat, packed_ref, block)
-            reduction.leave(block)
-
-    settle((3, 4, 5, 6, 7, 8, 9, 10), (3,))
+    settle((3, 4), ((3, 0),))
+    reduction.spread(3, 1)
 
     def rim_mask(rows, inner):
         place_row = lax.broadcasted_iota(jnp.int32, (CELLS + 2, rows, GROUP), 1)
@@ -729,7 +731,7 @@
         ref[0:8, :] = jnp.zeros((8, GROUP), F32)
         ref[ref.shape[0] - 8 :, :] = jnp.zeros((8, GROUP), F32)
 
-    reduction.spread(3)
+    reduction.spread(3, 0)
 
     def fold(grads, width, base, a, dst):
         total = None
@@ -755,7 +757,7 @@
     for g in range(CELLS):
         g3_ref[:, lanes(g)] = res3[4 * g + 1 : 4 * g + 3, :].astype(BF16)
 
-    settle((2,), (2, 1))
+    settle((2,), ((2, 0), (2, 1), (1, 0), (1, 1)))
 
     f2x = pad_f2[...].astype(BF16)
     back = None
@@ -772,8 +774,9 @@
     for g in range(CELLS):
         g2_ref[:, lanes(g)] = res2[8 * g + 2 : 8 * g + 6, :].astype(BF16)
 
-    reduction.spread(2)
-    reduction.spread(1)
+    settle((1,), ((0, 1),))
+    for block, half in ((2, 0), (2, 1), (1, 0), (1, 1)):
+        reduction.spread(block, half)
 
     f1 = f1_ref[...]
     f1 = jnp.concatenate([f1[:, lanes(g)].astype(F32) for g in range(CELLS)], axis=0).astype(BF16)
@@ -789,8 +792,9 @@
     for g in range(CELLS):
         g1_ref[:, lanes(g)] = back[8 * g : 8 * g + 8].astype(BF16)
 
-    settle((0, 1), (0,))
-    reduction.spread(0)
+    settle((0,), ((0, 0),))
+    reduction.spread(0, 1)
+    reduction.spread(0, 0)
     for block in (3, 2, 1, 0):
         reduction.turn_to_y(block)
     reduction.turn_to_x()
@@ -885,7 +889,7 @@
             f32(1, 1104, 128), f32(1, 1872, 128), f32(2, 2976, 128), f32(FLAT_ROWS, 128),
             bf16(4 * BLOCK, 128), bf16(4 * BLOCK, 128), bf16(12, PART, 128), bf16(4 * PART, 128), bf16(4, PART, 128),
             bf16(4, HALF, 128), bf16(HALF, 128), bf16(3, PART, 128),
-            dma((4,)), dma((4,)), dma((12,)), dma((12,)), dma((4,)), dma((4,)), dma((4,)), dma((4,)), dma((3,)), dma((3,)),
+            dma((8,)), dma((8,)), dma((12,)), dma((12,)), dma((4,)), dma((4,)), dma((4,)), dma((4,)), dma((3,)), dma((3,)),
             bf16(2 * PART, 128), bf16(15, WINDOW, 128), f32(WINDOW, 128), f32(8, 128), f32(7, 8, 128), f32(8, 128),
             f32(15, 8, 128), f32(8, 128), f32(3, 8, 128),
             dma((4,)), dma((15,)), dma((3,)), dma((1,)), dma((7,)), dma((7,)), dma((15,)), dma((15,)), dma((3,)), dma((3,)),

time: 77.9 us -> 76.7 us (0.985)
  Pallas kernels: 77.1 us -> 75.9 us
    pallas_call x1, Pallas kernels: 75.4 us -> 74.2 us  [local(): pl.pallas_call(backward_kernel, out_shape=[jax.ShapeDtypeStruct(value.sha...]
where the time goes in v7:
time: 76.7 us; the launch traced here: 76.5 us
  Pallas kernels  75.9 us (99%)
    pallas_call x1, Pallas kernels, local(): pl.pallas_call(backward_kernel, out_shape=[jax.ShapeDtypeStruct(value.sha...  74.2 us
    pallas_call x1, Pallas kernels, hand_over(): pl.pallas_call(hand_over_kernel, out_shape=[jax.ShapeDtypeStruct(value.sh...  1.7 us

profile of v7, /device:TPU:12, one launch (start us, length us, event | category | flops | bytes accessed | tf_op | source)
XLA Modules:
  0.0 76.5 jit_solution(14963303751512679032)
XLA Ops:
  0.6 74.2 %backward.1 = (bf16[8,9216]{1,0:T(8,128)(2,1)}, bf16[4,9216]{1,0:T(4,128)(2,1)}, bf16[2,9216]{1,0:T(2,128)(2,1)}, bf16[1,9216]{1,0:T(2,128)(2,1)}, f32[64,128]{1,0:T(8,128)}) custom-call(bf16[8,9216]{1,0:T(8,128)(2,1)} %u1_ref.1, bf16[4,9216]{1,0:T(4,128)(2,1)} %u2_ref.1, bf16[2,9216]{1,0:T(2,128)(2,1)} %u3_ref.1, bf16[8,9216]{1,0:T(8,128)(2,1)} %refs_0_.1, ...), custom_call_target="tpu_custom_call" | custom-call | tf_op jit(solution)/shard_map/backward/pallas_call | solution.py:871
  74.8 1.7 %hand_over.1 = (bf16[8,9216]{1,0:T(8,128)(2,1)}, bf16[4,9216]{1,0:T(4,128)(2,1)}, bf16[2,9216]{1,0:T(2,128)(2,1)}, bf16[1,9216]{1,0:T(2,128)(2,1)}, f32[56,128]{1,0:T(8,128)}) custom-call(bf16[8,9216]{1,0:T(8,128)(2,1)} %get-tuple-element.15.refs_0_, bf16[4,9216]{1,0:T(4,128)(2,1)} %get-tuple-element.16.refs_1_, bf16[2,9216]{1,0:T(2,128)(2,1)} %get-tuple-element.17.refs_2_, ...), custom_call_target="tpu_custom_call" | custom-call | tf_op jit(solution)/shard_map/hand_over/pallas_call | solution.py:835
